TPU v7x, 32 devices: a whole 2x2x4 slice. The times are simulated.
32 devices in a mesh: rep: 2 (over y), sec: 8 (over z, x), tp: 2 (over core).
Axes of the slice: x: 2, y: 2, z: 4, core: 2. Of those that a mesh axis runs over, the one named last changes fastest.
Arguments:
- patch_tokens: bfloat16 [16, 256, 1408], P(('rep', 'sec')), parts along dimension 0, may hold values from -6 to 6
- skip_features: bfloat16 [16, 256, 1024], P(('rep', 'sec')), parts along dimension 0, may hold values from -6 to 6
- exit_first: int32 [4], P('rep'), parts along dimension 0, may hold values from 0 to 7, as said below
- exit_second: int32 [4], P('rep'), parts along dimension 0, may hold values from 0 to 7, as said below
- skip_weight: bfloat16 [1024, 1408], replicated, may hold values from -0.1875 to 0.1875
- norm_gain: float32 [1408], replicated, may hold values from 0.1 to 1.9
- norm_bias: float32 [1408], replicated, may hold values from -3 to 3
- up_weight: bfloat16 [1408, 3584], P(None, ('sec', 'tp')), may hold values from -0.15625 to 0.15625
- up_bias: bfloat16 [3584], P(('sec', 'tp')), may hold values from -3 to 3
- down_weight: bfloat16 [1408, 3584], P(None, ('sec', 'tp')), may hold values from -0.09375 to 0.09375
- down_bias: float32 [1408], P('tp'), may hold values from -3 to 3
Outputs:
- refined: bfloat16 [16, 256, 1408], P(('rep', 'sec'), None, 'tp'), parts along dimension 0
There are 2 independent parts, one for each index of `rep`. A program takes and returns all parts, laid end to end along the dimension named above; an argument that names none is the same for every part. Nothing has to cross between parts.
Inputs may be any that keep to these rules, and one draw needn't show every extreme that they name: `exit_first`: distinct image ids; no id is in both lists, so exactly 4 images are in neither; in every draw some device holds 1 images that are in neither list. `exit_second`: distinct image ids, none of them in exit_first.
All inputs are finite; a program needn't handle non-finite values.
Results may differ from a plain program's by a relative error of at most 0.0054.
Values may be sent and summed in bfloat16 or wider, within the bound.
No kernel may reach another device: no remote copies, remote signals or barrier semaphores. Data moves between devices by JAX's collectives and lax.ppermute only.
A program may use at most 64 MiB of HBM per device.

v0:
```python
import jax
import jax.numpy as jnp
from jax import lax
from jax.sharding import PartitionSpec as P


def project(tokens_rows, skip_rows, skip_weight):
    joined = tokens_rows.astype(jnp.float32) + jnp.dot(
        skip_rows, skip_weight, preferred_element_type=jnp.float32
    )
    return joined.astype(jnp.bfloat16)


def normalize(carried, norm_gain, norm_bias):
    as_float = carried.astype(jnp.float32)
    row_mean = jnp.mean(as_float, axis=1, keepdims=True)
    centered = as_float - row_mean
    row_var = jnp.mean(centered * centered, axis=1, keepdims=True)
    return (centered * lax.rsqrt(row_var + 1e-06) * norm_gain + norm_bias).astype(jnp.bfloat16)


def select_images(selector, values):
    picked = jnp.einsum("ki,itd->ktd", selector, values, preferred_element_type=jnp.float32)
    return picked.astype(values.dtype)


def local(
    patch_tokens,
    skip_features,
    exit_first,
    exit_second,
    skip_weight,
    norm_gain,
    norm_bias,
    up_weight,
    up_bias,
    down_weight,
    down_bias,
):
    n_sec = lax.axis_size("sec")
    images, tok_count, model_width = patch_tokens.shape
    row_count = images * tok_count
    per_peer = row_count // n_sec
    half_rows = row_count // 2
    own_index = lax.axis_index("sec")
    image_ids = own_index * images + jnp.arange(images, dtype=jnp.int32)
    listed = jnp.concatenate([exit_first, exit_second])
    leaving = jnp.any(image_ids[:, None] == listed[None, :], axis=1)
    staying = jnp.where(leaving, 0, 1).astype(jnp.int32)
    counts = lax.all_gather(jnp.sum(staying).reshape(1) * tok_count, "sec", axis=0, tiled=True)
    row_offsets = jnp.cumsum(counts) - counts
    own_offset = lax.dynamic_index_in_dim(row_offsets, own_index, keepdims=False)
    image_rank = jnp.cumsum(staying) - staying
    image_slots = jnp.arange(images, dtype=jnp.int32)
    selector = ((image_slots[:, None] == image_rank[None, :]) & (staying[None, :] > 0)).astype(
        jnp.bfloat16
    )

    def pack(values):
        front = select_images(selector, values).reshape(per_peer, n_sec, values.shape[2])
        return jnp.roll(front, own_offset, axis=1)

    arrived = (
        lax.all_to_all(pack(patch_tokens), "sec", split_axis=1, concat_axis=1, tiled=True),
        lax.all_to_all(pack(skip_features), "sec", split_axis=1, concat_axis=1, tiled=True),
    )
    arrived_rows = [member.reshape(row_count, member.shape[2]) for member in arrived]
    rotation = (own_index - row_offsets) % n_sec
    lane_rank = rotation[None, :] + n_sec * jnp.arange(per_peer, dtype=jnp.int32)[:, None]
    valid_slot = (lane_rank < counts[None, :]).reshape(row_count)
    position = ((row_offsets[None, :] + lane_rank - own_index) // n_sec).reshape(row_count)
    placement_index = jnp.where(valid_slot, position, -1)
    gather_table = (
        jnp.arange(half_rows, dtype=jnp.int32)[:, None] == placement_index[None, :]
    ).astype(jnp.bfloat16)
    work_rows = [
        jnp.dot(gather_table, member, preferred_element_type=jnp.float32).astype(member.dtype)
        for member in arrived_rows
    ]
    carried = project(work_rows[0], work_rows[1], skip_weight)
    normed = normalize(carried, norm_gain, norm_bias)
    up_piece = lax.all_gather(up_weight, "sec", axis=1, tiled=True)
    down_piece = lax.all_gather(down_weight, "sec", axis=1, tiled=True)
    bias_piece = lax.all_gather(up_bias.reshape(1, -1), "sec", axis=1, tiled=True)
    pre_act = jnp.dot(normed, up_piece, preferred_element_type=jnp.float32) + bias_piece.astype(
        jnp.float32
    )
    hidden = jax.nn.gelu(pre_act, approximate=False).astype(jnp.bfloat16)
    mlp_sum = lax.dot_general(
        hidden, down_piece, (((1,), (1,)), ((), ())), preferred_element_type=jnp.float32
    )
    mlp_share = lax.psum_scatter(mlp_sum, "tp", scatter_dimension=1, tiled=True)
    columns = mlp_share.shape[1]
    residual = lax.dynamic_slice_in_dim(carried, lax.axis_index("tp") * columns, columns, 1)
    result = (residual.astype(jnp.float32) + mlp_share + down_bias).astype(jnp.bfloat16)
    returning = lax.dot_general(
        gather_table, result, (((0,), (0,)), ((), ())), preferred_element_type=jnp.float32
    ).astype(jnp.bfloat16)
    returned = lax.all_to_all(
        returning.reshape(per_peer, n_sec, columns), "sec", split_axis=1, concat_axis=1, tiled=True
    )
    front_rows = jnp.roll(returned, -own_offset, axis=1).reshape(images, tok_count, columns)
    return select_images(jnp.transpose(selector), front_rows)


def solution(mesh):
    in_specs = (
        P(("rep", "sec"), None, None),
        P(("rep", "sec"), None, None),
        P("rep"),
        P("rep"),
        P(),
        P(),
        P(),
        P(None, ("sec", "tp")),
        P(("sec", "tp")),
        P(None, ("sec", "tp")),
        P("tp"),
    )
    out_specs = P(("rep", "sec"), None, "tp")
    return jax.shard_map(local, mesh=mesh, in_specs=in_specs, out_specs=out_specs, check_vma=False)
```

profile of v0, /device:TPU:0, one launch (start us, length us, event | category | flops | bytes accessed | tf_op | source)
XLA Modules:
  0.0 250.1 jit_solution(3739502691076199773)
XLA Ops:
  6.5 0.0 copy-start
  6.5 0.0 all-gather.4.cloned.1.call-start
  6.5 0.7 all-gather.4.cloned.1.call-update
  7.3 0.0 all-gather.6.cloned.1.call-start
  7.3 0.7 all-gather.6.cloned.1.call-update
  8.0 1.4 compare_reduce_fusion
  10.1 1.3 dynamic-slice
  11.3 0.7 dynamic-update-slice
  12.1 13.1 %all-reduce = s32[8]{0:T(128)S(1)} all-reduce(s32[8]{0:T(128)S(1)} %dynamic-update-slice), channel_id=1, replica_groups=mesh['rep'=2,'sec'=8,'tp'=2] {'sec'}, use_global_device_ids=true, to_apply=%add | all-reduce | flops 8 | bytes 64
  25.2 0.2 reduce-window.10
  25.4 0.7 dynamic_slice.19
  28.2 0.0 copy-start.1
  28.2 1.3 fusion.18
  29.5 0.5 fusion.19
  30.0 1.0 copy.19
  30.9 0.0 copy-start.5
  30.9 4.3 %all-to-all-start = ((bf16[32,8,1408]{2,0,1:T(8,128)(2,1)}), bf16[32,8,1408]{2,0,1:T(8,128)(2,1)}, u32[]{:S(2)}, u32[]{:S(2)}) async-start(bf16[32,8,1408]{2,0,1:T(8,128)(2,1)} %copy.19), calls=%async_computation | async-start | bytes 1441792 | tf_op jit(solution)/shard_map/all_to_all | solution.py:64
  35.3 0.0 copy-done.1
  35.3 0.1 fusion.22
  35.4 0.4 fusion.23
  35.8 1.1 copy.21
  36.9 23.6 %all-to-all-done = bf16[32,8,1408]{2,0,1:T(8,128)(2,1)} async-done(((bf16[32,8,1408]{2,0,1:T(8,128)(2,1)}), bf16[32,8,1408]{2,0,1:T(8,128)(2,1)}, u32[]{:S(2)}, u32[]{:S(2)}) %all-to-all-start) | async-done | bytes 720928 | tf_op jit(solution)/shard_map/all_to_all | solution.py:64
  60.4 4.2 %all-to-all-start.1 = ((bf16[32,8,1024]{2,0,1:T(8,128)(2,1)}), bf16[32,8,1024]{2,0,1:T(8,128)(2,1)}, u32[]{:S(2)}, u32[]{:S(2)}) async-start(bf16[32,8,1024]{2,0,1:T(8,128)(2,1)} %copy.21), calls=%async_computation.1 | async-start | bytes 1048576 | tf_op jit(solution)/shard_map/all_to_all | solution.py:65
  64.6 0.0 reduce-scatter.4.cloned.1.call-start
  64.7 0.1 fusion.76
  64.7 0.1 sub.53
  64.8 0.1 add_compare_fusion
  64.9 0.1 lt.60
  65.7 0.0 copy-done.5
  65.7 0.2 dynamic-update-slice.1
  65.9 31.7 %all-reduce.1 = bf16[1792]{0:T(1024)(128)(2,1)S(1)} all-reduce(bf16[1792]{0:T(1024)(128)(2,1)S(1)} %dynamic-update-slice.1), channel_id=2, replica_groups=mesh['rep'=2,'sec'=8,'tp'=2] {'sec'}, use_global_device_ids=true, to_apply=%add.1 | all-reduce | flops 1792 | bytes 7168
  97.6 0.0 copy-start.3
  97.7 0.0 copy-start.4
  97.7 2.4 fusion.1
  100.1 0.0 all-to-all-done.1
  100.1 0.0 copy-done
  100.1 2.2 convert_reduce_fusion
  102.3 0.2 fusion.14
  102.6 0.0 copy-start.2
  102.6 14.4 %all-gather.4.cloned.1.call-done = bf16[1408,1792]{0,1:T(8,128)(2,1)} async-done(((bf16[1408,224]{0,1:T(8,128)(2,1)}), bf16[1408,1792]{0,1:T(8,128)(2,1)}) %all-gather.4.cloned.1.call-update) | async-done | bytes 5046288 | tf_op jit(solution)/shard_map/all_gather | solution.py:82
  117.0 85.3 %all-gather.6.cloned.1.call-done = bf16[1408,1792]{0,1:T(8,128)(2,1)} async-done(((bf16[1408,224]{0,1:T(8,128)(2,1)}), bf16[1408,1792]{0,1:T(8,128)(2,1)}) %all-gather.6.cloned.1.call-update) | async-done | bytes 5046288 | tf_op jit(solution)/shard_map/all_gather | solution.py:83
  202.3 0.0 copy-done.3
  202.3 0.0 copy-done.4
  202.3 9.4 %convolution_bitcast_fusion = f32[1408,128]{1,0:T(8,128)} fusion(bf16[1408,1792]{0,1:T(8,128)(2,1)} %all-gather.6.cloned.1.call-done, bf16[1408,1792]{0,1:T(8,128)(2,1)} %all-gather.4.cloned.1.call-done, f32[1792]{0:T(1024)S(1)} %add.151, bf16[128,1408]{1,0:T(8,128)(2,1)S(1)} %get-tuple-element.8, f32[1408]{0:T(1024)S(1)} %copy-done.3, ...), kind=kOutput, calls=%fused_computation.2 | convolution fusion | flops 1308065792 | bytes 11193344
  211.7 0.0 reduce-scatter.4.cloned.1.call-update
  211.8 6.5 %reduce-scatter.4.cloned.1.call-done = f32[704,128]{1,0:T(8,128)} async-done(((f32[1408,128]{1,0:T(8,128)}), f32[704,128]{1,0:T(8,128)}) %reduce-scatter.4.cloned.1.call-update) | async-done | bytes 360464
  218.3 1.9 copy.30
  220.2 0.0 copy-done.2
  220.2 2.1 convolution_convert_fusion.1
  222.3 1.2 copy.24
  223.5 0.8 copy.25
  224.3 5.8 %all-to-all-start.2 = ((bf16[32,8,704]{2,0,1:T(8,128)(2,1)}), bf16[32,8,704]{2,0,1:T(8,128)(2,1)S(1)}, u32[]{:S(2)}, u32[]{:S(2)}) async-start(bf16[32,8,704]{2,0,1:T(8,128)(2,1)} %copy.25), calls=%async_computation.2 | async-start | bytes 786432 | tf_op jit(solution)/shard_map/all_to_all | solution.py:99
  230.8 11.5 %all-to-all-done.2 = bf16[32,8,704]{2,0,1:T(8,128)(2,1)S(1)} async-done(((bf16[32,8,704]{2,0,1:T(8,128)(2,1)}), bf16[32,8,704]{2,0,1:T(8,128)(2,1)S(1)}, u32[]{:S(2)}, u32[]{:S(2)}) %all-to-all-start.2) | async-done | bytes 360480 | tf_op jit(solution)/shard_map/all_to_all | solution.py:99
  242.2 0.2 multiply_convert_fusion.2
  242.4 0.2 copy.43
  242.6 0.9 copy.27
  (8 shorter events, 0.1 us)
Async XLA Ops:
  6.5 93.5 %copy-start = (bf16[1024,1408]{1,0:T(8,128)(2,1)S(1)}, bf16[1024,1408]{1,0:T(8,128)(2,1)}, u32[]{:S(2)}) copy-start(bf16[1024,1408]{1,0:T(8,128)(2,1)} %param.15) | copy-start | bytes 8650756
  6.5 110.4 %all-gather.4.cloned.1.call-start = ((), (), s32[]{:S(2)}) async-start(), calls=%async_computation.4 | async-start | bytes 5677056 | tf_op jit(solution)/shard_map/all_gather | solution.py:82
  7.3 195.1 %all-gather.6.cloned.1.call-start = ((), (), s32[]{:S(2)}) async-start(), calls=%async_computation.5 | async-start | bytes 5677056 | tf_op jit(solution)/shard_map/all_gather | solution.py:83
  28.2 7.1 %copy-start.1 = (bf16[1,256,1024]{2,1,0:T(8,128)(2,1)S(1)}, bf16[1,256,1024]{2,1,0:T(8,128)(2,1)}, u32[]{:S(2)}) copy-start(bf16[1,256,1024]{2,1,0:T(8,128)(2,1)} %param.12) | copy-start | bytes 1572868
  30.9 34.7 %copy-start.5 = (bf16[224]{0:T(256)(128)(2,1)S(1)}, bf16[224]{0:T(256)(128)(2,1)}, u32[]{:S(2)}) copy-start(bf16[224]{0:T(256)(128)(2,1)} %param.19) | copy-start | bytes 1348
  30.9 29.5 %all-to-all-start = ((bf16[32,8,1408]{2,0,1:T(8,128)(2,1)}), bf16[32,8,1408]{2,0,1:T(8,128)(2,1)}, u32[]{:S(2)}, u32[]{:S(2)}) async-start(bf16[32,8,1408]{2,0,1:T(8,128)(2,1)} %copy.19), calls=%async_computation | async-start | bytes 1441792 | tf_op jit(solution)/shard_map/all_to_all | solution.py:64
  60.4 39.6 %all-to-all-start.1 = ((bf16[32,8,1024]{2,0,1:T(8,128)(2,1)}), bf16[32,8,1024]{2,0,1:T(8,128)(2,1)}, u32[]{:S(2)}, u32[]{:S(2)}) async-start(bf16[32,8,1024]{2,0,1:T(8,128)(2,1)} %copy.21), calls=%async_computation.1 | async-start | bytes 1048576 | tf_op jit(solution)/shard_map/all_to_all | solution.py:65
  64.6 153.7 %reduce-scatter.4.cloned.1.call-start = ((), (), s32[]{:S(2)}) async-start(), calls=%async_computation.6 | async-start | bytes 1081344
  97.6 104.7 %copy-start.3 = (f32[1408]{0:T(1024)S(1)}, f32[1408]{0:T(1024)}, u32[]{:S(2)}) copy-start(f32[1408]{0:T(1024)} %param.17) | copy-start | bytes 16900
  97.7 104.7 %copy-start.4 = (f32[1408]{0:T(1024)S(1)}, f32[1408]{0:T(1024)}, u32[]{:S(2)}) copy-start(f32[1408]{0:T(1024)} %param.16) | copy-start | bytes 16900
  102.6 117.6 %copy-start.2 = (f32[704]{0:T(1024)S(1)}, f32[704]{0:T(1024)}, u32[]{:S(2)}) copy-start(f32[704]{0:T(1024)} %param.21) | copy-start | bytes 8452
  224.3 17.9 %all-to-all-start.2 = ((bf16[32,8,704]{2,0,1:T(8,128)(2,1)}), bf16[32,8,704]{2,0,1:T(8,128)(2,1)S(1)}, u32[]{:S(2)}, u32[]{:S(2)}) async-start(bf16[32,8,704]{2,0,1:T(8,128)(2,1)} %copy.25), calls=%async_computation.2 | async-start | bytes 786432 | tf_op jit(solution)/shard_map/all_to_all | solution.py:99
Sparse Core Ops, SparseCore 0:
  9.5 107.3 all-gather.3
  119.2 83.1 all-gather.5
  211.9 6.3 reduce-scatter.3
where the time goes:
time: 251 us; the launch traced here: 250 us
  waiting for transfers between devices  143 us (57%)
  blocking collectives  44.8 us (18%)
  between operations  17.4 us (7%)
  matrix products  16.2 us (6%)
  starting transfers between devices  14.3 us (6%)
  local copies, waits for them, and re-layouts  10.2 us (4%)
  other arithmetic  4.47 us (2%)
    all_gather x1, waiting for transfers between devices, local(): down_piece = lax.all_gather(down_weight, 'sec', axis=1, tiled=True)  85.3 us
    unnamed x2, blocking collectives  44.8 us
    all_to_all x1, waiting for transfers between devices, local(): lax.all_to_all(pack(patch_tokens), 'sec', split_axis=1, concat_axis=1, ti...  23.6 us
    all_gather x1, waiting for transfers between devices, local(): up_piece = lax.all_gather(up_weight, 'sec', axis=1, tiled=True)  14.4 us
    all_to_all x1, waiting for transfers between devices, local(): lax.all_to_all(returning.reshape(per_peer, n_sec, columns), 'sec', split_...  11.5 us
    unnamed x1, matrix products  9.41 us
    unnamed x4, waiting for transfers between devices  7.94 us
    all_to_all x1, starting transfers between devices, local(): lax.all_to_all(returning.reshape(per_peer, n_sec, columns), 'sec', split_...  5.76 us
  transfers between devices with their start and end apart: 6, of which 5 were waited for; matrix products, arithmetic and copies ran while one was open for 6% of the time, Pallas kernels for 0%

commit v1 on v0

--- a/solution.py
+++ b/solution.py
@@ -19,12 +19,117 @@
     return (centered * lax.rsqrt(row_var + 1e-06) * norm_gain + norm_bias).astype(jnp.bfloat16)
 
 
+def swap(values, axis, mask):
+    size = lax.axis_size(axis)
+    return lax.ppermute(values, axis, [(i, i ^ mask) for i in range(size)])
+
+
+def by_index(index, own, other):
+    return jnp.where(index == 0, own, other), jnp.where(index == 0, other, own)
+
+
+def pair_order(core, own, other, half):
+    first, second = by_index(core, own, other)
+    return jnp.concatenate([first[:half], second[:half], first[half:], second[half:]])
+
+
+def square_plan(
+    patch_tokens,
+    skip_features,
+    exit_first,
+    exit_second,
+    skip_weight,
+    norm_gain,
+    norm_bias,
+    up_weight,
+    up_bias,
+    down_weight,
+    down_bias,
+):
+    core = lax.axis_index("tp")
+    plane = lax.axis_index("rep")
+    own_index = lax.axis_index("sec")
+    _, tok_count, width = patch_tokens.shape
+    units = up_weight.shape[1]
+    half = units // 2
+    columns = width // 2
+    rows = tok_count // 2
+
+    def plane_order(values):
+        first, second = by_index(plane, values[:half], values[half:])
+        return jnp.concatenate([first, second])
+
+    up_own = plane_order(up_weight.T)
+    up_cross = swap(up_own[:half], "sec", 4)
+    carried = project(patch_tokens[0], skip_features[0], skip_weight)
+    normed = normalize(carried, norm_gain, norm_bias)
+    mine = lax.dynamic_slice_in_dim(normed, core * rows, rows, 0)
+    tok_z = swap(mine, "sec", 2)
+    tok_x = swap(mine, "sec", 1)
+    tok_d = swap(tok_z, "sec", 1)
+
+    down_own = plane_order(down_weight.T)
+    keep, give = by_index(core, down_own[:, :columns], down_own[:, columns:])
+    down_here = pair_order(core, keep, swap(give, "tp", 1), half)
+    bias_own = plane_order(up_bias.reshape(units, 1)).reshape(1, units)
+    bias_far = swap(bias_own, "sec", 4)
+    bias_pair = jnp.concatenate([bias_own, bias_far])
+    bias_other = swap(bias_pair, "tp", 1)
+
+    up_here = pair_order(core, up_own, swap(up_own, "tp", 1), half)
+    up_far_own = jnp.concatenate([up_cross, swap(up_cross, "rep", 1)])
+    up_far = pair_order(core, up_far_own, swap(up_far_own, "tp", 1), half)
+
+    def bias_row(i):
+        return pair_order(core, bias_pair[i], bias_other[i], half).reshape(1, -1)
+
+    cuts = [0, 384, 576, columns]
+    down_far = []
+    for j in range(3):
+        piece = down_here[:, cuts[j] : cuts[j + 1]]
+        if j < 2:
+            crossed = swap(piece[:units], "sec", 4)
+            down_far.append(jnp.concatenate([crossed, swap(crossed, "rep", 1)]))
+        else:
+            down_far.append(swap(piece, "sec", 4))
+
+    work = jnp.concatenate([mine, tok_x, tok_z, tok_d])
+
+    def hidden_of(weights, bias):
+        pre_act = lax.dot_general(
+            work, weights, (((1,), (1,)), ((), ())), preferred_element_type=jnp.float32
+        ) + bias.astype(jnp.float32)
+        return jax.nn.gelu(pre_act, approximate=False).astype(jnp.bfloat16)
+
+    hidden_here = hidden_of(up_here, bias_row(0))
+    hidden_far = hidden_of(up_far, bias_row(1))
+    all_here = jnp.concatenate([hidden_here, swap(hidden_here, "tp", 1)])
+    all_far = jnp.concatenate([hidden_far, swap(hidden_far, "tp", 1)])
+    sums_here = jnp.dot(all_here, down_here, preferred_element_type=jnp.float32)
+    totals = []
+    for j in range(3):
+        sums = sums_here[:, cuts[j] : cuts[j + 1]] + jnp.dot(
+            all_far, down_far[j], preferred_element_type=jnp.float32
+        )
+        sums = sums.reshape(2, 4, rows, -1)
+        total = sums[:, 0]
+        for k, mask in ((1, 1), (2, 2), (3, 3)):
+            total = total + swap(sums[:, k].astype(jnp.bfloat16), "sec", mask).astype(jnp.float32)
+        totals.append(total)
+    mlp = jnp.concatenate(totals, axis=2)
+    mlp = jnp.concatenate(by_index(core, mlp[0], mlp[1]))
+    residual = lax.dynamic_slice_in_dim(carried, core * columns, columns, 1)
+    result = (residual.astype(jnp.float32) + mlp + down_bias).astype(jnp.bfloat16)
+    leaving = jnp.any(jnp.concatenate([exit_first, exit_second]) == own_index)
+    return jnp.where(leaving, jnp.zeros_like(result), result)[None]
+
+
 def select_images(selector, values):
     picked = jnp.einsum("ki,itd->ktd", selector, values, preferred_element_type=jnp.float32)
     return picked.astype(values.dtype)
 
 
-def local(
+def gather_plan(
     patch_tokens,
     skip_features,
     exit_first,
@@ -118,4 +223,6 @@
         P("tp"),
     )
     out_specs = P(("rep", "sec"), None, "tp")
+    sizes = (mesh.shape["rep"], mesh.shape["sec"], mesh.shape["tp"])
+    local = square_plan if sizes == (2, 8, 2) else gather_plan
     return jax.shard_map(local, mesh=mesh, in_specs=in_specs, out_specs=out_specs, check_vma=False)

time: 251 us -> 119 us (0.47)
  waiting for transfers between devices: 143 us -> 38.3 us
  blocking collectives: 44.8 us -> 0 us
  between operations: 17.4 us -> 0.35 us
  other arithmetic: 4.47 us -> 16.6 us
  starting transfers between devices: 14.3 us -> 25.3 us
  local copies, waits for them, and re-layouts: 10.2 us -> 18.3 us
  matrix products: 16.2 us -> 18.9 us
    all_gather x2 -> x0, waiting for transfers between devices: 99.8 us -> none  [the longest x1 85.3 us: local(): down_piece = lax.all_gather(down_weight, 'sec', axis=1, tiled=True)]
    unnamed x2 -> x0, blocking collectives: 44.8 us -> none
    ppermute x0 -> x26, waiting for transfers between devices: none -> 38.3 us  [swap(): return lax.ppermute(values, axis, [(i, i ^ mask) for i in range(size)])]
    all_to_all x3 -> x0, waiting for transfers between devices: 35 us -> none  [the longest x1 23.6 us: local(): lax.all_to_all(pack(patch_tokens), 'sec', split_axis=1, concat_axis=1, ti...]
    ppermute x0 -> x26, starting transfers between devices: none -> 25.3 us  [swap(): return lax.ppermute(values, axis, [(i, i ^ mask) for i in range(size)])]
    all_to_all x3 -> x0, starting transfers between devices: 14.2 us -> none  [the longest x1 5.76 us: local(): lax.all_to_all(returning.reshape(per_peer, n_sec, columns), 'sec', split_...]
    dot_general x2 -> x6, matrix products: 4.52 us -> 16.5 us  [the longest x2 7.95 us: hidden_of(): lax.dot_general(work, weights, (((1,), (1,)), ((), ())), preferred_elemen...]
    unnamed x1 -> x0, matrix products: 9.41 us -> none
  transfers between devices with their start and end apart: 6 -> 26, of which waited for: 5 -> 9; matrix products, arithmetic and copies ran while one was open for 6% -> 34% of each run, Pallas kernels for 0% -> 0%
where the time goes in v1:
time: 119 us; the launch traced here: 118 us
  waiting for transfers between devices  38.3 us (32%)
  starting transfers between devices  25.3 us (21%)
  matrix products  18.9 us (16%)
  local copies, waits for them, and re-layouts  18.3 us (15%)
  other arithmetic  16.6 us (14%)
    ppermute x26, waiting for transfers between devices, swap(): return lax.ppermute(values, axis, [(i, i ^ mask) for i in range(size)])  38.3 us
    ppermute x26, starting transfers between devices, swap(): return lax.ppermute(values, axis, [(i, i ^ mask) for i in range(size)])  25.3 us
    dot_general x2, matrix products, hidden_of(): lax.dot_general(work, weights, (((1,), (1,)), ((), ())), preferred_elemen...  7.95 us
    dot_general x3, matrix products, square_plan(): jnp.dot(all_far, down_far[j], preferred_element_type=jnp.float32)  7.61 us
    unnamed x33, local copies, waits for them, and re-layouts  6.95 us
    reshape x2, local copies, waits for them, and re-layouts, square_plan(): sums = sums.reshape(2, 4, rows, -1)  4.85 us
    select_n x9, other arithmetic, by_index(): jnp.where(index == 0, own, other)  4.79 us
    add x2, local copies, waits for them, and re-layouts, square_plan(): sums_here[:, cuts[j]:cuts[j + 1]]  4.29 us
  transfers between devices with their start and end apart: 26, of which 9 were waited for; matrix products, arithmetic and copies ran while one was open for 34% of the time, Pallas kernels for 0%

profile of v1, /device:TPU:0, one launch (start us, length us, event | category | flops | bytes accessed | tf_op | source)
XLA Modules:
  0.0 117.7 jit_solution(17615493264016601381)
XLA Ops:
  0.0 1.8 %copy-done = bf16[1024,1408]{1,0:T(8,128)(2,1)S(1)} copy-done((bf16[1024,1408]{1,0:T(8,128)(2,1)S(1)}, bf16[1024,1408]{1,0:T(8,128)(2,1)}, u32[]{:S(2)}) %copy-start) | copy-done | bytes 2883608
  1.8 2.3 %convert_reduce_fusion = (f32[256]{0:T(256)S(1)}, bf16[256,1408]{1,0:T(8,128)(2,1)S(1)}) fusion(bf16[1024,1408]{1,0:T(8,128)(2,1)S(1)} %copy-done, bf16[1,256,1024]{2,1,0:T(8,128)(2,1)} %param.12, bf16[1,256,1408]{2,1,0:T(8,128)(2,1)} %param.11), kind=kOutput, calls=%fused_computation.3 | convolution fusion | flops 739999488 | bytes 4850688 | tf_op jit(solution)/shard_map/dot_general | solution.py:8
  4.2 0.8 copy-done.4
  5.0 1.4 %multiply_reduce_fusion = (f32[256]{0:T(256)S(1)}, f32[256,1408]{1,0:T(8,128)}) fusion(f32[256]{0:T(256)S(1)} %broadcast_multiply_fusion, bf16[256,1408]{1,0:T(8,128)(2,1)S(1)} %get-tuple-element.58), kind=kLoop, calls=%fused_computation.6 | loop fusion | flops 1441536 | bytes 2164736 | tf_op jit(solution)/shard_map/reduce_sum | solution.py:18
  6.5 2.0 %fusion.43 = bf16[128,1408]{1,0:T(8,128)(2,1)} fusion(f32[256,1408]{1,0:T(8,128)} %get-tuple-element.17, s32[]{:T(128)S(6)} %select_n.137, f32[1408]{0:T(1024)S(1)} %copy-done.10, f32[1408]{0:T(1024)S(1)} %copy-done.11, f32[128]{0:T(128)S(1)} %dynamic-slice), kind=kLoop, calls=%fused_computation.74 | loop fusion | flops 720896 | bytes 1093124 | tf_op jit(solution)/shard_map/convert_element_type | solution.py:19
  8.5 3.0 %collective-permute-start.1 = (bf16[128,1408]{1,0:T(8,128)(2,1)}, bf16[128,1408]{1,0:T(8,128)(2,1)}, u32[]{:S(2)}, u32[]{:S(2)}) collective-permute-start(bf16[128,1408]{1,0:T(8,128)(2,1)} %fusion.43), channel_id=1, source_target_pairs={{0,4},{2,6},{4,0},{6,2},{8,12},{10,14},{12,8},{14,10},{1,5},{3,7},... | collective-permute-start | bytes 1081352 | tf_op jit(solution)/shard_map/ppermute | solution.py:24
  11.5 1.5 %collective-permute-start = (bf16[128,1408]{1,0:T(8,128)(2,1)}, bf16[128,1408]{1,0:T(8,128)(2,1)}, u32[]{:S(2)}, u32[]{:S(2)}) collective-permute-start(bf16[128,1408]{1,0:T(8,128)(2,1)} %fusion.43), channel_id=1, source_target_pairs={{0,2},{2,0},{4,6},{6,4},{8,10},{10,8},{12,14},{14,12},{1,3},{3,1},... | collective-permute-start | bytes 1081352 | tf_op jit(solution)/shard_map/ppermute | solution.py:24
  13.2 2.7 %collective-permute-start.4 = (bf16[1,224]{1,0:T(2,128)(2,1)S(1)}, bf16[1,224]{1,0:T(2,128)(2,1)S(1)}, u32[]{:S(2)}, u32[]{:S(2)}) collective-permute-start(bf16[1,224]{1,0:T(2,128)(2,1)S(1)} %get-tuple-element.50), channel_id=1, source_target_pairs={{0,8},{2,10},{4,12},{6,14},{8,0},{10,2},{12,4},{14,6},{1,9},{3,11}... | collective-permute-start | bytes 1352 | tf_op jit(solution)/shard_map/ppermute | solution.py:24
  15.9 0.9 broadcast_select_fusion.11
  16.8 0.3 collective-permute-start.8
  17.1 1.2 broadcast_select_fusion.9
  18.3 0.9 broadcast_select_fusion.6
  19.2 1.5 %collective-permute-done.4 = bf16[1,224]{1,0:T(2,128)(2,1)S(1)} collective-permute-done((bf16[1,224]{1,0:T(2,128)(2,1)S(1)}, bf16[1,224]{1,0:T(2,128)(2,1)S(1)}, u32[]{:S(2)}, u32[]{:S(2)}) %collective-permute-start.4) | collective-permute-done | bytes 480 | tf_op jit(solution)/shard_map/ppermute | solution.py:24
  20.8 1.8 %pad_maximum_fusion.3 = bf16[224,1408]{1,0:T(8,128)(2,1)} fusion(bf16[112,1408]{1,0:T(8,128)(2,1)S(1)} %copy-done.2, bf16[112,1408]{1,0:T(8,128)(2,1)} %get-tuple-element.28), kind=kLoop, calls=%fused_computation.82 | loop fusion | flops 1261568 | bytes 1261568 | tf_op jit(solution)/shard_map/concatenate | solution.py:60
  22.6 0.8 compare_reduce_fusion
  23.4 0.5 collective-permute-start.3
  24.3 8.9 %collective-permute-done.8 = bf16[112,1408]{1,0:T(8,128)(2,1)} collective-permute-done((bf16[112,1408]{1,0:T(8,128)(2,1)}, bf16[112,1408]{1,0:T(8,128)(2,1)}, u32[]{:S(2)}, u32[]{:S(2)}) %collective-permute-start.8) | collective-permute-done | bytes 315424 | tf_op jit(solution)/shard_map/ppermute | solution.py:24
  33.1 1.5 %collective-permute-start.9 = (bf16[112,1408]{1,0:T(8,128)(2,1)}, bf16[112,1408]{1,0:T(8,128)(2,1)S(1)}, u32[]{:S(2)}, u32[]{:S(2)}) collective-permute-start(bf16[112,1408]{1,0:T(8,128)(2,1)} %collective-permute-done.8), channel_id=1, source_target_pairs={{0,16},{16,0},{1,17},{17,1},{2,18},{18,2},{3,19},{19,3},{4,20},{20... | collective-permute-start | bytes 946184 | tf_op jit(solution)/shard_map/ppermute | solution.py:24
  34.7 1.3 %broadcast_select_fusion.5 = (bf16[224,704]{1,0:T(8,128)(2,1)S(1)}, bf16[224,704]{1,0:T(8,128)(2,1)S(1)}) fusion(bf16[224,704]{1,0:T(8,128)(2,1)} %collective-permute-done.7, pred[]{:T(512)S(6)} %eq.10, bf16[112,1408]{1,0:T(8,128)(2,1)S(1)} %get-tuple-element.23, bf16[112,1408]{1,0:T(8,128)(2,1)S(1)} %get-tuple-element.22), kind=kLoop, calls=%fused_computation.107 | loop fusion | flops 2523136 | bytes 1576961 | tf_op jit(solution)/shard_map/jit(_where)/select_n | solution.py:28
  35.9 1.0 constant_dynamic-update-slice_fusion.1
  37.0 0.6 collective-permute-start.2
  37.6 3.3 %collective-permute-done.9 = bf16[112,1408]{1,0:T(8,128)(2,1)S(1)} collective-permute-done((bf16[112,1408]{1,0:T(8,128)(2,1)}, bf16[112,1408]{1,0:T(8,128)(2,1)S(1)}, u32[]{:S(2)}, u32[]{:S(2)}) %collective-permute-start.9) | collective-permute-done | bytes 315424 | tf_op jit(solution)/shard_map/ppermute | solution.py:24
  41.1 1.2 %broadcast_select_fusion.3 = (bf16[224,1408]{1,0:T(8,128)(2,1)S(1)}, bf16[224,1408]{1,0:T(8,128)(2,1)S(1)}) fusion(bf16[224,1408]{1,0:T(8,128)(2,1)S(1)} %collective-permute-done.3, pred[]{:T(512)S(6)} %eq.10, bf16[112,1408]{1,0:T(8,128)(2,1)S(1)} %copy-done.3, bf16[112,1408]{1,0:T(8,128)(2,1)} %get-tuple-element.28), kind=kLoop, calls=%fused_computation.88 | loop fusion | flops 1892352 | bytes 2523137 | tf_op jit(solution)/shard_map/jit(_where)/select_n | solution.py:28
  42.3 0.1 fusion.88
  42.4 3.2 %collective-permute-done.2 = bf16[128,1408]{1,0:T(8,128)(2,1)S(1)} collective-permute-done((bf16[128,1408]{1,0:T(8,128)(2,1)}, bf16[128,1408]{1,0:T(8,128)(2,1)S(1)}, u32[]{:S(2)}, u32[]{:S(2)}) %collective-permute-start.2) | collective-permute-done | bytes 360480 | tf_op jit(solution)/shard_map/ppermute | solution.py:24
  45.6 4.0 %fusion.17 = bf16[512,448]{0,1:T(8,128)(2,1)S(1)} fusion(bf16[112,1408]{1,0:T(8,128)(2,1)S(1)} %get-tuple-element.63, bf16[112,1408]{1,0:T(8,128)(2,1)S(1)} %get-tuple-element.25, bf16[112,1408]{1,0:T(8,128)(2,1)S(1)} %get-tuple-element.64, bf16[112,1408]{1,0:T(8,128)(2,1)S(1)} %get-tuple-element.24, f32[448]{0:T(512)S(1)} %maximum_convert_fusion, ...), kind=kOutput, calls=%fused_computation.28 | convolution fusion | flops 671875072 | bytes 3163904 | tf_op jit(solution)/shard_map/dot_general | solution.py:99
  49.8 0.1 fusion.86
  49.9 4.0 %fusion.20 = bf16[512,448]{0,1:T(8,128)(2,1)S(1)} fusion(bf16[112,1408]{1,0:T(8,128)(2,1)S(1)} %get-tuple-element.67, bf16[112,1408]{1,0:T(8,128)(2,1)S(1)} %get-tuple-element.19, bf16[112,1408]{1,0:T(8,128)(2,1)S(1)} %get-tuple-element.68, bf16[112,1408]{1,0:T(8,128)(2,1)S(1)} %get-tuple-element.18, f32[448]{0:T(512)S(1)} %maximum_convert_fusion.1, ...), kind=kOutput, calls=%fused_computation.31 | convolution fusion | flops 671875072 | bytes 3163904 | tf_op jit(solution)/shard_map/dot_general | solution.py:99
  53.9 0.5 collective-permute-start.11
  54.6 3.0 %collective-permute-start.17 = (bf16[224,192]{1,0:T(8,128)(2,1)S(1)}, bf16[224,192]{1,0:T(8,128)(2,1)}, u32[]{:S(2)}, u32[]{:S(2)}) collective-permute-start(bf16[224,192]{1,0:T(8,128)(2,1)S(1)} %pad_maximum_fusion.13), channel_id=1, source_target_pairs={{0,8},{2,10},{4,12},{6,14},{8,0},{10,2},{12,4},{14,6},{1,9},{3,11}... | collective-permute-start | bytes 258056 | tf_op jit(solution)/shard_map/ppermute | solution.py:24
  57.7 12.8 %collective-permute-done.17 = bf16[224,192]{1,0:T(8,128)(2,1)} collective-permute-done((bf16[224,192]{1,0:T(8,128)(2,1)S(1)}, bf16[224,192]{1,0:T(8,128)(2,1)}, u32[]{:S(2)}, u32[]{:S(2)}) %collective-permute-start.17) | collective-permute-done | bytes 86048 | tf_op jit(solution)/shard_map/ppermute | solution.py:24
  70.5 0.5 collective-permute-start.18
  71.0 1.5 %collective-permute-start.13 = (bf16[224,384]{1,0:T(8,128)(2,1)}, bf16[224,384]{1,0:T(8,128)(2,1)}, u32[]{:S(2)}, u32[]{:S(2)}) collective-permute-start(bf16[224,384]{1,0:T(8,128)(2,1)} %collective-permute-done.12), channel_id=1, source_target_pairs={{0,16},{16,0},{1,17},{17,1},{2,18},{18,2},{3,19},{19,3},{4,20},{20... | collective-permute-start | bytes 516104 | tf_op jit(solution)/shard_map/ppermute | solution.py:24
  72.5 1.0 fusion.21
  73.5 1.5 %copy-done.6 = f32[1024,704]{0,1:T(8,128)} copy-done((f32[1024,704]{0,1:T(8,128)}, f32[1024,704]{0,1:T(8,128)S(1)}, u32[]{:S(2)}) %copy-start.6) | copy-done | bytes 2883608
  75.1 0.8 copy-done.9
  75.9 1.2 slice_add_fusion.1
  77.0 1.2 %copy.22 = f32[1024,128]{1,0:T(8,128)S(1)} copy(f32[1024,128]{0,1:T(8,128)} %slice_add_fusion.1) | data formatting | bytes 1048576 | tf_op jit(solution)/shard_map/add | solution.py:111
  78.3 0.7 slice_bitcast_fusion.11
  79.0 0.9 collective-permute-start.23
  79.8 1.2 collective-permute-start.25
  81.0 1.5 %collective-permute-start.24 = (bf16[2,128,128]{2,1,0:T(8,128)(2,1)}, bf16[2,128,128]{2,1,0:T(8,128)(2,1)}, u32[]{:S(2)}, u32[]{:S(2)}) collective-permute-start(bf16[2,128,128]{2,1,0:T(8,128)(2,1)} %get-tuple-element.39), channel_id=1, source_target_pairs={{0,4},{2,6},{4,0},{6,2},{8,12},{10,14},{12,8},{14,10},{1,5},{3,7},... | collective-permute-start | bytes 196616 | tf_op jit(solution)/shard_map/ppermute | solution.py:24
  82.4 3.6 %slice_add_fusion = f32[1024,384]{0,1:T(8,128)} fusion(f32[1024,704]{0,1:T(8,128)} %copy-done.6, bf16[224,384]{1,0:T(8,128)(2,1)} %collective-permute-done.13, bf16[224,384]{1,0:T(8,128)(2,1)} %collective-permute-done.12, bf16[512,448]{0,1:T(8,128)(2,1)} %copy-done.9, bf16[512,448]{0,1:T(8,128)(2,1)} %copy-done.8), kind=kOutput, calls=%fused_computation.4 | convolution fusion | flops 355237888 | bytes 4407296 | tf_op jit(solution)/shard_map/dot_general | solution.py:111
  86.1 3.1 %copy.16 = f32[1024,384]{1,0:T(8,128)} copy(f32[1024,384]{0,1:T(8,128)} %slice_add_fusion) | data formatting | bytes 3145728 | tf_op jit(solution)/shard_map/add | solution.py:111
  89.1 2.8 %convolution_add_fusion.3 = f32[1024,192]{0,1:T(8,128)} fusion(f32[1024,704]{0,1:T(8,128)} %copy-done.6, bf16[512,448]{0,1:T(8,128)(2,1)} %copy-done.9, bf16[512,448]{0,1:T(8,128)(2,1)} %copy-done.8, bf16[224,192]{1,0:T(8,128)(2,1)} %collective-permute-done.18, bf16[224,192]{1,0:T(8,128)(2,1)} %collective-permute-done.17), kind=kOutput, calls=%fused_computation.11 | convolution fusion | flops 178536448 | bytes 2662400 | tf_op jit(solution)/shard_map/dot_general | solution.py:111
  92.0 2.4 %reshape.119 = f32[2,4,128,192]{2,1,0,3:T(4,128)} reshape(f32[1024,192]{0,1:T(8,128)} %convolution_add_fusion.3) | data formatting | bytes 1572864 | tf_op jit(solution)/shard_map/reshape | solution.py:114
  94.3 2.5 %copy.19 = f32[2,4,128,192]{3,2,0,1:T(8,128)} copy(f32[2,4,128,192]{2,1,0,3:T(4,128)} %reshape.119) | data formatting | bytes 1572864 | tf_op jit(solution)/shard_map/reshape | solution.py:114
  96.8 1.4 %convert.17 = bf16[2,4,128,192]{3,2,0,1:T(8,128)(2,1)S(1)} convert(f32[2,4,128,192]{3,2,0,1:T(8,128)} %copy.19) | non-fusion elementwise | flops 196608 | bytes 1179648 | tf_op jit(solution)/shard_map/convert.6
  98.3 0.9 collective-permute-start.19
  99.2 1.2 collective-permute-start.21
  100.4 1.5 %collective-permute-start.20 = (bf16[2,128,192]{2,1,0:T(8,128)(2,1)S(1)}, bf16[2,128,192]{2,1,0:T(8,128)(2,1)S(1)}, u32[]{:S(2)}, u32[]{:S(2)}) collective-permute-start(bf16[2,128,192]{2,1,0:T(8,128)(2,1)S(1)} %get-tuple-element.32), channel_id=1, source_target_pairs={{0,4},{2,6},{4,0},{6,2},{8,12},{10,14},{12,8},{14,10},{1,5},{3,7},... | collective-permute-start | bytes 294920 | tf_op jit(solution)/shard_map/ppermute | solution.py:24
  102.0 0.9 collective-permute-start.14
  102.8 1.2 collective-permute-start.16
  104.0 0.9 fusion.75
  104.9 3.8 %collective-permute-done.19 = bf16[2,128,192]{2,1,0:T(8,128)(2,1)S(1)} collective-permute-done((bf16[2,128,192]{2,1,0:T(8,128)(2,1)S(1)}, bf16[2,128,192]{2,1,0:T(8,128)(2,1)S(1)}, u32[]{:S(2)}, u32[]{:S(2)}) %collective-permute-start.19) | collective-permute-done | bytes 98336 | tf_op jit(solution)/shard_map/ppermute | solution.py:24
  108.6 0.2 collective-permute-start.15
  108.8 0.3 collective-permute-done.20
  109.1 1.0 fusion.68
  110.1 3.5 %collective-permute-done.14 = bf16[2,128,384]{2,1,0:T(8,128)(2,1)S(1)} collective-permute-done((bf16[2,128,384]{2,1,0:T(8,128)(2,1)S(1)}, bf16[2,128,384]{2,1,0:T(8,128)(2,1)S(1)}, u32[]{:S(2)}, u32[]{:S(2)}) %collective-permute-start.14) | collective-permute-done | bytes 196640 | tf_op jit(solution)/shard_map/ppermute | solution.py:24
  113.6 1.1 collective-permute-done.15
  114.8 0.1 pad_maximum_fusion.2
  115.0 0.9 copy-done.5
  115.9 0.9 fusion.57
  116.8 0.9 copy.25
  (72 shorter events, 1.7 us)
Async XLA Ops:
  0.0 1.8 %copy-start = (bf16[1024,1408]{1,0:T(8,128)(2,1)S(1)}, bf16[1024,1408]{1,0:T(8,128)(2,1)}, u32[]{:S(2)}) copy-start(bf16[1024,1408]{1,0:T(8,128)(2,1)} %param.15) | copy-start | bytes 8650756
  4.1 0.9 copy-start.4
  4.2 2.4 %copy-start.10 = (f32[1408]{0:T(1024)S(1)}, f32[1408]{0:T(1024)}, u32[]{:S(2)}) copy-start(f32[1408]{0:T(1024)} %param.17) | copy-start | bytes 16900
  4.2 2.3 %copy-start.11 = (f32[1408]{0:T(1024)S(1)}, f32[1408]{0:T(1024)}, u32[]{:S(2)}) copy-start(f32[1408]{0:T(1024)} %param.16) | copy-start | bytes 16900
  5.0 8.0 %copy-start.13 = (bf16[224]{0:T(256)(128)(2,1)S(1)}, bf16[224]{0:T(256)(128)(2,1)}, u32[]{:S(2)}) copy-start(bf16[224]{0:T(256)(128)(2,1)} %param.19) | copy-start | bytes 1348
  5.0 10.8 %copy-start.7 = (bf16[1408,224]{0,1:T(8,128)(2,1)S(1)}, bf16[1408,224]{0,1:T(8,128)(2,1)}, u32[]{:S(2)}) copy-start(bf16[1408,224]{0,1:T(8,128)(2,1)} %param.18) | copy-start | bytes 1892356
  8.5 28.5 %collective-permute-start.1 = (bf16[128,1408]{1,0:T(8,128)(2,1)}, bf16[128,1408]{1,0:T(8,128)(2,1)}, u32[]{:S(2)}, u32[]{:S(2)}) collective-permute-start(bf16[128,1408]{1,0:T(8,128)(2,1)} %fusion.43), channel_id=1, source_target_pairs={{0,4},{2,6},{4,0},{6,2},{8,12},{10,14},{12,8},{14,10},{1,5},{3,7},... | collective-permute-start | bytes 1081352 | tf_op jit(solution)/shard_map/ppermute | solution.py:24
  11.5 30.9 %collective-permute-start = (bf16[128,1408]{1,0:T(8,128)(2,1)}, bf16[128,1408]{1,0:T(8,128)(2,1)}, u32[]{:S(2)}, u32[]{:S(2)}) collective-permute-start(bf16[128,1408]{1,0:T(8,128)(2,1)} %fusion.43), channel_id=1, source_target_pairs={{0,2},{2,0},{4,6},{6,4},{8,10},{10,8},{12,14},{14,12},{1,3},{3,1},... | collective-permute-start | bytes 1081352 | tf_op jit(solution)/shard_map/ppermute | solution.py:24
  13.2 7.5 %collective-permute-start.4 = (bf16[1,224]{1,0:T(2,128)(2,1)S(1)}, bf16[1,224]{1,0:T(2,128)(2,1)S(1)}, u32[]{:S(2)}, u32[]{:S(2)}) collective-permute-start(bf16[1,224]{1,0:T(2,128)(2,1)S(1)} %get-tuple-element.50), channel_id=1, source_target_pairs={{0,8},{2,10},{4,12},{6,14},{8,0},{10,2},{12,4},{14,6},{1,9},{3,11}... | collective-permute-start | bytes 1352 | tf_op jit(solution)/shard_map/ppermute | solution.py:24
  16.8 16.4 %collective-permute-start.8 = (bf16[112,1408]{1,0:T(8,128)(2,1)}, bf16[112,1408]{1,0:T(8,128)(2,1)}, u32[]{:S(2)}, u32[]{:S(2)}) collective-permute-start(bf16[112,1408]{1,0:T(8,128)(2,1)} %get-tuple-element.28), channel_id=1, source_target_pairs={{0,8},{2,10},{4,12},{6,14},{8,0},{10,2},{12,4},{14,6},{1,9},{3,11}... | collective-permute-start | bytes 946184 | tf_op jit(solution)/shard_map/ppermute | solution.py:24
  17.1 3.7 %copy-start.2 = (bf16[112,1408]{1,0:T(8,128)(2,1)S(1)}, bf16[112,1408]{1,0:T(8,128)(2,1)}, u32[]{:S(2)}) copy-start(bf16[112,1408]{1,0:T(8,128)(2,1)} %get-tuple-element.29) | copy-start | bytes 946180
  17.1 5.5 %copy-start.14 = (s32[2]{0:T(128)S(1)}, s32[2]{0:T(128)}, u32[]{:S(2)}) copy-start(s32[2]{0:T(128)} %param.14) | copy-start | bytes 28
  17.1 5.5 %copy-start.15 = (s32[2]{0:T(128)S(1)}, s32[2]{0:T(128)}, u32[]{:S(2)}) copy-start(s32[2]{0:T(128)} %param.13) | copy-start | bytes 28
  19.2 15.5 %collective-permute-start.7 = (bf16[224,704]{1,0:T(8,128)(2,1)}, bf16[224,704]{1,0:T(8,128)(2,1)}, u32[]{:S(2)}, u32[]{:S(2)}) collective-permute-start(bf16[224,704]{1,0:T(8,128)(2,1)} %broadcast_select_fusion.6), channel_id=1, source_target_pairs={{0,1},{1,0},{2,3},{3,2},{4,5},{5,4},{6,7},{7,6},{8,9},{9,8},{10,11... | collective-permute-start | bytes 946184 | tf_op jit(solution)/shard_map/ppermute | solution.py:24
  20.7 2.7 %collective-permute-start.5 = (bf16[2,224]{1,0:T(2,128)(2,1)S(1)}, bf16[2,224]{1,0:T(2,128)(2,1)S(1)}, u32[]{:S(2)}, u32[]{:S(2)}) collective-permute-start(bf16[2,224]{1,0:T(2,128)(2,1)S(1)} %pad_maximum_fusion.15), channel_id=1, source_target_pairs={{0,1},{1,0},{2,3},{3,2},{4,5},{5,4},{6,7},{7,6},{8,9},{9,8},{10,11... | collective-permute-start | bytes 2696 | tf_op jit(solution)/shard_map/ppermute | solution.py:24
  23.4 17.6 %collective-permute-start.3 = (bf16[224,1408]{1,0:T(8,128)(2,1)}, bf16[224,1408]{1,0:T(8,128)(2,1)S(1)}, u32[]{:S(2)}, u32[]{:S(2)}) collective-permute-start(bf16[224,1408]{1,0:T(8,128)(2,1)} %pad_maximum_fusion.3), channel_id=1, source_target_pairs={{0,1},{1,0},{2,3},{3,2},{4,5},{5,4},{6,7},{7,6},{8,9},{9,8},{10,11... | collective-permute-start | bytes 1892360 | tf_op jit(solution)/shard_map/ppermute | solution.py:24
  33.1 7.8 %collective-permute-start.9 = (bf16[112,1408]{1,0:T(8,128)(2,1)}, bf16[112,1408]{1,0:T(8,128)(2,1)S(1)}, u32[]{:S(2)}, u32[]{:S(2)}) collective-permute-start(bf16[112,1408]{1,0:T(8,128)(2,1)} %collective-permute-done.8), channel_id=1, source_target_pairs={{0,16},{16,0},{1,17},{17,1},{2,18},{18,2},{3,19},{19,3},{4,20},{20... | collective-permute-start | bytes 946184 | tf_op jit(solution)/shard_map/ppermute | solution.py:24
  35.9 5.1 %copy-start.3 = (bf16[112,1408]{1,0:T(8,128)(2,1)S(1)}, bf16[112,1408]{1,0:T(8,128)(2,1)}, u32[]{:S(2)}) copy-start(bf16[112,1408]{1,0:T(8,128)(2,1)} %get-tuple-element.29) | copy-start | bytes 946180
  37.0 8.5 %collective-permute-start.2 = (bf16[128,1408]{1,0:T(8,128)(2,1)}, bf16[128,1408]{1,0:T(8,128)(2,1)S(1)}, u32[]{:S(2)}, u32[]{:S(2)}) collective-permute-start(bf16[128,1408]{1,0:T(8,128)(2,1)} %collective-permute-done.1), channel_id=1, source_target_pairs={{0,2},{2,0},{4,6},{6,4},{8,10},{10,8},{12,14},{14,12},{1,3},{3,1},... | collective-permute-start | bytes 1081352 | tf_op jit(solution)/shard_map/ppermute | solution.py:24
  41.0 8.7 %collective-permute-start.10 = (bf16[224,1408]{1,0:T(8,128)(2,1)S(1)}, bf16[224,1408]{1,0:T(8,128)(2,1)S(1)}, u32[]{:S(2)}, u32[]{:S(2)}) collective-permute-start(bf16[224,1408]{1,0:T(8,128)(2,1)S(1)} %constant_dynamic-update-slice_fusion), channel_id=1, source_target_pairs={{0,1},{1,0},{2,3},{3,2},{4,5},{5,4},{6,7},{7,6},{8,9},{9,8},{10,11... | collective-permute-start | bytes 1892360 | tf_op jit(solution)/shard_map/ppermute | solution.py:24
  49.6 23.0 %collective-permute-start.6 = (bf16[512,448]{0,1:T(8,128)(2,1)S(1)}, bf16[512,448]{0,1:T(8,128)(2,1)S(1)}, u32[]{:S(2)}, u32[]{:S(2)}) collective-permute-start(bf16[512,448]{0,1:T(8,128)(2,1)S(1)} %fusion.17), channel_id=1, source_target_pairs={{0,1},{1,0},{2,3},{3,2},{4,5},{5,4},{6,7},{7,6},{8,9},{9,8},{10,11... | collective-permute-start | bytes 1376264 | tf_op jit(solution)/shard_map/ppermute | solution.py:24
  53.9 19.6 %copy-start.8 = (bf16[512,448]{0,1:T(8,128)(2,1)}, bf16[512,448]{0,1:T(8,128)(2,1)S(1)}, u32[]{:S(2)}) copy-start(bf16[512,448]{0,1:T(8,128)(2,1)S(1)} %fusion.20) | copy-start | bytes 1376260
  53.9 19.6 %collective-permute-start.11 = (bf16[512,448]{0,1:T(8,128)(2,1)S(1)}, bf16[512,448]{0,1:T(8,128)(2,1)S(1)}, u32[]{:S(2)}, u32[]{:S(2)}) collective-permute-start(bf16[512,448]{0,1:T(8,128)(2,1)S(1)} %fusion.20), channel_id=1, source_target_pairs={{0,1},{1,0},{2,3},{3,2},{4,5},{5,4},{6,7},{7,6},{8,9},{9,8},{10,11... | collective-permute-start | bytes 1376264 | tf_op jit(solution)/shard_map/ppermute | solution.py:24
  54.5 16.5 %collective-permute-start.12 = (bf16[224,384]{1,0:T(8,128)(2,1)S(1)}, bf16[224,384]{1,0:T(8,128)(2,1)}, u32[]{:S(2)}, u32[]{:S(2)}) collective-permute-start(bf16[224,384]{1,0:T(8,128)(2,1)S(1)} %fusion.72), channel_id=1, source_target_pairs={{0,8},{2,10},{4,12},{6,14},{8,0},{10,2},{12,4},{14,6},{1,9},{3,11}... | collective-permute-start | bytes 516104 | tf_op jit(solution)/shard_map/ppermute | solution.py:24
  54.6 15.9 %collective-permute-start.17 = (bf16[224,192]{1,0:T(8,128)(2,1)S(1)}, bf16[224,192]{1,0:T(8,128)(2,1)}, u32[]{:S(2)}, u32[]{:S(2)}) collective-permute-start(bf16[224,192]{1,0:T(8,128)(2,1)S(1)} %pad_maximum_fusion.13), channel_id=1, source_target_pairs={{0,8},{2,10},{4,12},{6,14},{8,0},{10,2},{12,4},{14,6},{1,9},{3,11}... | collective-permute-start | bytes 258056 | tf_op jit(solution)/shard_map/ppermute | solution.py:24
  57.6 15.9 %collective-permute-start.22 = (bf16[448,128]{1,0:T(8,128)(2,1)S(1)}, bf16[448,128]{1,0:T(8,128)(2,1)S(1)}, u32[]{:S(2)}, u32[]{:S(2)}) collective-permute-start(bf16[448,128]{1,0:T(8,128)(2,1)S(1)} %pad_maximum_fusion.12), channel_id=1, source_target_pairs={{0,8},{2,10},{4,12},{6,14},{8,0},{10,2},{12,4},{14,6},{1,9},{3,11}... | collective-permute-start | bytes 344072 | tf_op jit(solution)/shard_map/ppermute | solution.py:24
  70.5 18.6 %collective-permute-start.18 = (bf16[224,192]{1,0:T(8,128)(2,1)}, bf16[224,192]{1,0:T(8,128)(2,1)}, u32[]{:S(2)}, u32[]{:S(2)}) collective-permute-start(bf16[224,192]{1,0:T(8,128)(2,1)} %collective-permute-done.17), channel_id=1, source_target_pairs={{0,16},{16,0},{1,17},{17,1},{2,18},{18,2},{3,19},{19,3},{4,20},{20... | collective-permute-start | bytes 258056 | tf_op jit(solution)/shard_map/ppermute | solution.py:24
  71.0 11.4 %collective-permute-start.13 = (bf16[224,384]{1,0:T(8,128)(2,1)}, bf16[224,384]{1,0:T(8,128)(2,1)}, u32[]{:S(2)}, u32[]{:S(2)}) collective-permute-start(bf16[224,384]{1,0:T(8,128)(2,1)} %collective-permute-done.12), channel_id=1, source_target_pairs={{0,16},{16,0},{1,17},{17,1},{2,18},{18,2},{3,19},{19,3},{4,20},{20... | collective-permute-start | bytes 516104 | tf_op jit(solution)/shard_map/ppermute | solution.py:24
  73.5 1.6 %copy-start.6 = (f32[1024,704]{0,1:T(8,128)}, f32[1024,704]{0,1:T(8,128)S(1)}, u32[]{:S(2)}) copy-start(f32[1024,704]{0,1:T(8,128)S(1)} %fusion.21) | copy-start | bytes 8650756
  75.1 0.8 copy-start.9
  79.0 21.5 %collective-permute-start.23 = (bf16[2,128,128]{2,1,0:T(8,128)(2,1)}, bf16[2,128,128]{2,1,0:T(8,128)(2,1)S(1)}, u32[]{:S(2)}, u32[]{:S(2)}) collective-permute-start(bf16[2,128,128]{2,1,0:T(8,128)(2,1)} %get-tuple-element.37), channel_id=1, source_target_pairs={{0,2},{2,0},{4,6},{6,4},{8,10},{10,8},{12,14},{14,12},{1,3},{3,1},... | collective-permute-start | bytes 196616 | tf_op jit(solution)/shard_map/ppermute | solution.py:24
  79.8 22.1 %collective-permute-start.25 = (bf16[2,128,128]{2,1,0:T(8,128)(2,1)}, bf16[2,128,128]{2,1,0:T(8,128)(2,1)S(1)}, u32[]{:S(2)}, u32[]{:S(2)}) collective-permute-start(bf16[2,128,128]{2,1,0:T(8,128)(2,1)} %get-tuple-element.38), channel_id=1, source_target_pairs={{0,6},{2,4},{4,2},{6,0},{8,14},{10,12},{12,10},{14,8},{1,7},{3,5},... | collective-permute-start | bytes 196616 | tf_op jit(solution)/shard_map/ppermute | solution.py:24
  81.0 21.9 %collective-permute-start.24 = (bf16[2,128,128]{2,1,0:T(8,128)(2,1)}, bf16[2,128,128]{2,1,0:T(8,128)(2,1)}, u32[]{:S(2)}, u32[]{:S(2)}) collective-permute-start(bf16[2,128,128]{2,1,0:T(8,128)(2,1)} %get-tuple-element.39), channel_id=1, source_target_pairs={{0,4},{2,6},{4,0},{6,2},{8,12},{10,14},{12,8},{14,10},{1,5},{3,7},... | collective-permute-start | bytes 196616 | tf_op jit(solution)/shard_map/ppermute | solution.py:24
  96.8 3.5 %copy-start.1 = (f32[1024,384]{1,0:T(8,128)S(1)}, f32[1024,384]{1,0:T(8,128)}, u32[]{:S(2)}) copy-start(f32[1024,384]{1,0:T(8,128)} %copy.16) | copy-start | bytes 4718596
  98.3 10.4 %collective-permute-start.19 = (bf16[2,128,192]{2,1,0:T(8,128)(2,1)S(1)}, bf16[2,128,192]{2,1,0:T(8,128)(2,1)S(1)}, u32[]{:S(2)}, u32[]{:S(2)}) collective-permute-start(bf16[2,128,192]{2,1,0:T(8,128)(2,1)S(1)} %get-tuple-element.30), channel_id=1, source_target_pairs={{0,2},{2,0},{4,6},{6,4},{8,10},{10,8},{12,14},{14,12},{1,3},{3,1},... | collective-permute-start | bytes 294920 | tf_op jit(solution)/shard_map/ppermute | solution.py:24
  99.2 9.6 %collective-permute-start.21 = (bf16[2,128,192]{2,1,0:T(8,128)(2,1)S(1)}, bf16[2,128,192]{2,1,0:T(8,128)(2,1)S(1)}, u32[]{:S(2)}, u32[]{:S(2)}) collective-permute-start(bf16[2,128,192]{2,1,0:T(8,128)(2,1)S(1)} %get-tuple-element.31), channel_id=1, source_target_pairs={{0,6},{2,4},{4,2},{6,0},{8,14},{10,12},{12,10},{14,8},{1,7},{3,5},... | collective-permute-start | bytes 294920 | tf_op jit(solution)/shard_map/ppermute | solution.py:24
  100.4 8.6 %collective-permute-start.20 = (bf16[2,128,192]{2,1,0:T(8,128)(2,1)S(1)}, bf16[2,128,192]{2,1,0:T(8,128)(2,1)S(1)}, u32[]{:S(2)}, u32[]{:S(2)}) collective-permute-start(bf16[2,128,192]{2,1,0:T(8,128)(2,1)S(1)} %get-tuple-element.32), channel_id=1, source_target_pairs={{0,4},{2,6},{4,0},{6,2},{8,12},{10,14},{12,8},{14,10},{1,5},{3,7},... | collective-permute-start | bytes 294920 | tf_op jit(solution)/shard_map/ppermute | solution.py:24
  102.0 11.6 %collective-permute-start.14 = (bf16[2,128,384]{2,1,0:T(8,128)(2,1)S(1)}, bf16[2,128,384]{2,1,0:T(8,128)(2,1)S(1)}, u32[]{:S(2)}, u32[]{:S(2)}) collective-permute-start(bf16[2,128,384]{2,1,0:T(8,128)(2,1)S(1)} %get-tuple-element.13), channel_id=1, source_target_pairs={{0,2},{2,0},{4,6},{6,4},{8,10},{10,8},{12,14},{14,12},{1,3},{3,1},... | collective-permute-start | bytes 589832 | tf_op jit(solution)/shard_map/ppermute | solution.py:24
  102.8 10.7 %collective-permute-start.16 = (bf16[2,128,384]{2,1,0:T(8,128)(2,1)S(1)}, bf16[2,128,384]{2,1,0:T(8,128)(2,1)S(1)}, u32[]{:S(2)}, u32[]{:S(2)}) collective-permute-start(bf16[2,128,384]{2,1,0:T(8,128)(2,1)S(1)} %get-tuple-element.14), channel_id=1, source_target_pairs={{0,6},{2,4},{4,2},{6,0},{8,14},{10,12},{12,10},{14,8},{1,7},{3,5},... | collective-permute-start | bytes 589832 | tf_op jit(solution)/shard_map/ppermute | solution.py:24
  108.6 6.1 %collective-permute-start.15 = (bf16[2,128,384]{2,1,0:T(8,128)(2,1)S(1)}, bf16[2,128,384]{2,1,0:T(8,128)(2,1)S(1)}, u32[]{:S(2)}, u32[]{:S(2)}) collective-permute-start(bf16[2,128,384]{2,1,0:T(8,128)(2,1)S(1)} %get-tuple-element.15), channel_id=1, source_target_pairs={{0,4},{2,6},{4,0},{6,2},{8,12},{10,14},{12,8},{14,10},{1,5},{3,7},... | collective-permute-start | bytes 589832 | tf_op jit(solution)/shard_map/ppermute | solution.py:24
  114.8 1.1 copy-start.5
  114.8 1.1 copy-start.12

commit v2 on v0

--- a/solution.py
+++ b/solution.py
@@ -1,7 +1,421 @@
 import jax
 import jax.numpy as jnp
 from jax import lax
+from jax.experimental import pallas as pl
+from jax.experimental.pallas import tpu as pltpu
 from jax.sharding import PartitionSpec as P
+
+
+NT = (((1,), (1,)), ((), ()))
+CHUNKS = (384, 320)
+ANY = pl.BlockSpec(memory_space=pl.ANY)
+
+
+def swap(values, axis, mask):
+    size = lax.axis_size(axis)
+    return lax.ppermute(values, axis, [(i, i ^ mask) for i in range(size)])
+
+
+def after(values, *others):
+    return lax.optimization_barrier((values, *others))[0]
+
+
+def full(shape):
+    return pl.BlockSpec(shape, lambda *_: (0,) * len(shape))
+
+
+def call(kernel, out_shape, in_specs, out_specs, scratch_shapes=(), room=16):
+    return pl.pallas_call(
+        kernel,
+        out_shape=out_shape,
+        grid_spec=pltpu.PrefetchScalarGridSpec(
+            num_scalar_prefetch=1,
+            grid=(1,),
+            in_specs=in_specs,
+            out_specs=out_specs,
+            scratch_shapes=scratch_shapes,
+        ),
+        compiler_params=pltpu.CompilerParams(vmem_limit_bytes=room * 1024 * 1024),
+        cost_estimate=pl.CostEstimate(flops=1000, bytes_accessed=1000, transcendentals=0),
+    )
+
+
+def aligned(start, size):
+    return pl.ds(pl.multiple_of(start, 16), size)
+
+
+def front_kernel(
+    place, tokens, skips, weight, gain, shift, residual_out, normed_out, *scratch
+):
+    held_tokens, held_skips, held_weight, joined, sems = scratch
+    rows, width = normed_out.shape
+    columns = width // 2
+    depth = weight.shape[0]
+    steps = sems.shape[0] - 2
+    size = depth // steps
+    first = [
+        pltpu.make_async_copy(skips, held_skips, sems.at[steps]),
+        pltpu.make_async_copy(tokens, held_tokens, sems.at[steps + 1]),
+    ]
+    loads = [
+        pltpu.make_async_copy(
+            weight.at[pl.ds(i * size, size), :], held_weight.at[pl.ds(i * size, size), :], sems.at[i]
+        )
+        for i in range(steps)
+    ]
+    for copy in [first[0], *loads, first[1]]:
+        copy.start()
+    first[0].wait()
+    for i, copy in enumerate(loads):
+        copy.wait()
+        block = slice(i * size, (i + 1) * size)
+        product = jnp.dot(
+            held_skips[:, block], held_weight[block, :], preferred_element_type=jnp.float32
+        )
+        if i == 0:
+            joined[...] = product
+        else:
+            joined[...] += product
+    first[1].wait()
+    kept = (held_tokens[...].astype(jnp.float32) + joined[...]).astype(jnp.bfloat16)
+
+    @pl.when(place[0] == 0)
+    def _():
+        residual_out[...] = kept[:, :columns]
+
+    @pl.when(place[0] != 0)
+    def _():
+        residual_out[...] = kept[:, columns:]
+
+    kept = kept.astype(jnp.float32)
+    centered = kept - jnp.mean(kept, axis=1, keepdims=True)
+    spread = jnp.mean(centered * centered, axis=1, keepdims=True)
+    scaled = centered * lax.rsqrt(spread + 1e-06) * gain[...] + shift[...]
+    normed_out[...] = scaled.astype(jnp.bfloat16)
+
+
+def front(place, tokens, skips, weight, gain, shift):
+    rows, width = tokens.shape
+    depth = weight.shape[0]
+    return call(
+        front_kernel,
+        (
+            jax.ShapeDtypeStruct((rows, width // 2), jnp.bfloat16),
+            jax.ShapeDtypeStruct((rows, width), jnp.bfloat16),
+        ),
+        [ANY, ANY, ANY, full((width,)), full((width,))],
+        (full((rows, width // 2)), full((rows, width))),
+        [
+            pltpu.VMEM((rows, width), jnp.bfloat16),
+            pltpu.VMEM((rows, depth), jnp.bfloat16),
+            pltpu.VMEM((depth, width), jnp.bfloat16),
+            pltpu.VMEM((rows, width), jnp.float32),
+            pltpu.SemaphoreType.DMA((4,)),
+        ],
+        room=60,
+    )(place, tokens, skips, weight, gain, shift)
+
+
+def lead_kernel(place, tokens, skips, weight, gain, shift, mine_out, *scratch):
+    held_tokens, held_skips, held_weight, joined, sems = scratch
+    rows, width = mine_out.shape
+    depth = weight.shape[0]
+    steps = sems.shape[0] - 2
+    size = depth // steps
+    own = aligned(place[0] * rows, rows)
+    first = [
+        pltpu.make_async_copy(skips.at[own, :], held_skips, sems.at[steps]),
+        pltpu.make_async_copy(tokens.at[own, :], held_tokens, sems.at[steps + 1]),
+    ]
+    loads = [
+        pltpu.make_async_copy(
+            weight.at[pl.ds(i * size, size), :], held_weight.at[pl.ds(i * size, size), :], sems.at[i]
+        )
+        for i in range(steps)
+    ]
+    for copy in [first[0], *loads, first[1]]:
+        copy.start()
+    first[0].wait()
+    for i, copy in enumerate(loads):
+        copy.wait()
+        block = slice(i * size, (i + 1) * size)
+        product = jnp.dot(
+            held_skips[:, block], held_weight[block, :], preferred_element_type=jnp.float32
+        )
+        if i == 0:
+            joined[...] = product
+        else:
+            joined[...] += product
+    first[1].wait()
+    kept = (held_tokens[...].astype(jnp.float32) + joined[...]).astype(jnp.bfloat16)
+    kept = kept.astype(jnp.float32)
+    centered = kept - jnp.mean(kept, axis=1, keepdims=True)
+    spread = jnp.mean(centered * centered, axis=1, keepdims=True)
+    scaled = centered * lax.rsqrt(spread + 1e-06) * gain[...] + shift[...]
+    mine_out[...] = scaled.astype(jnp.bfloat16)
+
+
+def lead(place, tokens, skips, weight, gain, shift):
+    rows, width = tokens.shape
+    rows //= 2
+    depth = weight.shape[0]
+    return call(
+        lead_kernel,
+        jax.ShapeDtypeStruct((rows, width), jnp.bfloat16),
+        [ANY, ANY, ANY, full((width,)), full((width,))],
+        full((rows, width)),
+        [
+            pltpu.VMEM((rows, width), jnp.bfloat16),
+            pltpu.VMEM((rows, depth), jnp.bfloat16),
+            pltpu.VMEM((depth, width), jnp.bfloat16),
+            pltpu.VMEM((rows, width), jnp.float32),
+            pltpu.SemaphoreType.DMA((6,)),
+        ],
+        room=60,
+    )(place, tokens, skips, weight, gain, shift)
+
+
+def layout_kernel(place, own, given, *refs):
+    outs, scratch = refs[:-1], refs[-1]
+    units, columns = given.shape
+    half = units // 2
+    core, plane = place[0], place[1]
+
+    @pl.when(core == 0)
+    def _():
+        scratch[...] = own[:, :columns]
+
+    @pl.when(core != 0)
+    def _():
+        scratch[...] = own[:, columns:]
+
+    rows = aligned(plane * half, half)
+    for lane, source in enumerate((scratch, given)):
+        at = 0
+        for j, size in enumerate(CHUNKS):
+            here, message = outs[2 * j : 2 * j + 2]
+            here[lane * units : (lane + 1) * units, :] = source[:, at : at + size]
+            message[lane * half : (lane + 1) * half, :] = source[rows, at : at + size]
+            at += size
+
+
+def layout(place, own, given):
+    units, width = own.shape
+    columns = given.shape[1]
+    shapes = [(height, size) for size in CHUNKS for height in (2 * units, units)]
+    return call(
+        layout_kernel,
+        [jax.ShapeDtypeStruct(s, jnp.bfloat16) for s in shapes],
+        [full((units, width)), full((units, columns))],
+        [full(s) for s in shapes],
+        [pltpu.VMEM((units, columns), jnp.bfloat16)],
+        room=60,
+    )(place, own, given)
+
+
+def hidden_kernel(place, *refs):
+    out, tokens, held, token_sems, weight_sems = refs[-5:]
+    sources, weights, biases = refs[:-10], refs[-10:-7], refs[-7:-5]
+    images = out.shape[0] // (2 * sources[-1].shape[0])
+    rows = out.shape[0] // images
+    half = rows // 2
+    core = place[0]
+    copies = [[(sources[0], pl.ds(0, rows))]]
+    sources = sources[1:]
+    for k in range(0, len(sources), 2):
+        start = len(copies) * rows
+        copies.append(
+            [
+                (sources[k], aligned(start + core * half, half)),
+                (sources[k + 1], aligned(start + (1 - core) * half, half)),
+            ]
+        )
+    count = 0
+    for pair in copies:
+        for k, (source, block) in enumerate(pair):
+            pair[k] = pltpu.make_async_copy(source, tokens.at[block, :], token_sems.at[count])
+            count += 1
+    loads = []
+    at = 0
+    for k, source in enumerate(weights):
+        height = source.shape[0]
+        block = pl.ds(at, height)
+        loads.append(pltpu.make_async_copy(source, held.at[block, :], weight_sems.at[k]))
+        at += height
+    for copy in loads + sum(copies, []):
+        copy.start()
+    for copy in loads:
+        copy.wait()
+    units = biases[0].shape[1]
+    for k, pair in enumerate(copies):
+        for copy in pair:
+            copy.wait()
+        block = pl.ds(k * rows, rows)
+        for j, bias in enumerate(biases):
+            lanes = slice(j * units, (j + 1) * units)
+            pre_act = (
+                lax.dot_general(
+                    tokens[block, :], held[lanes, :], NT, preferred_element_type=jnp.float32
+                )
+                + bias[...].astype(jnp.float32)
+            )
+            scaled = 0.5 * pre_act * (1.0 + lax.erf(pre_act * (0.5**0.5)))
+            out[block, lanes] = scaled.astype(jnp.bfloat16)
+
+
+def hidden_of(place, normed, halves, weights, biases):
+    rows, width = halves[0].shape
+    images = len(halves) // 2 + 1
+    units = biases[0].shape[1]
+    sources = [normed, *halves]
+    return call(
+        hidden_kernel,
+        jax.ShapeDtypeStruct((images * 2 * rows, 2 * units), jnp.bfloat16),
+        [ANY] * (len(sources) + 3) + [full((1, units))] * 2,
+        full((images * 2 * rows, 2 * units)),
+        [
+            pltpu.VMEM((images * 2 * rows, width), jnp.bfloat16),
+            pltpu.VMEM((2 * units, width), jnp.bfloat16),
+            pltpu.SemaphoreType.DMA((len(sources),)),
+            pltpu.SemaphoreType.DMA((3,)),
+        ],
+    )(place, *sources, *weights, *biases)
+
+
+def down_kernel(place, ours, theirs, weights, near, crossed, *refs):
+    outs, (held, sems) = refs[:-2], refs[-2:]
+    units = held.shape[1] // 2
+    half = units // 2
+    rows = outs[0].shape[0]
+    copies = []
+    for lane in range(2):
+        copies.append((weights.at[pl.ds(lane * units, units), :], held.at[lane, pl.ds(0, units), :]))
+        for part, source in enumerate((near, crossed)):
+            copies.append(
+                (
+                    source.at[pl.ds(lane * half, half), :],
+                    held.at[lane, pl.ds(units + part * half, half), :],
+                )
+            )
+    copies = [pltpu.make_async_copy(a, b, sems.at[k]) for k, (a, b) in enumerate(copies)]
+    for copy in copies:
+        copy.start()
+    for copy in copies:
+        copy.wait()
+    for k, out in enumerate(outs):
+        block = pl.ds(k * rows, rows)
+        total = jnp.dot(ours[block, :], held[0], preferred_element_type=jnp.float32)
+        total += jnp.dot(theirs[block, :], held[1], preferred_element_type=jnp.float32)
+        out[...] = total.astype(out.dtype)
+
+
+def down(place, ours, theirs, weights, near, crossed):
+    height, units = ours.shape
+    size = weights.shape[1]
+    out = (height // 4, size)
+    types = [jnp.float32] + [jnp.bfloat16] * 3
+    return call(
+        down_kernel,
+        [jax.ShapeDtypeStruct(out, t) for t in types],
+        [full((height, units))] * 2 + [ANY] * 3,
+        [full(out)] * len(types),
+        [pltpu.VMEM((2, units, size), jnp.bfloat16), pltpu.SemaphoreType.DMA((6,))],
+    )(place, ours, theirs, weights, near, crossed)
+
+
+def final_kernel(place, first, second, residual, bias, *refs):
+    out = refs[-1]
+    left = jnp.int32(0)
+    for listed in (first, second):
+        for i in range(listed.shape[0]):
+            left += (listed[i] == place[2]).astype(jnp.int32)
+
+    @pl.when(left != 0)
+    def _():
+        out[...] = jnp.zeros_like(out)
+
+    @pl.when(left == 0)
+    def _():
+        at = 0
+        for j, size in enumerate(CHUNKS):
+            own, *others = refs[4 * j : 4 * j + 4]
+            total = own[...]
+            for other in others:
+                total = total + other[...].astype(jnp.float32)
+            total = total + residual[:, at : at + size].astype(jnp.float32)
+            total = total + bias[at : at + size]
+            out[:, at : at + size] = total.astype(jnp.bfloat16)
+            at += size
+
+
+def final(place, first, second, residual, bias, parts):
+    rows, columns = residual.shape
+    scalars = pl.BlockSpec(memory_space=pltpu.SMEM)
+    return call(
+        final_kernel,
+        jax.ShapeDtypeStruct((rows, columns), jnp.bfloat16),
+        [scalars] * 2 + [full((rows, columns)), full((columns,))] + [full(p.shape) for p in parts],
+        full((rows, columns)),
+    )(place, first, second, residual, bias, *parts)
+
+
+def square_plan(
+    patch_tokens,
+    skip_features,
+    exit_first,
+    exit_second,
+    skip_weight,
+    norm_gain,
+    norm_bias,
+    up_weight,
+    up_bias,
+    down_weight,
+    down_bias,
+):
+    core = lax.axis_index("tp")
+    plane = lax.axis_index("rep")
+    place = jnp.stack([core, plane, lax.axis_index("sec")]).astype(jnp.int32)
+    width = patch_tokens.shape[2]
+    units = up_weight.shape[1]
+    half = units // 2
+    columns = width // 2
+
+    up_own = up_weight.T
+    down_own = down_weight.T
+    up_half = lax.dynamic_slice_in_dim(up_own, plane * half, half, 0)
+    cross_a = swap(up_half, "sec", 4)
+    inputs = (patch_tokens[0], skip_features[0], skip_weight, norm_gain, norm_bias)
+    mine = lead(place, *inputs)
+    tok_x = swap(mine, "sec", 1)
+    tok_z = swap(mine, "sec", 2)
+    give = jnp.where(core == 0, down_own[:, columns:], down_own[:, :columns])
+    here_0, message_0, here_1, message_1 = layout(after(place, mine), down_own, swap(give, "tp", 1))
+    residual, normed = front(after(place, message_0), *inputs)
+    cross_a, tok_x, tok_z, residual = lax.optimization_barrier((cross_a, tok_x, tok_z, residual))
+    tok_d = swap(tok_z, "sec", 1)
+    pair_x = swap(tok_x, "tp", 1)
+    pair_z = swap(tok_z, "tp", 1)
+    pair_d = swap(tok_d, "tp", 1)
+    cross_b = swap(after(cross_a, mine), "rep", 1)
+    near_0 = swap(message_0, "sec", 4)
+    near_1 = swap(message_1, "sec", 4)
+    pair_z = swap(after(tok_z, near_0), "tp", 1)
+    bias_own = up_bias.reshape(1, units)
+    bias_far = swap(bias_own, "sec", 4)
+    bias_far = jnp.where(
+        plane == 0, bias_far, jnp.concatenate([bias_far[:, half:], bias_far[:, :half]], axis=1)
+    )
+    halves = (tok_x, pair_x, tok_z, pair_z, tok_d, pair_d)
+    ours = hidden_of(place, normed, halves, (up_own, cross_a, cross_b), (bias_own, bias_far))
+    theirs = swap(after(ours, near_1), "tp", 1)
+    crossed_0 = swap(near_0, "rep", 1)
+    crossed_1 = swap(near_1, "rep", 1)
+    sums_0 = down(place, ours, theirs, here_0, near_0, crossed_0)
+    sums_1 = down(after(place, sums_0[0]), ours, theirs, here_1, near_1, crossed_1)
+    parts = []
+    for own, *sent in (sums_0, sums_1):
+        parts += [own, *(swap(part, "sec", mask) for mask, part in enumerate(sent, 1))]
+    return final(place, exit_first, exit_second, residual, down_bias, parts)[None]
 
 
 def project(tokens_rows, skip_rows, skip_weight):
@@ -24,7 +438,7 @@
     return picked.astype(values.dtype)
 
 
-def local(
+def gather_plan(
     patch_tokens,
     skip_features,
     exit_first,
@@ -118,4 +532,6 @@
         P("tp"),
     )
     out_specs = P(("rep", "sec"), None, "tp")
+    sizes = (mesh.shape["rep"], mesh.shape["sec"], mesh.shape["tp"])
+    local = square_plan if sizes == (2, 8, 2) else gather_plan
     return jax.shard_map(local, mesh=mesh, in_specs=in_specs, out_specs=out_specs, check_vma=False)

time: 251 us -> 87 us (0.35)
  waiting for transfers between devices: 143 us -> 35 us
  blocking collectives: 44.8 us -> 0 us
  Pallas kernels: 0 us -> 26.1 us
  between operations: 17.4 us -> 0.27 us
  matrix products: 16.2 us -> 0 us
  local copies, waits for them, and re-layouts: 10.2 us -> 4.87 us
  starting transfers between devices: 14.3 us -> 19.6 us
  other arithmetic: 4.47 us -> 0.86 us
    all_gather x2 -> x0, waiting for transfers between devices: 99.8 us -> none  [the longest x1 85.3 us: local(): down_piece = lax.all_gather(down_weight, 'sec', axis=1, tiled=True)]
    unnamed x2 -> x0, blocking collectives: 44.8 us -> none
    all_to_all x3 -> x0, waiting for transfers between devices: 35 us -> none  [the longest x1 23.6 us: local(): lax.all_to_all(pack(patch_tokens), 'sec', split_axis=1, concat_axis=1, ti...]
    ppermute x0 -> x21, waiting for transfers between devices: none -> 35 us  [swap(): return lax.ppermute(values, axis, [(i, i ^ mask) for i in range(size)])]
    pallas_call x0 -> x7, Pallas kernels: none -> 26.1 us  [the longest x2 6.15 us: down(): call(down_kernel, [jax.ShapeDtypeStruct(out, t) for t in types], [full((h...]
    ppermute x0 -> x21, starting transfers between devices: none -> 19.6 us  [swap(): return lax.ppermute(values, axis, [(i, i ^ mask) for i in range(size)])]
    all_to_all x3 -> x0, starting transfers between devices: 14.2 us -> none  [the longest x1 5.76 us: local(): lax.all_to_all(returning.reshape(per_peer, n_sec, columns), 'sec', split_...]
    unnamed x1 -> x0, matrix products: 9.41 us -> none
  transfers between devices with their start and end apart: 6 -> 21, of which waited for: 5 -> 9; matrix products, arithmetic and copies ran while one was open for 6% -> 2% of each run, Pallas kernels for 0% -> 20%
where the time goes in v2:
time: 87 us; the launch traced here: 86.7 us
  waiting for transfers between devices  35 us (40%)
  Pallas kernels  26.1 us (30%)
  starting transfers between devices  19.6 us (23%)
  local copies, waits for them, and re-layouts  4.87 us (6%)
    ppermute x21, waiting for transfers between devices, swap(): return lax.ppermute(values, axis, [(i, i ^ mask) for i in range(size)])  35 us
    ppermute x21, starting transfers between devices, swap(): return lax.ppermute(values, axis, [(i, i ^ mask) for i in range(size)])  19.6 us
    pallas_call x2, Pallas kernels, down(): call(down_kernel, [jax.ShapeDtypeStruct(out, t) for t in types], [full((h...  6.15 us
    pallas_call x1, Pallas kernels, front(): call(front_kernel, (jax.ShapeDtypeStruct((rows, width // 2), jnp.bfloat16...  5.91 us
    pallas_call x1, Pallas kernels, hidden_of(): call(hidden_kernel, jax.ShapeDtypeStruct((images * 2 * rows, 2 * units),...  5.02 us
    pallas_call x1, Pallas kernels, lead(): call(lead_kernel, jax.ShapeDtypeStruct((rows, width), jnp.bfloat16), [ANY...  4.73 us
    pallas_call x1, Pallas kernels, layout(): call(layout_kernel, [jax.ShapeDtypeStruct(s, jnp.bfloat16) for s in shape...  2.91 us
    unnamed x26, local copies, waits for them, and re-layouts  1.89 us
  transfers between devices with their start and end apart: 21, of which 9 were waited for; matrix products, arithmetic and copies ran while one was open for 2% of the time, Pallas kernels for 20%

profile of v2, /device:TPU:0, one launch (start us, length us, event | category | flops | bytes accessed | tf_op | source)
XLA Modules:
  0.0 86.7 jit_solution(5147842602123799400)
XLA Ops:
  0.0 0.6 pad_add_fusion.place
  0.6 4.7 %shard_map.109 = bf16[128,1408]{1,0:T(8,128)(2,1)} custom-call(s32[3]{0:T(128)} %pad_add_fusion.place, bf16[256,1408]{1,0:T(8,128)(2,1)} %bitcast.12, bf16[256,1024]{1,0:T(8,128)(2,1)} %bitcast.16, bf16[1024,1408]{1,0:T(8,128)(2,1)} %weight.3, f32[1408]{0:T(1024)} %gain.3, f32[1408]{0:T(1024)} %shift.3), custom_call_target="tpu_custom_call" | custom-call | flops 1000 | bytes 1000 | tf_op jit(solution)/shard_map/pallas_call | solution.py:162
  5.4 3.0 %collective-permute-start.1 = (bf16[128,1408]{1,0:T(8,128)(2,1)}, bf16[128,1408]{1,0:T(8,128)(2,1)S(1)}, u32[]{:S(2)}, u32[]{:S(2)}) collective-permute-start(bf16[128,1408]{1,0:T(8,128)(2,1)} %shard_map.109), channel_id=1, source_target_pairs={{0,2},{2,0},{4,6},{6,4},{8,10},{10,8},{12,14},{14,12},{1,3},{3,1},... | collective-permute-start | bytes 1081352 | tf_op jit(solution)/shard_map/ppermute | solution.py:16
  8.4 1.6 %collective-permute-start.2 = (bf16[128,1408]{1,0:T(8,128)(2,1)}, bf16[128,1408]{1,0:T(8,128)(2,1)S(1)}, u32[]{:S(2)}, u32[]{:S(2)}) collective-permute-start(bf16[128,1408]{1,0:T(8,128)(2,1)} %shard_map.109), channel_id=1, source_target_pairs={{0,4},{2,6},{4,0},{6,2},{8,12},{10,14},{12,8},{14,10},{1,5},{3,7},... | collective-permute-start | bytes 1081352 | tf_op jit(solution)/shard_map/ppermute | solution.py:16
  9.9 0.2 slice_select_fusion
  10.1 0.0 copy-start.12
  10.1 0.1 collective-permute-start.3
  10.3 2.7 %collective-permute-start = (bf16[112,1408]{1,0:T(8,128)(2,1)S(1)}, bf16[112,1408]{1,0:T(8,128)(2,1)S(1)}, u32[]{:S(2)}, u32[]{:S(2)}) collective-permute-start(bf16[112,1408]{1,0:T(8,128)(2,1)S(1)} %dynamic-slice_bitcast_fusion), channel_id=1, source_target_pairs={{0,8},{2,10},{4,12},{6,14},{8,0},{10,2},{12,4},{14,6},{1,9},{3,11}... | collective-permute-start | bytes 946184 | tf_op jit(solution)/shard_map/ppermute | solution.py:16
  12.9 0.0 collective-permute-done.3.given
  12.9 0.7 copy-done.10
  13.7 2.9 %shard_map.110 = (bf16[448,384]{1,0:T(8,128)(2,1)}, bf16[224,384]{1,0:T(8,128)(2,1)}, bf16[448,320]{1,0:T(8,128)(2,1)}, bf16[224,320]{1,0:T(8,128)(2,1)}) custom-call(s32[3]{0:T(128)} %pad_add_fusion.place, bf16[224,1408]{1,0:T(8,128)(2,1)} %bitcast.14, bf16[224,704]{1,0:T(8,128)(2,1)} %copy-done.10), custom_call_target="tpu_custom_call" | custom-call | flops 1000 | bytes 1000 | tf_op jit(solution)/shard_map/pallas_call | solution.py:206
  16.6 5.9 %shard_map.111 = (bf16[256,704]{1,0:T(8,128)(2,1)}, bf16[256,1408]{1,0:T(8,128)(2,1)}) custom-call(s32[3]{0:T(128)} %pad_add_fusion.place, bf16[256,1408]{1,0:T(8,128)(2,1)} %bitcast.13, bf16[256,1024]{1,0:T(8,128)(2,1)} %bitcast.17, bf16[1024,1408]{1,0:T(8,128)(2,1)} %weight.3, f32[1408]{0:T(1024)} %gain.3, f32[1408]{0:T(1024)} %shift.3), custom_call_target="tpu_custom_call" | custom-call | flops 1000 | bytes 1000 | tf_op jit(solution)/shard_map/pallas_call | solution.py:100
  22.5 5.4 %collective-permute-done.refs_8_ = bf16[112,1408]{1,0:T(8,128)(2,1)S(1)} collective-permute-done((bf16[112,1408]{1,0:T(8,128)(2,1)S(1)}, bf16[112,1408]{1,0:T(8,128)(2,1)S(1)}, u32[]{:S(2)}, u32[]{:S(2)}) %collective-permute-start) | collective-permute-done | bytes 315424 | tf_op jit(solution)/shard_map/ppermute | solution.py:16
  27.9 0.0 collective-permute-done.1.refs_1_
  27.9 0.0 collective-permute-done.2.refs_3_
  27.9 0.5 collective-permute-start.7
  28.4 0.0 copy-done.11
  28.4 0.0 collective-permute-start.5
  28.4 2.9 %collective-permute-start.10 = (bf16[1,224]{1,0:T(2,128)(2,1)S(1)}, bf16[1,224]{1,0:T(2,128)(2,1)S(1)}, u32[]{:S(2)}, u32[]{:S(2)}) collective-permute-start(bf16[1,224]{1,0:T(2,128)(2,1)S(1)} %reshape.3.refs_10_), channel_id=1, source_target_pairs={{0,8},{2,10},{4,12},{6,14},{8,0},{10,2},{12,4},{14,6},{1,9},{3,11}... | collective-permute-start | bytes 1352 | tf_op jit(solution)/shard_map/ppermute | solution.py:16
  31.3 0.0 collective-permute-start.4
  31.3 1.5 %collective-permute-start.9 = (bf16[112,1408]{1,0:T(8,128)(2,1)S(1)}, bf16[112,1408]{1,0:T(8,128)(2,1)S(1)}, u32[]{:S(2)}, u32[]{:S(2)}) collective-permute-start(bf16[112,1408]{1,0:T(8,128)(2,1)S(1)} %collective-permute-done.refs_8_), channel_id=1, source_target_pairs={{0,16},{16,0},{1,17},{17,1},{2,18},{18,2},{3,19},{19,3},{4,20},{20... | collective-permute-start | bytes 946184 | tf_op jit(solution)/shard_map/ppermute | solution.py:16
  32.9 5.7 %collective-permute-done.5.near = bf16[224,384]{1,0:T(8,128)(2,1)S(1)} collective-permute-done((bf16[224,384]{1,0:T(8,128)(2,1)S(1)}, bf16[224,384]{1,0:T(8,128)(2,1)S(1)}, u32[]{:S(2)}, u32[]{:S(2)}) %collective-permute-start.5) | collective-permute-done | bytes 172064 | tf_op jit(solution)/shard_map/ppermute | solution.py:16
  38.5 0.0 collective-permute-start.6
  38.5 0.0 collective-permute-done.7.refs_5_
  38.5 0.5 collective-permute-start.8
  39.0 0.0 collective-permute-done.10
  39.0 0.1 fusion
  39.1 0.0 collective-permute-start.11
  39.1 0.1 broadcast_select_fusion.refs_11_
  39.2 2.0 %collective-permute-done.9.refs_9_ = bf16[112,1408]{1,0:T(8,128)(2,1)S(1)} collective-permute-done((bf16[112,1408]{1,0:T(8,128)(2,1)S(1)}, bf16[112,1408]{1,0:T(8,128)(2,1)S(1)}, u32[]{:S(2)}, u32[]{:S(2)}) %collective-permute-start.9) | collective-permute-done | bytes 315424 | tf_op jit(solution)/shard_map/ppermute | solution.py:16
  41.2 0.0 collective-permute-done.4.refs_2_
  41.2 0.0 collective-permute-done.6.refs_4_
  41.2 0.0 collective-permute-done.8.refs_6_
  41.2 0.0 copy-done.5
  41.2 1.1 %copy-done.1 = bf16[256,1408]{1,0:T(8,128)(2,1)S(1)} copy-done((bf16[256,1408]{1,0:T(8,128)(2,1)S(1)}, bf16[256,1408]{1,0:T(8,128)(2,1)}, u32[]{:S(2)}) %copy-start.1) | copy-done | bytes 720920
  42.3 5.0 %shard_map.112.ours = bf16[1024,448]{1,0:T(8,128)(2,1)S(1)} custom-call(s32[3]{0:T(128)S(1)} %copy-done.5, bf16[256,1408]{1,0:T(8,128)(2,1)S(1)} %copy-done.1, bf16[128,1408]{1,0:T(8,128)(2,1)S(1)} %collective-permute-done.1.refs_1_, bf16[128,1408]{1,0:T(8,128)(2,1)S(1)} %collective-permute-done.4.refs_2_, ...), custom_call_target="tpu_custom_call" | custom-call | flops 1000 | bytes 1000 | tf_op jit(solution)/shard_map/pallas_call | solution.py:271
  47.4 2.0 %collective-permute-done.11.near = bf16[224,320]{1,0:T(8,128)(2,1)S(1)} collective-permute-done((bf16[224,320]{1,0:T(8,128)(2,1)}, bf16[224,320]{1,0:T(8,128)(2,1)S(1)}, u32[]{:S(2)}, u32[]{:S(2)}) %collective-permute-start.11) | collective-permute-done | bytes 143392 | tf_op jit(solution)/shard_map/ppermute | solution.py:16
  49.4 0.5 copy.13
  49.9 0.1 collective-permute-start.12
  50.0 1.6 %collective-permute-start.13 = (bf16[224,384]{1,0:T(8,128)(2,1)S(1)}, bf16[224,384]{1,0:T(8,128)(2,1)}, u32[]{:S(2)}, u32[]{:S(2)}) collective-permute-start(bf16[224,384]{1,0:T(8,128)(2,1)S(1)} %collective-permute-done.5.near), channel_id=1, source_target_pairs={{0,16},{16,0},{1,17},{17,1},{2,18},{18,2},{3,19},{19,3},{4,20},{20... | collective-permute-start | bytes 516104 | tf_op jit(solution)/shard_map/ppermute | solution.py:16
  51.5 0.5 collective-permute-start.17
  52.0 0.5 collective-permute-done.12
  52.5 1.5 %copy.14.theirs = bf16[1024,448]{1,0:T(8,128)(2,1)S(1)} copy(bf16[1024,448]{0,1:T(8,128)(2,1)} %collective-permute-done.12) | data formatting | bytes 1835008 | tf_op jit(solution)/shard_map/ppermute | solution.py:16
  54.0 0.0 copy-start.6
  54.0 0.0 copy-start.7
  54.0 0.0 copy-start.8
  54.1 3.2 %collective-permute-done.13.crossed = bf16[224,384]{1,0:T(8,128)(2,1)} collective-permute-done((bf16[224,384]{1,0:T(8,128)(2,1)S(1)}, bf16[224,384]{1,0:T(8,128)(2,1)}, u32[]{:S(2)}, u32[]{:S(2)}) %collective-permute-start.13) | collective-permute-done | bytes 172064 | tf_op jit(solution)/shard_map/ppermute | solution.py:16
  57.3 3.4 %shard_map.113 = (f32[256,384]{1,0:T(8,128)S(1)}, bf16[256,384]{1,0:T(8,128)(2,1)S(1)}, bf16[256,384]{1,0:T(8,128)(2,1)S(1)}, bf16[256,384]{1,0:T(8,128)(2,1)S(1)}) custom-call(s32[3]{0:T(128)S(1)} %copy-done.5, bf16[1024,448]{1,0:T(8,128)(2,1)S(1)} %shard_map.112.ours, bf16[1024,448]{1,0:T(8,128)(2,1)S(1)} %copy.14.theirs, bf16[448,384]{1,0:T(8,128)(2,1)S(1)} %copy-done.4, ...), custom_call_target="tpu_custom_call" | custom-call | flops 1000 | bytes 1000 | tf_op jit(solution)/shard_map/pallas_call | solution.py:317
  60.7 0.0 collective-permute-done.17.crossed
  60.7 2.7 %shard_map.114 = (f32[256,320]{1,0:T(8,128)S(1)}, bf16[256,320]{1,0:T(8,128)(2,1)S(1)}, bf16[256,320]{1,0:T(8,128)(2,1)S(1)}, bf16[256,320]{1,0:T(8,128)(2,1)S(1)}) custom-call(s32[3]{0:T(128)S(1)} %copy-done.5, bf16[1024,448]{1,0:T(8,128)(2,1)S(1)} %shard_map.112.ours, bf16[1024,448]{1,0:T(8,128)(2,1)S(1)} %copy.14.theirs, bf16[448,320]{1,0:T(8,128)(2,1)S(1)} %copy-done.3, ...), custom_call_target="tpu_custom_call" | custom-call | flops 1000 | bytes 1000 | tf_op jit(solution)/shard_map/pallas_call | solution.py:317
  63.5 1.1 %collective-permute-start.18 = (bf16[256,320]{1,0:T(8,128)(2,1)S(1)}, bf16[256,320]{1,0:T(8,128)(2,1)S(1)}, u32[]{:S(2)}, u32[]{:S(2)}) collective-permute-start(bf16[256,320]{1,0:T(8,128)(2,1)S(1)} %get-tuple-element.50), channel_id=1, source_target_pairs={{0,2},{2,0},{4,6},{6,4},{8,10},{10,8},{12,14},{14,12},{1,3},{3,1},... | collective-permute-start | bytes 491528 | tf_op jit(solution)/shard_map/ppermute | solution.py:16
  64.6 1.0 %collective-permute-start.14 = (bf16[256,384]{1,0:T(8,128)(2,1)S(1)}, bf16[256,384]{1,0:T(8,128)(2,1)S(1)}, u32[]{:S(2)}, u32[]{:S(2)}) collective-permute-start(bf16[256,384]{1,0:T(8,128)(2,1)S(1)} %get-tuple-element.44), channel_id=1, source_target_pairs={{0,2},{2,0},{4,6},{6,4},{8,10},{10,8},{12,14},{14,12},{1,3},{3,1},... | collective-permute-start | bytes 589832 | tf_op jit(solution)/shard_map/ppermute | solution.py:16
  65.6 0.0 collective-permute-start.15
  65.6 2.5 %collective-permute-start.16 = (bf16[256,384]{1,0:T(8,128)(2,1)S(1)}, bf16[256,384]{1,0:T(8,128)(2,1)S(1)}, u32[]{:S(2)}, u32[]{:S(2)}) collective-permute-start(bf16[256,384]{1,0:T(8,128)(2,1)S(1)} %get-tuple-element.46), channel_id=1, source_target_pairs={{0,6},{2,4},{4,2},{6,0},{8,14},{10,12},{12,10},{14,8},{1,7},{3,5},... | collective-permute-start | bytes 589832 | tf_op jit(solution)/shard_map/ppermute | solution.py:16
  68.1 0.0 collective-permute-start.19
  68.1 5.3 %collective-permute-done.18.refs_5_ = bf16[256,320]{1,0:T(8,128)(2,1)S(1)} collective-permute-done((bf16[256,320]{1,0:T(8,128)(2,1)S(1)}, bf16[256,320]{1,0:T(8,128)(2,1)S(1)}, u32[]{:S(2)}, u32[]{:S(2)}) %collective-permute-start.18) | collective-permute-done | bytes 163872 | tf_op jit(solution)/shard_map/ppermute | solution.py:16
  73.4 0.0 collective-permute-start.20
  73.4 8.4 %collective-permute-done.19.refs_6_ = bf16[256,320]{1,0:T(8,128)(2,1)S(1)} collective-permute-done((bf16[256,320]{1,0:T(8,128)(2,1)S(1)}, bf16[256,320]{1,0:T(8,128)(2,1)S(1)}, u32[]{:S(2)}, u32[]{:S(2)}) %collective-permute-start.19) | collective-permute-done | bytes 163872 | tf_op jit(solution)/shard_map/ppermute | solution.py:16
  81.7 2.6 %collective-permute-done.20.refs_7_ = bf16[256,320]{1,0:T(8,128)(2,1)S(1)} collective-permute-done((bf16[256,320]{1,0:T(8,128)(2,1)S(1)}, bf16[256,320]{1,0:T(8,128)(2,1)S(1)}, u32[]{:S(2)}, u32[]{:S(2)}) %collective-permute-start.20) | collective-permute-done | bytes 163872 | tf_op jit(solution)/shard_map/ppermute | solution.py:16
  84.3 0.0 collective-permute-done.14.refs_1_
  84.3 0.0 collective-permute-done.15.refs_2_
  84.3 0.0 collective-permute-done.16.refs_3_
  84.4 1.4 %shard_map.115 = bf16[256,704]{1,0:T(8,128)(2,1)S(1)} custom-call(s32[3]{0:T(128)S(1)} %copy-done.5, s32[2]{0:T(128)S(1)} %copy-done.7, s32[2]{0:T(128)S(1)} %copy-done.8, bf16[256,704]{1,0:T(8,128)(2,1)S(1)} %copy-done.2, f32[704]{0:T(1024)S(1)} %copy-done.6, f32[256,384]{1,0:T(8,128)S(1)} %get-tuple-element.43.refs_0_, ...), custom_call_target="tpu_custom_call" | custom-call | flops 1000 | bytes 1000 | tf_op jit(solution)/shard_map/pallas_call | solution.py:354
  85.7 0.9 %copy.16 = bf16[1,256,704]{1,2,0:T(8,128)(2,1)} copy(bf16[1,256,704]{2,1,0:T(8,128)(2,1)S(1)} %bitcast.10) | data formatting | bytes 720896 | tf_op jit(solution)/shard_map/broadcast_in_dim | solution.py:418
  (20 shorter events, 0.1 us)
Async XLA Ops:
  0.0 9.9 %copy-start.9 = (bf16[1408,224]{0,1:T(8,128)(2,1)S(1)}, bf16[1408,224]{0,1:T(8,128)(2,1)}, u32[]{:S(2)}) copy-start(bf16[1408,224]{0,1:T(8,128)(2,1)} %param.20) | copy-start | bytes 1892356
  0.0 10.2 %copy-start = (bf16[1408,224]{0,1:T(8,128)(2,1)S(1)}, bf16[1408,224]{0,1:T(8,128)(2,1)}, u32[]{:S(2)}) copy-start(bf16[1408,224]{0,1:T(8,128)(2,1)} %param.18) | copy-start | bytes 1892356
  5.4 22.5 %collective-permute-start.1 = (bf16[128,1408]{1,0:T(8,128)(2,1)}, bf16[128,1408]{1,0:T(8,128)(2,1)S(1)}, u32[]{:S(2)}, u32[]{:S(2)}) collective-permute-start(bf16[128,1408]{1,0:T(8,128)(2,1)} %shard_map.109), channel_id=1, source_target_pairs={{0,2},{2,0},{4,6},{6,4},{8,10},{10,8},{12,14},{14,12},{1,3},{3,1},... | collective-permute-start | bytes 1081352 | tf_op jit(solution)/shard_map/ppermute | solution.py:16
  8.4 19.5 %collective-permute-start.2 = (bf16[128,1408]{1,0:T(8,128)(2,1)}, bf16[128,1408]{1,0:T(8,128)(2,1)S(1)}, u32[]{:S(2)}, u32[]{:S(2)}) collective-permute-start(bf16[128,1408]{1,0:T(8,128)(2,1)} %shard_map.109), channel_id=1, source_target_pairs={{0,4},{2,6},{4,0},{6,2},{8,12},{10,14},{12,8},{14,10},{1,5},{3,7},... | collective-permute-start | bytes 1081352 | tf_op jit(solution)/shard_map/ppermute | solution.py:16
  10.1 18.3 %copy-start.12 = (bf16[224]{0:T(256)(128)(2,1)S(1)}, bf16[224]{0:T(256)(128)(2,1)}, u32[]{:S(2)}) copy-start(bf16[224]{0:T(256)(128)(2,1)} %param.19) | copy-start | bytes 1348
  10.1 2.8 %collective-permute-start.3 = (bf16[224,704]{1,0:T(8,128)(2,1)S(1)}, bf16[224,704]{1,0:T(8,128)(2,1)S(1)}, u32[]{:S(2)}, u32[]{:S(2)}) collective-permute-start(bf16[224,704]{1,0:T(8,128)(2,1)S(1)} %slice_select_fusion), channel_id=1, source_target_pairs={{0,1},{1,0},{2,3},{3,2},{4,5},{5,4},{6,7},{7,6},{8,9},{9,8},{10,11... | collective-permute-start | bytes 946184 | tf_op jit(solution)/shard_map/ppermute | solution.py:16
  10.2 31.0 %copy-start.5 = (s32[3]{0:T(128)S(1)}, s32[3]{0:T(128)}, u32[]{:S(2)}) copy-start(s32[3]{0:T(128)} %pad_add_fusion.place) | copy-start | bytes 40
  10.3 17.6 %collective-permute-start = (bf16[112,1408]{1,0:T(8,128)(2,1)S(1)}, bf16[112,1408]{1,0:T(8,128)(2,1)S(1)}, u32[]{:S(2)}, u32[]{:S(2)}) collective-permute-start(bf16[112,1408]{1,0:T(8,128)(2,1)S(1)} %dynamic-slice_bitcast_fusion), channel_id=1, source_target_pairs={{0,8},{2,10},{4,12},{6,14},{8,0},{10,2},{12,4},{14,6},{1,9},{3,11}... | collective-permute-start | bytes 946184 | tf_op jit(solution)/shard_map/ppermute | solution.py:16
  12.9 0.7 copy-start.10
  16.6 11.8 %copy-start.11 = (bf16[224,384]{1,0:T(8,128)(2,1)S(1)}, bf16[224,384]{1,0:T(8,128)(2,1)}, u32[]{:S(2)}) copy-start(bf16[224,384]{1,0:T(8,128)(2,1)} %get-tuple-element.30) | copy-start | bytes 516100
  27.9 10.7 %collective-permute-start.7 = (bf16[128,1408]{1,0:T(8,128)(2,1)S(1)}, bf16[128,1408]{1,0:T(8,128)(2,1)S(1)}, u32[]{:S(2)}, u32[]{:S(2)}) collective-permute-start(bf16[128,1408]{1,0:T(8,128)(2,1)S(1)} %collective-permute-done.2.refs_3_), channel_id=1, source_target_pairs={{0,2},{2,0},{4,6},{6,4},{8,10},{10,8},{12,14},{14,12},{1,3},{3,1},... | collective-permute-start | bytes 1081352 | tf_op jit(solution)/shard_map/ppermute | solution.py:16
  28.4 10.1 %collective-permute-start.5 = (bf16[224,384]{1,0:T(8,128)(2,1)S(1)}, bf16[224,384]{1,0:T(8,128)(2,1)S(1)}, u32[]{:S(2)}, u32[]{:S(2)}) collective-permute-start(bf16[224,384]{1,0:T(8,128)(2,1)S(1)} %copy-done.11), channel_id=1, source_target_pairs={{0,8},{2,10},{4,12},{6,14},{8,0},{10,2},{12,4},{14,6},{1,9},{3,11}... | collective-permute-start | bytes 516104 | tf_op jit(solution)/shard_map/ppermute | solution.py:16
  28.4 10.6 %collective-permute-start.10 = (bf16[1,224]{1,0:T(2,128)(2,1)S(1)}, bf16[1,224]{1,0:T(2,128)(2,1)S(1)}, u32[]{:S(2)}, u32[]{:S(2)}) collective-permute-start(bf16[1,224]{1,0:T(2,128)(2,1)S(1)} %reshape.3.refs_10_), channel_id=1, source_target_pairs={{0,8},{2,10},{4,12},{6,14},{8,0},{10,2},{12,4},{14,6},{1,9},{3,11}... | collective-permute-start | bytes 1352 | tf_op jit(solution)/shard_map/ppermute | solution.py:16
  31.3 9.9 %collective-permute-start.4 = (bf16[128,1408]{1,0:T(8,128)(2,1)S(1)}, bf16[128,1408]{1,0:T(8,128)(2,1)S(1)}, u32[]{:S(2)}, u32[]{:S(2)}) collective-permute-start(bf16[128,1408]{1,0:T(8,128)(2,1)S(1)} %collective-permute-done.1.refs_1_), channel_id=1, source_target_pairs={{0,1},{1,0},{2,3},{3,2},{4,5},{5,4},{6,7},{7,6},{8,9},{9,8},{10,11... | collective-permute-start | bytes 1081352 | tf_op jit(solution)/shard_map/ppermute | solution.py:16
  31.3 9.9 %collective-permute-start.9 = (bf16[112,1408]{1,0:T(8,128)(2,1)S(1)}, bf16[112,1408]{1,0:T(8,128)(2,1)S(1)}, u32[]{:S(2)}, u32[]{:S(2)}) collective-permute-start(bf16[112,1408]{1,0:T(8,128)(2,1)S(1)} %collective-permute-done.refs_8_), channel_id=1, source_target_pairs={{0,16},{16,0},{1,17},{17,1},{2,18},{18,2},{3,19},{19,3},{4,20},{20... | collective-permute-start | bytes 946184 | tf_op jit(solution)/shard_map/ppermute | solution.py:16
  38.5 2.7 %collective-permute-start.6 = (bf16[128,1408]{1,0:T(8,128)(2,1)S(1)}, bf16[128,1408]{1,0:T(8,128)(2,1)S(1)}, u32[]{:S(2)}, u32[]{:S(2)}) collective-permute-start(bf16[128,1408]{1,0:T(8,128)(2,1)S(1)} %collective-permute-done.2.refs_3_), channel_id=1, source_target_pairs={{0,1},{1,0},{2,3},{3,2},{4,5},{5,4},{6,7},{7,6},{8,9},{9,8},{10,11... | collective-permute-start | bytes 1081352 | tf_op jit(solution)/shard_map/ppermute | solution.py:16
  38.5 2.7 %collective-permute-start.8 = (bf16[128,1408]{1,0:T(8,128)(2,1)S(1)}, bf16[128,1408]{1,0:T(8,128)(2,1)S(1)}, u32[]{:S(2)}, u32[]{:S(2)}) collective-permute-start(bf16[128,1408]{1,0:T(8,128)(2,1)S(1)} %collective-permute-done.7.refs_5_), channel_id=1, source_target_pairs={{0,1},{1,0},{2,3},{3,2},{4,5},{5,4},{6,7},{7,6},{8,9},{9,8},{10,11... | collective-permute-start | bytes 1081352 | tf_op jit(solution)/shard_map/ppermute | solution.py:16
  39.1 10.2 %collective-permute-start.11 = (bf16[224,320]{1,0:T(8,128)(2,1)}, bf16[224,320]{1,0:T(8,128)(2,1)S(1)}, u32[]{:S(2)}, u32[]{:S(2)}) collective-permute-start(bf16[224,320]{1,0:T(8,128)(2,1)} %get-tuple-element.40), channel_id=1, source_target_pairs={{0,8},{2,10},{4,12},{6,14},{8,0},{10,2},{12,4},{14,6},{1,9},{3,11}... | collective-permute-start | bytes 430088 | tf_op jit(solution)/shard_map/ppermute | solution.py:16
  41.2 1.1 %copy-start.1 = (bf16[256,1408]{1,0:T(8,128)(2,1)S(1)}, bf16[256,1408]{1,0:T(8,128)(2,1)}, u32[]{:S(2)}) copy-start(bf16[256,1408]{1,0:T(8,128)(2,1)} %get-tuple-element.34.refs_0_) | copy-start | bytes 2162692
  47.4 9.9 %copy-start.4 = (bf16[448,384]{1,0:T(8,128)(2,1)S(1)}, bf16[448,384]{1,0:T(8,128)(2,1)}, u32[]{:S(2)}) copy-start(bf16[448,384]{1,0:T(8,128)(2,1)} %get-tuple-element.42.weights) | copy-start | bytes 1032196
  47.4 13.4 %copy-start.3 = (bf16[448,320]{1,0:T(8,128)(2,1)S(1)}, bf16[448,320]{1,0:T(8,128)(2,1)}, u32[]{:S(2)}) copy-start(bf16[448,320]{1,0:T(8,128)(2,1)} %get-tuple-element.48.weights) | copy-start | bytes 860164
  49.9 2.7 %collective-permute-start.12 = (bf16[1024,448]{0,1:T(8,128)(2,1)S(1)}, bf16[1024,448]{0,1:T(8,128)(2,1)}, u32[]{:S(2)}, u32[]{:S(2)}) collective-permute-start(bf16[1024,448]{0,1:T(8,128)(2,1)S(1)} %copy.13), channel_id=1, source_target_pairs={{0,1},{1,0},{2,3},{3,2},{4,5},{5,4},{6,7},{7,6},{8,9},{9,8},{10,11... | collective-permute-start | bytes 2752520 | tf_op jit(solution)/shard_map/ppermute | solution.py:16
  50.0 7.3 %collective-permute-start.13 = (bf16[224,384]{1,0:T(8,128)(2,1)S(1)}, bf16[224,384]{1,0:T(8,128)(2,1)}, u32[]{:S(2)}, u32[]{:S(2)}) collective-permute-start(bf16[224,384]{1,0:T(8,128)(2,1)S(1)} %collective-permute-done.5.near), channel_id=1, source_target_pairs={{0,16},{16,0},{1,17},{17,1},{2,18},{18,2},{3,19},{19,3},{4,20},{20... | collective-permute-start | bytes 516104 | tf_op jit(solution)/shard_map/ppermute | solution.py:16
  51.5 9.2 %collective-permute-start.17 = (bf16[224,320]{1,0:T(8,128)(2,1)S(1)}, bf16[224,320]{1,0:T(8,128)(2,1)S(1)}, u32[]{:S(2)}, u32[]{:S(2)}) collective-permute-start(bf16[224,320]{1,0:T(8,128)(2,1)S(1)} %collective-permute-done.11.near), channel_id=1, source_target_pairs={{0,16},{16,0},{1,17},{17,1},{2,18},{18,2},{3,19},{19,3},{4,20},{20... | collective-permute-start | bytes 430088 | tf_op jit(solution)/shard_map/ppermute | solution.py:16
  54.0 30.3 %copy-start.2 = (bf16[256,704]{1,0:T(8,128)(2,1)S(1)}, bf16[256,704]{1,0:T(8,128)(2,1)}, u32[]{:S(2)}) copy-start(bf16[256,704]{1,0:T(8,128)(2,1)} %get-tuple-element.33.residual) | copy-start | bytes 1081348
  54.0 30.3 %copy-start.6 = (f32[704]{0:T(1024)S(1)}, f32[704]{0:T(1024)}, u32[]{:S(2)}) copy-start(f32[704]{0:T(1024)} %bias.1) | copy-start | bytes 8452
  54.0 30.3 %copy-start.7 = (s32[2]{0:T(128)S(1)}, s32[2]{0:T(128)}, u32[]{:S(2)}) copy-start(s32[2]{0:T(128)} %first.1) | copy-start | bytes 28
  54.0 30.3 %copy-start.8 = (s32[2]{0:T(128)S(1)}, s32[2]{0:T(128)}, u32[]{:S(2)}) copy-start(s32[2]{0:T(128)} %second.1) | copy-start | bytes 28
  63.5 9.9 %collective-permute-start.18 = (bf16[256,320]{1,0:T(8,128)(2,1)S(1)}, bf16[256,320]{1,0:T(8,128)(2,1)S(1)}, u32[]{:S(2)}, u32[]{:S(2)}) collective-permute-start(bf16[256,320]{1,0:T(8,128)(2,1)S(1)} %get-tuple-element.50), channel_id=1, source_target_pairs={{0,2},{2,0},{4,6},{6,4},{8,10},{10,8},{12,14},{14,12},{1,3},{3,1},... | collective-permute-start | bytes 491528 | tf_op jit(solution)/shard_map/ppermute | solution.py:16
  64.6 19.7 %collective-permute-start.14 = (bf16[256,384]{1,0:T(8,128)(2,1)S(1)}, bf16[256,384]{1,0:T(8,128)(2,1)S(1)}, u32[]{:S(2)}, u32[]{:S(2)}) collective-permute-start(bf16[256,384]{1,0:T(8,128)(2,1)S(1)} %get-tuple-element.44), channel_id=1, source_target_pairs={{0,2},{2,0},{4,6},{6,4},{8,10},{10,8},{12,14},{14,12},{1,3},{3,1},... | collective-permute-start | bytes 589832 | tf_op jit(solution)/shard_map/ppermute | solution.py:16
  65.6 18.7 %collective-permute-start.15 = (bf16[256,384]{1,0:T(8,128)(2,1)S(1)}, bf16[256,384]{1,0:T(8,128)(2,1)S(1)}, u32[]{:S(2)}, u32[]{:S(2)}) collective-permute-start(bf16[256,384]{1,0:T(8,128)(2,1)S(1)} %get-tuple-element.45), channel_id=1, source_target_pairs={{0,4},{2,6},{4,0},{6,2},{8,12},{10,14},{12,8},{14,10},{1,5},{3,7},... | collective-permute-start | bytes 589832 | tf_op jit(solution)/shard_map/ppermute | solution.py:16
  65.6 18.7 %collective-permute-start.16 = (bf16[256,384]{1,0:T(8,128)(2,1)S(1)}, bf16[256,384]{1,0:T(8,128)(2,1)S(1)}, u32[]{:S(2)}, u32[]{:S(2)}) collective-permute-start(bf16[256,384]{1,0:T(8,128)(2,1)S(1)} %get-tuple-element.46), channel_id=1, source_target_pairs={{0,6},{2,4},{4,2},{6,0},{8,14},{10,12},{12,10},{14,8},{1,7},{3,5},... | collective-permute-start | bytes 589832 | tf_op jit(solution)/shard_map/ppermute | solution.py:16
  68.1 13.6 %collective-permute-start.19 = (bf16[256,320]{1,0:T(8,128)(2,1)S(1)}, bf16[256,320]{1,0:T(8,128)(2,1)S(1)}, u32[]{:S(2)}, u32[]{:S(2)}) collective-permute-start(bf16[256,320]{1,0:T(8,128)(2,1)S(1)} %get-tuple-element.51), channel_id=1, source_target_pairs={{0,4},{2,6},{4,0},{6,2},{8,12},{10,14},{12,8},{14,10},{1,5},{3,7},... | collective-permute-start | bytes 491528 | tf_op jit(solution)/shard_map/ppermute | solution.py:16
  73.4 10.9 %collective-permute-start.20 = (bf16[256,320]{1,0:T(8,128)(2,1)S(1)}, bf16[256,320]{1,0:T(8,128)(2,1)S(1)}, u32[]{:S(2)}, u32[]{:S(2)}) collective-permute-start(bf16[256,320]{1,0:T(8,128)(2,1)S(1)} %get-tuple-element.52), channel_id=1, source_target_pairs={{0,6},{2,4},{4,2},{6,0},{8,14},{10,12},{12,10},{14,8},{1,7},{3,5},... | collective-permute-start | bytes 491528 | tf_op jit(solution)/shard_map/ppermute | solution.py:16

commit v3 on v2

--- a/solution.py
+++ b/solution.py
@@ -7,7 +7,7 @@
 
 
 NT = (((1,), (1,)), ((), ()))
-CHUNKS = (384, 320)
+CHUNK = 384
 ANY = pl.BlockSpec(memory_space=pl.ANY)
 
 
@@ -44,79 +44,60 @@
     return pl.ds(pl.multiple_of(start, 16), size)
 
 
-def front_kernel(
-    place, tokens, skips, weight, gain, shift, residual_out, normed_out, *scratch
-):
-    held_tokens, held_skips, held_weight, joined, sems = scratch
-    rows, width = normed_out.shape
-    columns = width // 2
-    depth = weight.shape[0]
-    steps = sems.shape[0] - 2
-    size = depth // steps
-    first = [
-        pltpu.make_async_copy(skips, held_skips, sems.at[steps]),
-        pltpu.make_async_copy(tokens, held_tokens, sems.at[steps + 1]),
-    ]
-    loads = [
-        pltpu.make_async_copy(
-            weight.at[pl.ds(i * size, size), :], held_weight.at[pl.ds(i * size, size), :], sems.at[i]
-        )
-        for i in range(steps)
-    ]
-    for copy in [first[0], *loads, first[1]]:
+def window_of(core, width, window):
+    return pl.ds(pl.multiple_of(core * (width - window), 128), window)
+
+
+def give_kernel(place, own, out, sem):
+    width, window = own.shape[1], out.shape[1]
+    copy = pltpu.make_async_copy(own.at[:, window_of(1 - place[0], width, window)], out, sem)
+    copy.start()
+    copy.wait()
+
+
+def give(place, own, window):
+    units = own.shape[0]
+    return call(
+        give_kernel,
+        jax.ShapeDtypeStruct((units, window), jnp.bfloat16),
+        [ANY],
+        full((units, window)),
+        [pltpu.SemaphoreType.DMA],
+        room=60,
+    )(place, own)
+
+
+def message_kernel(place, own, given, first, second, sems):
+    units, window = given.shape
+    half = units // 2
+    rows = aligned(place[1] * half, half)
+    start = place[0] * (own.shape[1] - window)
+    copies = []
+    for j, out in enumerate((first, second)):
+        size = out.shape[1]
+        lanes = pl.ds(pl.multiple_of(start + j * size, 128), size)
+        copies.append((own.at[rows, lanes], out.at[pl.ds(0, half), :]))
+        copies.append((given.at[rows, pl.ds(j * size, size)], out.at[pl.ds(half, half), :]))
+    copies = [pltpu.make_async_copy(a, b, sems.at[k]) for k, (a, b) in enumerate(copies)]
+    for copy in copies:
         copy.start()
-    first[0].wait()
-    for i, copy in enumerate(loads):
+    for copy in copies:
         copy.wait()
-        block = slice(i * size, (i + 1) * size)
-        product = jnp.dot(
-            held_skips[:, block], held_weight[block, :], preferred_element_type=jnp.float32
-        )
-        if i == 0:
-            joined[...] = product
-        else:
-            joined[...] += product
-    first[1].wait()
-    kept = (held_tokens[...].astype(jnp.float32) + joined[...]).astype(jnp.bfloat16)
-
-    @pl.when(place[0] == 0)
-    def _():
-        residual_out[...] = kept[:, :columns]
-
-    @pl.when(place[0] != 0)
-    def _():
-        residual_out[...] = kept[:, columns:]
-
-    kept = kept.astype(jnp.float32)
-    centered = kept - jnp.mean(kept, axis=1, keepdims=True)
-    spread = jnp.mean(centered * centered, axis=1, keepdims=True)
-    scaled = centered * lax.rsqrt(spread + 1e-06) * gain[...] + shift[...]
-    normed_out[...] = scaled.astype(jnp.bfloat16)
-
-
-def front(place, tokens, skips, weight, gain, shift):
-    rows, width = tokens.shape
-    depth = weight.shape[0]
-    return call(
-        front_kernel,
-        (
-            jax.ShapeDtypeStruct((rows, width // 2), jnp.bfloat16),
-            jax.ShapeDtypeStruct((rows, width), jnp.bfloat16),
-        ),
-        [ANY, ANY, ANY, full((width,)), full((width,))],
-        (full((rows, width // 2)), full((rows, width))),
-        [
-            pltpu.VMEM((rows, width), jnp.bfloat16),
-            pltpu.VMEM((rows, depth), jnp.bfloat16),
-            pltpu.VMEM((depth, width), jnp.bfloat16),
-            pltpu.VMEM((rows, width), jnp.float32),
-            pltpu.SemaphoreType.DMA((4,)),
-        ],
+
+
+def messages(place, own, given):
+    units = own.shape[0]
+    return call(
+        message_kernel,
+        [jax.ShapeDtypeStruct((units, CHUNK), jnp.bfloat16)] * 2,
+        [ANY, ANY],
+        [full((units, CHUNK))] * 2,
+        [pltpu.SemaphoreType.DMA((4,))],
         room=60,
-    )(place, tokens, skips, weight, gain, shift)
-
-
-def lead_kernel(place, tokens, skips, weight, gain, shift, mine_out, *scratch):
+    )(place, own, given)
+
+
+def lead_kernel(place, tokens, skips, weight, gain, shift, mine_out, keep_out, give_out, *scratch):
     held_tokens, held_skips, held_weight, joined, sems = scratch
     rows, width = mine_out.shape
     depth = weight.shape[0]
@@ -148,6 +129,18 @@
             joined[...] += product
     first[1].wait()
     kept = (held_tokens[...].astype(jnp.float32) + joined[...]).astype(jnp.bfloat16)
+    window = keep_out.shape[1]
+
+    @pl.when(place[0] == 0)
+    def _():
+        keep_out[...] = kept[:, :window]
+        give_out[...] = kept[:, width - window :]
+
+    @pl.when(place[0] != 0)
+    def _():
+        keep_out[...] = kept[:, width - window :]
+        give_out[...] = kept[:, :window]
+
     kept = kept.astype(jnp.float32)
     centered = kept - jnp.mean(kept, axis=1, keepdims=True)
     spread = jnp.mean(centered * centered, axis=1, keepdims=True)
@@ -155,15 +148,15 @@
     mine_out[...] = scaled.astype(jnp.bfloat16)
 
 
-def lead(place, tokens, skips, weight, gain, shift):
+def lead(place, window, tokens, skips, weight, gain, shift):
     rows, width = tokens.shape
     rows //= 2
     depth = weight.shape[0]
     return call(
         lead_kernel,
-        jax.ShapeDtypeStruct((rows, width), jnp.bfloat16),
+        [jax.ShapeDtypeStruct((rows, size), jnp.bfloat16) for size in (width, window, window)],
         [ANY, ANY, ANY, full((width,)), full((width,))],
-        full((rows, width)),
+        [full((rows, size)) for size in (width, window, window)],
         [
             pltpu.VMEM((rows, width), jnp.bfloat16),
             pltpu.VMEM((rows, depth), jnp.bfloat16),
@@ -220,8 +213,7 @@
     rows = out.shape[0] // images
     half = rows // 2
     core = place[0]
-    copies = [[(sources[0], pl.ds(0, rows))]]
-    sources = sources[1:]
+    copies = []
     for k in range(0, len(sources), 2):
         start = len(copies) * rows
         copies.append(
@@ -261,35 +253,42 @@
             )
             scaled = 0.5 * pre_act * (1.0 + lax.erf(pre_act * (0.5**0.5)))
             out[block, lanes] = scaled.astype(jnp.bfloat16)
-
-
-def hidden_of(place, normed, halves, weights, biases):
-    rows, width = halves[0].shape
-    images = len(halves) // 2 + 1
+    used = len(biases) * units
+    out[:, used:] = jnp.zeros((out.shape[0], out.shape[1] - used), out.dtype)
+
+
+def hidden_of(place, sources, weights, biases):
+    rows, width = sources[0].shape
+    images = len(sources) // 2
     units = biases[0].shape[1]
-    sources = [normed, *halves]
+    out = (images * 2 * rows, -(-2 * units // 128) * 128)
     return call(
         hidden_kernel,
-        jax.ShapeDtypeStruct((images * 2 * rows, 2 * units), jnp.bfloat16),
+        jax.ShapeDtypeStruct(out, jnp.bfloat16),
         [ANY] * (len(sources) + 3) + [full((1, units))] * 2,
-        full((images * 2 * rows, 2 * units)),
+        full(out),
         [
             pltpu.VMEM((images * 2 * rows, width), jnp.bfloat16),
             pltpu.VMEM((2 * units, width), jnp.bfloat16),
             pltpu.SemaphoreType.DMA((len(sources),)),
             pltpu.SemaphoreType.DMA((3,)),
         ],
+        room=16,
     )(place, *sources, *weights, *biases)
 
 
-def down_kernel(place, ours, theirs, weights, near, crossed, *refs):
-    outs, (held, sems) = refs[:-2], refs[-2:]
-    units = held.shape[1] // 2
+def down_kernel(chunk, place, ours, theirs, own, given, near, crossed, *refs):
+    outs, (values, held, value_sems, sems) = refs[:4], refs[4:]
+    units = given.shape[0]
     half = units // 2
-    rows = outs[0].shape[0]
-    copies = []
+    rows, size = outs[0].shape
+    start = place[0] * (own.shape[1] - given.shape[1]) + chunk * size
+    lanes = pl.ds(pl.multiple_of(start, 128), size)
+    copies = [
+        (own.at[:, lanes], held.at[0, pl.ds(0, units), :]),
+        (given.at[:, pl.ds(chunk * size, size)], held.at[1, pl.ds(0, units), :]),
+    ]
     for lane in range(2):
-        copies.append((weights.at[pl.ds(lane * units, units), :], held.at[lane, pl.ds(0, units), :]))
         for part, source in enumerate((near, crossed)):
             copies.append(
                 (
@@ -298,33 +297,56 @@
                 )
             )
     copies = [pltpu.make_async_copy(a, b, sems.at[k]) for k, (a, b) in enumerate(copies)]
-    for copy in copies:
+    loads = []
+    for k in range(4):
+        block = pl.ds(k * rows, rows)
+        loads.append(
+            [
+                pltpu.make_async_copy(
+                    source.at[block, :], values.at[lane, block, :], value_sems.at[2 * k + lane]
+                )
+                for lane, source in enumerate((ours, theirs))
+            ]
+        )
+    order = (1, 2, 3, 0)
+    for copy in copies + sum((loads[k] for k in order), []):
         copy.start()
     for copy in copies:
         copy.wait()
-    for k, out in enumerate(outs):
+    for k in order:
+        for copy in loads[k]:
+            copy.wait()
         block = pl.ds(k * rows, rows)
-        total = jnp.dot(ours[block, :], held[0], preferred_element_type=jnp.float32)
-        total += jnp.dot(theirs[block, :], held[1], preferred_element_type=jnp.float32)
-        out[...] = total.astype(out.dtype)
-
-
-def down(place, ours, theirs, weights, near, crossed):
-    height, units = ours.shape
-    size = weights.shape[1]
-    out = (height // 4, size)
-    types = [jnp.float32] + [jnp.bfloat16] * 3
-    return call(
-        down_kernel,
-        [jax.ShapeDtypeStruct(out, t) for t in types],
-        [full((height, units))] * 2 + [ANY] * 3,
-        [full(out)] * len(types),
-        [pltpu.VMEM((2, units, size), jnp.bfloat16), pltpu.SemaphoreType.DMA((6,))],
-    )(place, ours, theirs, weights, near, crossed)
-
-
-def final_kernel(place, first, second, residual, bias, *refs):
-    out = refs[-1]
+        used = slice(0, 2 * units)
+        total = jnp.dot(values[0, block, used], held[0], preferred_element_type=jnp.float32)
+        total += jnp.dot(values[1, block, used], held[1], preferred_element_type=jnp.float32)
+        outs[k][...] = total.astype(outs[k].dtype)
+
+
+def down(chunk, place, ours, theirs, own, given, near, crossed):
+    height, depth = ours.shape
+    units = given.shape[0]
+    out = (height // 4, CHUNK)
+    return call(
+        lambda *refs: down_kernel(chunk, *refs),
+        [jax.ShapeDtypeStruct(out, jnp.float32)] + [jax.ShapeDtypeStruct(out, jnp.bfloat16)] * 3,
+        [ANY] * 6,
+        [full(out)] * 4,
+        [
+            pltpu.VMEM((2, height, depth), jnp.bfloat16),
+            pltpu.VMEM((2, 2 * units, CHUNK), jnp.bfloat16),
+            pltpu.SemaphoreType.DMA((8,)),
+            pltpu.SemaphoreType.DMA((6,)),
+        ],
+        room=16,
+    )(place, ours, theirs, own, given, near, crossed)
+
+
+def final_kernel(place, first, second, keep, other, bias, *refs):
+    parts, out = refs[:-1], refs[-1]
+    core = place[0]
+    rows = keep.shape[0]
+    columns = out.shape[0]
     left = jnp.int32(0)
     for listed in (first, second):
         for i in range(listed.shape[0]):
@@ -334,29 +356,38 @@
     def _():
         out[...] = jnp.zeros_like(out)
 
-    @pl.when(left == 0)
-    def _():
-        at = 0
-        for j, size in enumerate(CHUNKS):
-            own, *others = refs[4 * j : 4 * j + 4]
+    def write(is_first):
+        spare = 2 * CHUNK - columns
+        for j in range(2):
+            lanes = slice(j * CHUNK, (j + 1) * CHUNK)
+            own, *others = parts[4 * j : 4 * j + 4]
             total = own[...]
-            for other in others:
-                total = total + other[...].astype(jnp.float32)
-            total = total + residual[:, at : at + size].astype(jnp.float32)
-            total = total + bias[at : at + size]
-            out[:, at : at + size] = total.astype(jnp.bfloat16)
-            at += size
-
-
-def final(place, first, second, residual, bias, parts):
-    rows, columns = residual.shape
+            for part in others:
+                total = total + part[...].astype(jnp.float32)
+            halves = (keep, other) if is_first else (other, keep)
+            residual = jnp.concatenate([half[:, lanes] for half in halves], axis=0)
+            total = total + residual.astype(jnp.float32)
+            total = (total + bias[:, lanes]).astype(jnp.bfloat16).T
+            if is_first and j == 1:
+                total = total[: CHUNK - spare]
+            if not is_first and j == 0:
+                total = total[spare:]
+            at = j * CHUNK if is_first or j == 0 else CHUNK - spare
+            out[at : at + total.shape[0], :] = total
+
+    for side in range(2):
+        pl.when((left == 0) & (core == side))(lambda side=side: write(side == 0))
+
+
+def final(place, first, second, keep, other, bias, parts, columns):
+    rows = 2 * keep.shape[0]
     scalars = pl.BlockSpec(memory_space=pltpu.SMEM)
     return call(
         final_kernel,
-        jax.ShapeDtypeStruct((rows, columns), jnp.bfloat16),
-        [scalars] * 2 + [full((rows, columns)), full((columns,))] + [full(p.shape) for p in parts],
-        full((rows, columns)),
-    )(place, first, second, residual, bias, *parts)
+        jax.ShapeDtypeStruct((columns, rows), jnp.bfloat16),
+        [scalars] * 2 + [full(v.shape) for v in (keep, other, bias, *parts)],
+        full((columns, rows)),
+    )(place, first, second, keep, other, bias, *parts).T
 
 
 def square_plan(
@@ -380,42 +411,49 @@
     half = units // 2
     columns = width // 2
 
+    window = 2 * CHUNK
+    spare = window - columns
     up_own = up_weight.T
     down_own = down_weight.T
     up_half = lax.dynamic_slice_in_dim(up_own, plane * half, half, 0)
     cross_a = swap(up_half, "sec", 4)
-    inputs = (patch_tokens[0], skip_features[0], skip_weight, norm_gain, norm_bias)
-    mine = lead(place, *inputs)
+    mine, keep, lend = lead(
+        place, window, patch_tokens[0], skip_features[0], skip_weight, norm_gain, norm_bias
+    )
+    tok_z = swap(mine, "sec", 2)
     tok_x = swap(mine, "sec", 1)
-    tok_z = swap(mine, "sec", 2)
-    give = jnp.where(core == 0, down_own[:, columns:], down_own[:, :columns])
-    here_0, message_0, here_1, message_1 = layout(after(place, mine), down_own, swap(give, "tp", 1))
-    residual, normed = front(after(place, message_0), *inputs)
-    cross_a, tok_x, tok_z, residual = lax.optimization_barrier((cross_a, tok_x, tok_z, residual))
+    given = swap(give(place, down_own, window), "tp", 1)
+    message_0, message_1 = messages(after(place, mine), down_own, given)
+    bias_own = up_bias.reshape(1, units)
+    bias_far = swap(bias_own, "sec", 4)
+    near_0 = swap(message_0, "sec", 4)
+    near_1 = swap(message_1, "sec", 4)
     tok_d = swap(tok_z, "sec", 1)
     pair_x = swap(tok_x, "tp", 1)
     pair_z = swap(tok_z, "tp", 1)
-    pair_d = swap(tok_d, "tp", 1)
-    cross_b = swap(after(cross_a, mine), "rep", 1)
-    near_0 = swap(message_0, "sec", 4)
-    near_1 = swap(message_1, "sec", 4)
-    pair_z = swap(after(tok_z, near_0), "tp", 1)
-    bias_own = up_bias.reshape(1, units)
-    bias_far = swap(bias_own, "sec", 4)
+    pair_own = swap(mine, "tp", 1)
+    pair_keep = swap(lend, "tp", 1)
+    pair_d = swap(after(tok_d, near_0), "tp", 1)
+    cross_b = swap(after(cross_a, message_0), "rep", 1)
+    crossed_0 = swap(near_0, "rep", 1)
+    crossed_1 = swap(near_1, "rep", 1)
     bias_far = jnp.where(
         plane == 0, bias_far, jnp.concatenate([bias_far[:, half:], bias_far[:, :half]], axis=1)
     )
-    halves = (tok_x, pair_x, tok_z, pair_z, tok_d, pair_d)
-    ours = hidden_of(place, normed, halves, (up_own, cross_a, cross_b), (bias_own, bias_far))
-    theirs = swap(after(ours, near_1), "tp", 1)
-    crossed_0 = swap(near_0, "rep", 1)
-    crossed_1 = swap(near_1, "rep", 1)
-    sums_0 = down(place, ours, theirs, here_0, near_0, crossed_0)
-    sums_1 = down(after(place, sums_0[0]), ours, theirs, here_1, near_1, crossed_1)
+    tokens = (mine, pair_own, tok_x, pair_x, tok_z, pair_z, tok_d, pair_d)
+    ours = hidden_of(place, tokens, (up_own, cross_a, cross_b), (bias_own, bias_far))
+    theirs = swap(after(ours, near_1, crossed_0), "tp", 1)
+    sums_0 = down(0, place, ours, theirs, down_own, given, near_0, crossed_0)
+    sums_1 = down(1, after(place, sums_0[0]), ours, theirs, down_own, given, near_1, crossed_1)
     parts = []
     for own, *sent in (sums_0, sums_1):
         parts += [own, *(swap(part, "sec", mask) for mask, part in enumerate(sent, 1))]
-    return final(place, exit_first, exit_second, residual, down_bias, parts)[None]
+    shift = jnp.where(
+        core == 0, jnp.pad(down_bias, (0, spare)), jnp.pad(down_bias, (spare, 0))
+    ).reshape(1, window)
+    return final(
+        place, exit_first, exit_second, keep, pair_keep, shift, parts, columns
+    )[None]
 
 
 def project(tokens_rows, skip_rows, skip_weight):

time: 87 us -> 83.4 us (0.959)
  starting transfers between devices: 19.6 us -> 24 us
  Pallas kernels: 26.1 us -> 23 us
  local copies, waits for them, and re-layouts: 4.87 us -> 1.86 us
  waiting for transfers between devices: 35 us -> 33.1 us
    ppermute x21 -> x23, starting transfers between devices: 19.6 us -> 24 us  [swap(): return lax.ppermute(values, axis, [(i, i ^ mask) for i in range(size)])]
    pallas_call x7, Pallas kernels: 26.1 us -> 23 us  [the longest x2 6.39 us: down(): call(lambda *refs: down_kernel(chunk, *refs), [jax.ShapeDtypeStruct(out,...]
    ppermute x21 -> x23, waiting for transfers between devices: 35 us -> 33.1 us  [swap(): return lax.ppermute(values, axis, [(i, i ^ mask) for i in range(size)])]
    ppermute x1 -> x0, local copies, waits for them, and re-layouts: 1.46 us -> none  [swap(): return lax.ppermute(values, axis, [(i, i ^ mask) for i in range(size)])]
    broadcast_in_dim x1 -> x0, local copies, waits for them, and re-layouts: 0.91 us -> none  [square_plan(): final(place, exit_first, exit_second, residual, down_bias, parts)[None]]
    unnamed x26 -> x24, local copies, waits for them, and re-layouts: 1.89 us -> 1.75 us
  transfers between devices with their start and end apart: 21 -> 23, of which waited for: 9 -> 14; matrix products, arithmetic and copies ran while one was open for 2% -> 0% of each run, Pallas kernels for 20% -> 19%
where the time goes in v3:
time: 83.4 us; the launch traced here: 83 us
  waiting for transfers between devices  33.1 us (40%)
  starting transfers between devices  24 us (29%)
  Pallas kernels  23 us (28%)
  local copies, waits for them, and re-layouts  1.86 us (2%)
    ppermute x23, waiting for transfers between devices, swap(): return lax.ppermute(values, axis, [(i, i ^ mask) for i in range(size)])  33.1 us
    ppermute x23, starting transfers between devices, swap(): return lax.ppermute(values, axis, [(i, i ^ mask) for i in range(size)])  24 us
    pallas_call x2, Pallas kernels, down(): call(lambda *refs: down_kernel(chunk, *refs), [jax.ShapeDtypeStruct(out,...  6.39 us
    pallas_call x1, Pallas kernels, lead(): call(lead_kernel, [jax.ShapeDtypeStruct((rows, size), jnp.bfloat16) for s...  5.01 us
    pallas_call x1, Pallas kernels, hidden_of(): call(hidden_kernel, jax.ShapeDtypeStruct(out, jnp.bfloat16), [ANY] * (len...  4.95 us
    pallas_call x1, Pallas kernels, messages(): call(message_kernel, [jax.ShapeDtypeStruct((units, CHUNK), jnp.bfloat16)]...  2.45 us
    pallas_call x1, Pallas kernels, give(): call(give_kernel, jax.ShapeDtypeStruct((units, window), jnp.bfloat16), [A...  2.38 us
    pallas_call x1, Pallas kernels, final(): call(final_kernel, jax.ShapeDtypeStruct((columns, rows), jnp.bfloat16), [...  1.87 us
  transfers between devices with their start and end apart: 23, of which 14 were waited for; matrix products, arithmetic and copies ran while one was open for 0% of the time, Pallas kernels for 19%

profile of v3, /device:TPU:0, one launch (start us, length us, event | category | flops | bytes accessed | tf_op | source)
XLA Modules:
  0.0 83.0 jit_solution(11516960785815745169)
XLA Ops:
  0.0 0.6 pad_add_fusion.place.refs_0_
  0.6 5.0 %shard_map.109 = (bf16[128,1408]{1,0:T(8,128)(2,1)}, bf16[128,768]{1,0:T(8,128)(2,1)}, bf16[128,768]{1,0:T(8,128)(2,1)}) custom-call(s32[3]{0:T(128)} %pad_add_fusion.place.refs_0_, bf16[256,1408]{1,0:T(8,128)(2,1)} %bitcast.17, bf16[256,1024]{1,0:T(8,128)(2,1)} %bitcast.18, bf16[1024,1408]{1,0:T(8,128)(2,1)} %weight.1, f32[1408]{0:T(1024)} %gain.1, f32[1408]{0:T(1024)} %shift.1), custom_call_target="tpu_custom_call" | custom-call | flops 1000 | bytes 1000 | tf_op jit(solution)/shard_map/pallas_call | solution.py:155
  5.6 3.1 %collective-permute-start.4 = (bf16[128,1408]{1,0:T(8,128)(2,1)}, bf16[128,1408]{1,0:T(8,128)(2,1)S(1)}, u32[]{:S(2)}, u32[]{:S(2)}) collective-permute-start(bf16[128,1408]{1,0:T(8,128)(2,1)} %get-tuple-element.25.refs_0_), channel_id=1, source_target_pairs={{0,4},{2,6},{4,0},{6,2},{8,12},{10,14},{12,8},{14,10},{1,5},{3,7},... | collective-permute-start | bytes 1081352 | tf_op jit(solution)/shard_map/ppermute | solution.py:16
  8.7 2.4 %shard_map.110 = bf16[224,768]{1,0:T(8,128)(2,1)} custom-call(s32[3]{0:T(128)} %pad_add_fusion.place.refs_0_, bf16[224,1408]{1,0:T(8,128)(2,1)} %bitcast.12), custom_call_target="tpu_custom_call" | custom-call | flops 1000 | bytes 1000 | tf_op jit(solution)/shard_map/pallas_call | solution.py:60
  11.1 0.1 collective-permute-start.7
  11.3 0.0 copy-start
  11.3 2.7 %collective-permute-start.10 = (bf16[112,1408]{1,0:T(8,128)(2,1)S(1)}, bf16[112,1408]{1,0:T(8,128)(2,1)S(1)}, u32[]{:S(2)}, u32[]{:S(2)}) collective-permute-start(bf16[112,1408]{1,0:T(8,128)(2,1)S(1)} %dynamic-slice_bitcast_fusion), channel_id=1, source_target_pairs={{0,8},{2,10},{4,12},{6,14},{8,0},{10,2},{12,4},{14,6},{1,9},{3,11}... | collective-permute-start | bytes 946184 | tf_op jit(solution)/shard_map/ppermute | solution.py:16
  13.9 1.5 %collective-permute-start.2 = (bf16[128,1408]{1,0:T(8,128)(2,1)}, bf16[128,1408]{1,0:T(8,128)(2,1)S(1)}, u32[]{:S(2)}, u32[]{:S(2)}) collective-permute-start(bf16[128,1408]{1,0:T(8,128)(2,1)} %get-tuple-element.25.refs_0_), channel_id=1, source_target_pairs={{0,2},{2,0},{4,6},{6,4},{8,10},{10,8},{12,14},{14,12},{1,3},{3,1},... | collective-permute-start | bytes 1081352 | tf_op jit(solution)/shard_map/ppermute | solution.py:16
  15.4 6.3 %collective-permute-done.4.refs_4_ = bf16[128,1408]{1,0:T(8,128)(2,1)S(1)} collective-permute-done((bf16[128,1408]{1,0:T(8,128)(2,1)}, bf16[128,1408]{1,0:T(8,128)(2,1)S(1)}, u32[]{:S(2)}, u32[]{:S(2)}) %collective-permute-start.4) | collective-permute-done | bytes 360480 | tf_op jit(solution)/shard_map/ppermute | solution.py:16
  21.7 1.7 %collective-permute-start.6 = (bf16[128,1408]{1,0:T(8,128)(2,1)S(1)}, bf16[128,1408]{1,0:T(8,128)(2,1)S(1)}, u32[]{:S(2)}, u32[]{:S(2)}) collective-permute-start(bf16[128,1408]{1,0:T(8,128)(2,1)S(1)} %collective-permute-done.4.refs_4_), channel_id=1, source_target_pairs={{0,2},{2,0},{4,6},{6,4},{8,10},{10,8},{12,14},{14,12},{1,3},{3,1},... | collective-permute-start | bytes 1081352 | tf_op jit(solution)/shard_map/ppermute | solution.py:16
  23.3 0.0 collective-permute-done.7.given.refs_4_
  23.3 0.7 copy-done.1
  24.1 2.5 %shard_map.111 = (bf16[224,384]{1,0:T(8,128)(2,1)}, bf16[224,384]{1,0:T(8,128)(2,1)}) custom-call(s32[3]{0:T(128)} %pad_add_fusion.place.refs_0_, bf16[224,1408]{1,0:T(8,128)(2,1)} %bitcast.13, bf16[224,768]{1,0:T(8,128)(2,1)} %copy-done.1), custom_call_target="tpu_custom_call" | custom-call | flops 1000 | bytes 1000 | tf_op jit(solution)/shard_map/pallas_call | solution.py:90
  26.5 0.7 collective-permute-start.8
  27.3 0.0 collective-permute-start.1
  27.3 1.7 %collective-permute-done.10.refs_9_ = bf16[112,1408]{1,0:T(8,128)(2,1)S(1)} collective-permute-done((bf16[112,1408]{1,0:T(8,128)(2,1)S(1)}, bf16[112,1408]{1,0:T(8,128)(2,1)S(1)}, u32[]{:S(2)}, u32[]{:S(2)}) %collective-permute-start.10) | collective-permute-done | bytes 315424 | tf_op jit(solution)/shard_map/ppermute | solution.py:16
  28.9 3.4 %collective-permute-start.11 = (bf16[112,1408]{1,0:T(8,128)(2,1)S(1)}, bf16[112,1408]{1,0:T(8,128)(2,1)}, u32[]{:S(2)}, u32[]{:S(2)}) collective-permute-start(bf16[112,1408]{1,0:T(8,128)(2,1)S(1)} %collective-permute-done.10.refs_9_), channel_id=1, source_target_pairs={{0,16},{16,0},{1,17},{17,1},{2,18},{18,2},{3,19},{19,3},{4,20},{20... | collective-permute-start | bytes 946184 | tf_op jit(solution)/shard_map/ppermute | solution.py:16
  32.3 0.0 copy-done.11
  32.3 0.0 collective-permute-done.2.refs_2_
  32.3 0.1 collective-permute-start.12
  32.4 3.9 %collective-permute-done.8.refs_5_ = bf16[224,384]{1,0:T(8,128)(2,1)S(1)} collective-permute-done((bf16[224,384]{1,0:T(8,128)(2,1)}, bf16[224,384]{1,0:T(8,128)(2,1)S(1)}, u32[]{:S(2)}, u32[]{:S(2)}) %collective-permute-start.8) | collective-permute-done | bytes 172064 | tf_op jit(solution)/shard_map/ppermute | solution.py:16
  36.3 0.0 collective-permute-start.5
  36.3 0.0 collective-permute-done.6.refs_6_
  36.3 0.5 collective-permute-start.3
  36.8 0.1 collective-permute-done.12
  36.9 0.0 collective-permute-start.9
  36.9 0.1 fusion
  36.9 0.0 collective-permute-done.1.refs_1_
  36.9 0.0 collective-permute-start.13
  37.0 1.1 %collective-permute-done.11.refs_10_ = bf16[112,1408]{1,0:T(8,128)(2,1)} collective-permute-done((bf16[112,1408]{1,0:T(8,128)(2,1)S(1)}, bf16[112,1408]{1,0:T(8,128)(2,1)}, u32[]{:S(2)}, u32[]{:S(2)}) %collective-permute-start.11) | collective-permute-done | bytes 315424 | tf_op jit(solution)/shard_map/ppermute | solution.py:16
  38.0 1.5 %collective-permute-start.14 = (bf16[224,384]{1,0:T(8,128)(2,1)S(1)}, bf16[224,384]{1,0:T(8,128)(2,1)S(1)}, u32[]{:S(2)}, u32[]{:S(2)}) collective-permute-start(bf16[224,384]{1,0:T(8,128)(2,1)S(1)} %collective-permute-done.8.refs_5_), channel_id=1, source_target_pairs={{0,16},{16,0},{1,17},{17,1},{2,18},{18,2},{3,19},{19,3},{4,20},{20... | collective-permute-start | bytes 516104 | tf_op jit(solution)/shard_map/ppermute | solution.py:16
  39.5 0.1 broadcast_select_fusion.refs_12_
  39.6 0.0 collective-permute-done.5.refs_5_
  39.6 0.0 collective-permute-done.3.refs_3_
  39.6 0.0 collective-permute-done.9.refs_7_
  39.6 0.0 copy-start.4
  39.6 1.0 %copy-done.4 = bf16[128,1408]{1,0:T(8,128)(2,1)S(1)} copy-done((bf16[128,1408]{1,0:T(8,128)(2,1)S(1)}, bf16[128,1408]{1,0:T(8,128)(2,1)}, u32[]{:S(2)}) %copy-start.4) | copy-done | bytes 360472
  40.6 4.9 %shard_map.112.refs_1_ = bf16[1024,512]{1,0:T(8,128)(2,1)S(1)} custom-call(s32[3]{0:T(128)S(1)} %copy-done.6, bf16[128,1408]{1,0:T(8,128)(2,1)S(1)} %copy-done.4, bf16[128,1408]{1,0:T(8,128)(2,1)S(1)} %collective-permute-done.1.refs_1_, bf16[128,1408]{1,0:T(8,128)(2,1)S(1)} %collective-permute-done.2.refs_2_, ...), custom_call_target="tpu_custom_call" | custom-call | flops 1000 | bytes 1000 | tf_op jit(solution)/shard_map/pallas_call | solution.py:265
  45.6 2.9 %collective-permute-done.13.refs_5_ = bf16[224,384]{1,0:T(8,128)(2,1)S(1)} collective-permute-done((bf16[224,384]{1,0:T(8,128)(2,1)}, bf16[224,384]{1,0:T(8,128)(2,1)S(1)}, u32[]{:S(2)}, u32[]{:S(2)}) %collective-permute-start.13) | collective-permute-done | bytes 172064 | tf_op jit(solution)/shard_map/ppermute | solution.py:16
  48.5 0.0 collective-permute-done.14.refs_6_
  48.5 0.0 collective-permute-start.15
  48.5 1.4 %collective-permute-start.19 = (bf16[224,384]{1,0:T(8,128)(2,1)S(1)}, bf16[224,384]{1,0:T(8,128)(2,1)S(1)}, u32[]{:S(2)}, u32[]{:S(2)}) collective-permute-start(bf16[224,384]{1,0:T(8,128)(2,1)S(1)} %collective-permute-done.13.refs_5_), channel_id=1, source_target_pairs={{0,16},{16,0},{1,17},{17,1},{2,18},{18,2},{3,19},{19,3},{4,20},{20... | collective-permute-start | bytes 516104 | tf_op jit(solution)/shard_map/ppermute | solution.py:16
  50.0 0.0 copy-start.8
  50.0 0.3 collective-permute-start
  50.3 0.9 %collective-permute-done.15.refs_2_ = bf16[1024,512]{1,0:T(8,128)(2,1)S(1)} collective-permute-done((bf16[1024,512]{1,0:T(8,128)(2,1)S(1)}, bf16[1024,512]{1,0:T(8,128)(2,1)S(1)}, u32[]{:S(2)}, u32[]{:S(2)}) %collective-permute-start.15) | collective-permute-done | bytes 1048608 | tf_op jit(solution)/shard_map/ppermute | solution.py:16
  51.2 3.1 %shard_map.113 = (f32[256,384]{1,0:T(8,128)S(1)}, bf16[256,384]{1,0:T(8,128)(2,1)S(1)}, bf16[256,384]{1,0:T(8,128)(2,1)S(1)}, bf16[256,384]{1,0:T(8,128)(2,1)S(1)}) custom-call(s32[3]{0:T(128)S(1)} %copy-done.6, bf16[1024,512]{1,0:T(8,128)(2,1)S(1)} %shard_map.112.refs_1_, bf16[1024,512]{1,0:T(8,128)(2,1)S(1)} %collective-permute-done.15.refs_2_, ...), custom_call_target="tpu_custom_call" | custom-call | flops 1000 | bytes 1000 | tf_op jit(solution)/shard_map/pallas_call | solution.py:330
  54.3 1.0 %collective-permute-done.19.refs_6_ = bf16[224,384]{1,0:T(8,128)(2,1)S(1)} collective-permute-done((bf16[224,384]{1,0:T(8,128)(2,1)S(1)}, bf16[224,384]{1,0:T(8,128)(2,1)S(1)}, u32[]{:S(2)}, u32[]{:S(2)}) %collective-permute-start.19) | collective-permute-done | bytes 172064 | tf_op jit(solution)/shard_map/ppermute | solution.py:16
  55.3 3.3 %shard_map.114 = (f32[256,384]{1,0:T(8,128)S(1)}, bf16[256,384]{1,0:T(8,128)(2,1)S(1)}, bf16[256,384]{1,0:T(8,128)(2,1)}, bf16[256,384]{1,0:T(8,128)(2,1)S(1)}) custom-call(s32[3]{0:T(128)S(1)} %copy-done.6, bf16[1024,512]{1,0:T(8,128)(2,1)S(1)} %shard_map.112.refs_1_, bf16[1024,512]{1,0:T(8,128)(2,1)S(1)} %collective-permute-done.15.refs_2_, ...), custom_call_target="tpu_custom_call" | custom-call | flops 1000 | bytes 1000 | tf_op jit(solution)/shard_map/pallas_call | solution.py:330
  58.6 3.6 %collective-permute-start.20 = (bf16[256,384]{1,0:T(8,128)(2,1)S(1)}, bf16[256,384]{1,0:T(8,128)(2,1)S(1)}, u32[]{:S(2)}, u32[]{:S(2)}) collective-permute-start(bf16[256,384]{1,0:T(8,128)(2,1)S(1)} %get-tuple-element.38), channel_id=1, source_target_pairs={{0,2},{2,0},{4,6},{6,4},{8,10},{10,8},{12,14},{14,12},{1,3},{3,1},... | collective-permute-start | bytes 589832 | tf_op jit(solution)/shard_map/ppermute | solution.py:16
  62.2 0.0 collective-permute-start.21
  62.2 1.5 %collective-permute-start.22 = (bf16[256,384]{1,0:T(8,128)(2,1)S(1)}, bf16[256,384]{1,0:T(8,128)(2,1)S(1)}, u32[]{:S(2)}, u32[]{:S(2)}) collective-permute-start(bf16[256,384]{1,0:T(8,128)(2,1)S(1)} %get-tuple-element.40), channel_id=1, source_target_pairs={{0,6},{2,4},{4,2},{6,0},{8,14},{10,12},{12,10},{14,8},{1,7},{3,5},... | collective-permute-start | bytes 589832 | tf_op jit(solution)/shard_map/ppermute | solution.py:16
  63.8 1.9 %collective-permute-start.16 = (bf16[256,384]{1,0:T(8,128)(2,1)S(1)}, bf16[256,384]{1,0:T(8,128)(2,1)S(1)}, u32[]{:S(2)}, u32[]{:S(2)}) collective-permute-start(bf16[256,384]{1,0:T(8,128)(2,1)S(1)} %get-tuple-element.33), channel_id=1, source_target_pairs={{0,2},{2,0},{4,6},{6,4},{8,10},{10,8},{12,14},{14,12},{1,3},{3,1},... | collective-permute-start | bytes 589832 | tf_op jit(solution)/shard_map/ppermute | solution.py:16
  65.7 0.0 collective-permute-done.other
  65.7 0.0 collective-permute-start.17
  65.7 3.2 %collective-permute-done.20.refs_5_ = bf16[256,384]{1,0:T(8,128)(2,1)S(1)} collective-permute-done((bf16[256,384]{1,0:T(8,128)(2,1)S(1)}, bf16[256,384]{1,0:T(8,128)(2,1)S(1)}, u32[]{:S(2)}, u32[]{:S(2)}) %collective-permute-start.20) | collective-permute-done | bytes 196640 | tf_op jit(solution)/shard_map/ppermute | solution.py:16
  68.9 0.0 collective-permute-start.18
  68.9 0.0 copy-done.9
  68.9 0.1 pad_select_fusion
  69.0 1.3 %collective-permute-done.21.refs_6_ = bf16[256,384]{1,0:T(8,128)(2,1)S(1)} collective-permute-done((bf16[256,384]{1,0:T(8,128)(2,1)}, bf16[256,384]{1,0:T(8,128)(2,1)S(1)}, u32[]{:S(2)}, u32[]{:S(2)}) %collective-permute-start.21) | collective-permute-done | bytes 196640 | tf_op jit(solution)/shard_map/ppermute | solution.py:16
  70.3 3.8 %collective-permute-done.22.refs_7_ = bf16[256,384]{1,0:T(8,128)(2,1)S(1)} collective-permute-done((bf16[256,384]{1,0:T(8,128)(2,1)S(1)}, bf16[256,384]{1,0:T(8,128)(2,1)S(1)}, u32[]{:S(2)}, u32[]{:S(2)}) %collective-permute-start.22) | collective-permute-done | bytes 196640 | tf_op jit(solution)/shard_map/ppermute | solution.py:16
  74.0 1.3 %collective-permute-done.16.refs_1_ = bf16[256,384]{1,0:T(8,128)(2,1)S(1)} collective-permute-done((bf16[256,384]{1,0:T(8,128)(2,1)S(1)}, bf16[256,384]{1,0:T(8,128)(2,1)S(1)}, u32[]{:S(2)}, u32[]{:S(2)}) %collective-permute-start.16) | collective-permute-done | bytes 196640 | tf_op jit(solution)/shard_map/ppermute | solution.py:16
  75.4 3.3 %collective-permute-done.17.refs_2_ = bf16[256,384]{1,0:T(8,128)(2,1)S(1)} collective-permute-done((bf16[256,384]{1,0:T(8,128)(2,1)S(1)}, bf16[256,384]{1,0:T(8,128)(2,1)S(1)}, u32[]{:S(2)}, u32[]{:S(2)}) %collective-permute-start.17) | collective-permute-done | bytes 196640 | tf_op jit(solution)/shard_map/ppermute | solution.py:16
  78.7 2.4 %collective-permute-done.18.refs_3_ = bf16[256,384]{1,0:T(8,128)(2,1)S(1)} collective-permute-done((bf16[256,384]{1,0:T(8,128)(2,1)S(1)}, bf16[256,384]{1,0:T(8,128)(2,1)S(1)}, u32[]{:S(2)}, u32[]{:S(2)}) %collective-permute-start.18) | collective-permute-done | bytes 196640 | tf_op jit(solution)/shard_map/ppermute | solution.py:16
  81.1 1.9 %shard_map.115 = bf16[704,256]{1,0:T(8,128)(2,1)} custom-call(s32[3]{0:T(128)S(1)} %copy-done.6, s32[2]{0:T(128)S(1)} %copy-done.7, s32[2]{0:T(128)S(1)} %copy-done.8, bf16[128,768]{1,0:T(8,128)(2,1)S(1)} %copy-done.5, bf16[128,768]{1,0:T(8,128)(2,1)S(1)} %collective-permute-done.other, f32[1,768]{1,0:T(1,128)S(1)} %reshape.6.bias, ...), custom_call_target="tpu_custom_call" | custom-call | flops 1000 | bytes 1000 | tf_op jit(solution)/shard_map/pallas_call | solution.py:385
  (20 shorter events, 0.1 us)
Async XLA Ops:
  0.0 11.2 %copy-start.3 = (bf16[1408,224]{0,1:T(8,128)(2,1)S(1)}, bf16[1408,224]{0,1:T(8,128)(2,1)}, u32[]{:S(2)}) copy-start(bf16[1408,224]{0,1:T(8,128)(2,1)} %param.18) | copy-start | bytes 1892356
  0.6 31.7 %copy-start.11 = (bf16[224]{0:T(256)(128)(2,1)S(1)}, bf16[224]{0:T(256)(128)(2,1)}, u32[]{:S(2)}) copy-start(bf16[224]{0:T(256)(128)(2,1)} %param.19) | copy-start | bytes 1348
  0.6 39.0 %copy-start.6 = (s32[3]{0:T(128)S(1)}, s32[3]{0:T(128)}, u32[]{:S(2)}) copy-start(s32[3]{0:T(128)} %pad_add_fusion.place.refs_0_) | copy-start | bytes 40
  5.6 16.0 %collective-permute-start.4 = (bf16[128,1408]{1,0:T(8,128)(2,1)}, bf16[128,1408]{1,0:T(8,128)(2,1)S(1)}, u32[]{:S(2)}, u32[]{:S(2)}) collective-permute-start(bf16[128,1408]{1,0:T(8,128)(2,1)} %get-tuple-element.25.refs_0_), channel_id=1, source_target_pairs={{0,4},{2,6},{4,0},{6,2},{8,12},{10,14},{12,8},{14,10},{1,5},{3,7},... | collective-permute-start | bytes 1081352 | tf_op jit(solution)/shard_map/ppermute | solution.py:16
  11.1 12.2 %collective-permute-start.7 = (bf16[224,768]{1,0:T(8,128)(2,1)}, bf16[224,768]{1,0:T(8,128)(2,1)S(1)}, u32[]{:S(2)}, u32[]{:S(2)}) collective-permute-start(bf16[224,768]{1,0:T(8,128)(2,1)} %shard_map.110), channel_id=1, source_target_pairs={{0,1},{1,0},{2,3},{3,2},{4,5},{5,4},{6,7},{7,6},{8,9},{9,8},{10,11... | collective-permute-start | bytes 1032200 | tf_op jit(solution)/shard_map/ppermute | solution.py:16
  11.3 39.9 %copy-start = (bf16[1408,224]{0,1:T(8,128)(2,1)S(1)}, bf16[1408,224]{0,1:T(8,128)(2,1)}, u32[]{:S(2)}) copy-start(bf16[1408,224]{0,1:T(8,128)(2,1)} %param.20) | copy-start | bytes 1892356
  11.3 17.7 %collective-permute-start.10 = (bf16[112,1408]{1,0:T(8,128)(2,1)S(1)}, bf16[112,1408]{1,0:T(8,128)(2,1)S(1)}, u32[]{:S(2)}, u32[]{:S(2)}) collective-permute-start(bf16[112,1408]{1,0:T(8,128)(2,1)S(1)} %dynamic-slice_bitcast_fusion), channel_id=1, source_target_pairs={{0,8},{2,10},{4,12},{6,14},{8,0},{10,2},{12,4},{14,6},{1,9},{3,11}... | collective-permute-start | bytes 946184 | tf_op jit(solution)/shard_map/ppermute | solution.py:16
  13.9 18.4 %collective-permute-start.2 = (bf16[128,1408]{1,0:T(8,128)(2,1)}, bf16[128,1408]{1,0:T(8,128)(2,1)S(1)}, u32[]{:S(2)}, u32[]{:S(2)}) collective-permute-start(bf16[128,1408]{1,0:T(8,128)(2,1)} %get-tuple-element.25.refs_0_), channel_id=1, source_target_pairs={{0,2},{2,0},{4,6},{6,4},{8,10},{10,8},{12,14},{14,12},{1,3},{3,1},... | collective-permute-start | bytes 1081352 | tf_op jit(solution)/shard_map/ppermute | solution.py:16
  21.7 14.6 %collective-permute-start.6 = (bf16[128,1408]{1,0:T(8,128)(2,1)S(1)}, bf16[128,1408]{1,0:T(8,128)(2,1)S(1)}, u32[]{:S(2)}, u32[]{:S(2)}) collective-permute-start(bf16[128,1408]{1,0:T(8,128)(2,1)S(1)} %collective-permute-done.4.refs_4_), channel_id=1, source_target_pairs={{0,2},{2,0},{4,6},{6,4},{8,10},{10,8},{12,14},{14,12},{1,3},{3,1},... | collective-permute-start | bytes 1081352 | tf_op jit(solution)/shard_map/ppermute | solution.py:16
  23.3 0.7 copy-start.1
  26.5 24.7 %copy-start.2 = (bf16[224,768]{1,0:T(8,128)(2,1)S(1)}, bf16[224,768]{1,0:T(8,128)(2,1)}, u32[]{:S(2)}) copy-start(bf16[224,768]{1,0:T(8,128)(2,1)} %copy-done.1) | copy-start | bytes 1032196
  26.5 9.7 %collective-permute-start.8 = (bf16[224,384]{1,0:T(8,128)(2,1)}, bf16[224,384]{1,0:T(8,128)(2,1)S(1)}, u32[]{:S(2)}, u32[]{:S(2)}) collective-permute-start(bf16[224,384]{1,0:T(8,128)(2,1)} %get-tuple-element.27), channel_id=1, source_target_pairs={{0,8},{2,10},{4,12},{6,14},{8,0},{10,2},{12,4},{14,6},{1,9},{3,11}... | collective-permute-start | bytes 516104 | tf_op jit(solution)/shard_map/ppermute | solution.py:16
  27.3 9.7 %collective-permute-start.1 = (bf16[128,1408]{1,0:T(8,128)(2,1)}, bf16[128,1408]{1,0:T(8,128)(2,1)S(1)}, u32[]{:S(2)}, u32[]{:S(2)}) collective-permute-start(bf16[128,1408]{1,0:T(8,128)(2,1)} %get-tuple-element.25.refs_0_), channel_id=1, source_target_pairs={{0,1},{1,0},{2,3},{3,2},{4,5},{5,4},{6,7},{7,6},{8,9},{9,8},{10,11... | collective-permute-start | bytes 1081352 | tf_op jit(solution)/shard_map/ppermute | solution.py:16
  28.9 9.1 %collective-permute-start.11 = (bf16[112,1408]{1,0:T(8,128)(2,1)S(1)}, bf16[112,1408]{1,0:T(8,128)(2,1)}, u32[]{:S(2)}, u32[]{:S(2)}) collective-permute-start(bf16[112,1408]{1,0:T(8,128)(2,1)S(1)} %collective-permute-done.10.refs_9_), channel_id=1, source_target_pairs={{0,16},{16,0},{1,17},{17,1},{2,18},{18,2},{3,19},{19,3},{4,20},{20... | collective-permute-start | bytes 946184 | tf_op jit(solution)/shard_map/ppermute | solution.py:16
  32.3 4.5 %collective-permute-start.12 = (bf16[1,224]{1,0:T(2,128)(2,1)S(1)}, bf16[1,224]{1,0:T(2,128)(2,1)S(1)}, u32[]{:S(2)}, u32[]{:S(2)}) collective-permute-start(bf16[1,224]{1,0:T(2,128)(2,1)S(1)} %reshape.7.refs_11_), channel_id=1, source_target_pairs={{0,8},{2,10},{4,12},{6,14},{8,0},{10,2},{12,4},{14,6},{1,9},{3,11}... | collective-permute-start | bytes 1352 | tf_op jit(solution)/shard_map/ppermute | solution.py:16
  36.3 3.4 %collective-permute-start.5 = (bf16[128,1408]{1,0:T(8,128)(2,1)S(1)}, bf16[128,1408]{1,0:T(8,128)(2,1)S(1)}, u32[]{:S(2)}, u32[]{:S(2)}) collective-permute-start(bf16[128,1408]{1,0:T(8,128)(2,1)S(1)} %collective-permute-done.4.refs_4_), channel_id=1, source_target_pairs={{0,1},{1,0},{2,3},{3,2},{4,5},{5,4},{6,7},{7,6},{8,9},{9,8},{10,11... | collective-permute-start | bytes 1081352 | tf_op jit(solution)/shard_map/ppermute | solution.py:16
  36.3 3.3 %collective-permute-start.3 = (bf16[128,1408]{1,0:T(8,128)(2,1)S(1)}, bf16[128,1408]{1,0:T(8,128)(2,1)S(1)}, u32[]{:S(2)}, u32[]{:S(2)}) collective-permute-start(bf16[128,1408]{1,0:T(8,128)(2,1)S(1)} %collective-permute-done.2.refs_2_), channel_id=1, source_target_pairs={{0,1},{1,0},{2,3},{3,2},{4,5},{5,4},{6,7},{7,6},{8,9},{9,8},{10,11... | collective-permute-start | bytes 1081352 | tf_op jit(solution)/shard_map/ppermute | solution.py:16
  36.9 2.8 %collective-permute-start.9 = (bf16[128,1408]{1,0:T(8,128)(2,1)S(1)}, bf16[128,1408]{1,0:T(8,128)(2,1)S(1)}, u32[]{:S(2)}, u32[]{:S(2)}) collective-permute-start(bf16[128,1408]{1,0:T(8,128)(2,1)S(1)} %collective-permute-done.6.refs_6_), channel_id=1, source_target_pairs={{0,1},{1,0},{2,3},{3,2},{4,5},{5,4},{6,7},{7,6},{8,9},{9,8},{10,11... | collective-permute-start | bytes 1081352 | tf_op jit(solution)/shard_map/ppermute | solution.py:16
  36.9 11.6 %collective-permute-start.13 = (bf16[224,384]{1,0:T(8,128)(2,1)}, bf16[224,384]{1,0:T(8,128)(2,1)S(1)}, u32[]{:S(2)}, u32[]{:S(2)}) collective-permute-start(bf16[224,384]{1,0:T(8,128)(2,1)} %get-tuple-element.30), channel_id=1, source_target_pairs={{0,8},{2,10},{4,12},{6,14},{8,0},{10,2},{12,4},{14,6},{1,9},{3,11}... | collective-permute-start | bytes 516104 | tf_op jit(solution)/shard_map/ppermute | solution.py:16
  38.0 10.5 %collective-permute-start.14 = (bf16[224,384]{1,0:T(8,128)(2,1)S(1)}, bf16[224,384]{1,0:T(8,128)(2,1)S(1)}, u32[]{:S(2)}, u32[]{:S(2)}) collective-permute-start(bf16[224,384]{1,0:T(8,128)(2,1)S(1)} %collective-permute-done.8.refs_5_), channel_id=1, source_target_pairs={{0,16},{16,0},{1,17},{17,1},{2,18},{18,2},{3,19},{19,3},{4,20},{20... | collective-permute-start | bytes 516104 | tf_op jit(solution)/shard_map/ppermute | solution.py:16
  39.6 1.0 %copy-start.4 = (bf16[128,1408]{1,0:T(8,128)(2,1)S(1)}, bf16[128,1408]{1,0:T(8,128)(2,1)}, u32[]{:S(2)}) copy-start(bf16[128,1408]{1,0:T(8,128)(2,1)} %get-tuple-element.25.refs_0_) | copy-start | bytes 1081348
  40.6 9.3 %copy-start.10 = (bf16[128,768]{1,0:T(8,128)(2,1)S(1)}, bf16[128,768]{1,0:T(8,128)(2,1)}, u32[]{:S(2)}) copy-start(bf16[128,768]{1,0:T(8,128)(2,1)} %get-tuple-element.24) | copy-start | bytes 589828
  48.5 2.7 %collective-permute-start.15 = (bf16[1024,512]{1,0:T(8,128)(2,1)S(1)}, bf16[1024,512]{1,0:T(8,128)(2,1)S(1)}, u32[]{:S(2)}, u32[]{:S(2)}) collective-permute-start(bf16[1024,512]{1,0:T(8,128)(2,1)S(1)} %shard_map.112.refs_1_), channel_id=1, source_target_pairs={{0,1},{1,0},{2,3},{3,2},{4,5},{5,4},{6,7},{7,6},{8,9},{9,8},{10,11... | collective-permute-start | bytes 3145736 | tf_op jit(solution)/shard_map/ppermute | solution.py:16
  48.5 6.8 %collective-permute-start.19 = (bf16[224,384]{1,0:T(8,128)(2,1)S(1)}, bf16[224,384]{1,0:T(8,128)(2,1)S(1)}, u32[]{:S(2)}, u32[]{:S(2)}) collective-permute-start(bf16[224,384]{1,0:T(8,128)(2,1)S(1)} %collective-permute-done.13.refs_5_), channel_id=1, source_target_pairs={{0,16},{16,0},{1,17},{17,1},{2,18},{18,2},{3,19},{19,3},{4,20},{20... | collective-permute-start | bytes 516104 | tf_op jit(solution)/shard_map/ppermute | solution.py:16
  50.0 18.9 %copy-start.9 = (f32[704]{0:T(1024)S(1)}, f32[704]{0:T(1024)}, u32[]{:S(2)}) copy-start(f32[704]{0:T(1024)} %param.21) | copy-start | bytes 8452
  50.0 31.1 %copy-start.5 = (bf16[128,768]{1,0:T(8,128)(2,1)S(1)}, bf16[128,768]{1,0:T(8,128)(2,1)}, u32[]{:S(2)}) copy-start(bf16[128,768]{1,0:T(8,128)(2,1)} %get-tuple-element.23.keep) | copy-start | bytes 589828
  50.0 31.1 %copy-start.7 = (s32[2]{0:T(128)S(1)}, s32[2]{0:T(128)}, u32[]{:S(2)}) copy-start(s32[2]{0:T(128)} %first.1) | copy-start | bytes 28
  50.0 31.1 %copy-start.8 = (s32[2]{0:T(128)S(1)}, s32[2]{0:T(128)}, u32[]{:S(2)}) copy-start(s32[2]{0:T(128)} %second.1) | copy-start | bytes 28
  50.0 15.7 %collective-permute-start = (bf16[128,768]{1,0:T(8,128)(2,1)S(1)}, bf16[128,768]{1,0:T(8,128)(2,1)S(1)}, u32[]{:S(2)}, u32[]{:S(2)}) collective-permute-start(bf16[128,768]{1,0:T(8,128)(2,1)S(1)} %copy-done.10), channel_id=1, source_target_pairs={{0,1},{1,0},{2,3},{3,2},{4,5},{5,4},{6,7},{7,6},{8,9},{9,8},{10,11... | collective-permute-start | bytes 589832 | tf_op jit(solution)/shard_map/ppermute | solution.py:16
  58.6 10.3 %collective-permute-start.20 = (bf16[256,384]{1,0:T(8,128)(2,1)S(1)}, bf16[256,384]{1,0:T(8,128)(2,1)S(1)}, u32[]{:S(2)}, u32[]{:S(2)}) collective-permute-start(bf16[256,384]{1,0:T(8,128)(2,1)S(1)} %get-tuple-element.38), channel_id=1, source_target_pairs={{0,2},{2,0},{4,6},{6,4},{8,10},{10,8},{12,14},{14,12},{1,3},{3,1},... | collective-permute-start | bytes 589832 | tf_op jit(solution)/shard_map/ppermute | solution.py:16
  62.2 8.0 %collective-permute-start.21 = (bf16[256,384]{1,0:T(8,128)(2,1)}, bf16[256,384]{1,0:T(8,128)(2,1)S(1)}, u32[]{:S(2)}, u32[]{:S(2)}) collective-permute-start(bf16[256,384]{1,0:T(8,128)(2,1)} %get-tuple-element.39), channel_id=1, source_target_pairs={{0,4},{2,6},{4,0},{6,2},{8,12},{10,14},{12,8},{14,10},{1,5},{3,7},... | collective-permute-start | bytes 589832 | tf_op jit(solution)/shard_map/ppermute | solution.py:16
  62.2 11.8 %collective-permute-start.22 = (bf16[256,384]{1,0:T(8,128)(2,1)S(1)}, bf16[256,384]{1,0:T(8,128)(2,1)S(1)}, u32[]{:S(2)}, u32[]{:S(2)}) collective-permute-start(bf16[256,384]{1,0:T(8,128)(2,1)S(1)} %get-tuple-element.40), channel_id=1, source_target_pairs={{0,6},{2,4},{4,2},{6,0},{8,14},{10,12},{12,10},{14,8},{1,7},{3,5},... | collective-permute-start | bytes 589832 | tf_op jit(solution)/shard_map/ppermute | solution.py:16
  63.8 11.6 %collective-permute-start.16 = (bf16[256,384]{1,0:T(8,128)(2,1)S(1)}, bf16[256,384]{1,0:T(8,128)(2,1)S(1)}, u32[]{:S(2)}, u32[]{:S(2)}) collective-permute-start(bf16[256,384]{1,0:T(8,128)(2,1)S(1)} %get-tuple-element.33), channel_id=1, source_target_pairs={{0,2},{2,0},{4,6},{6,4},{8,10},{10,8},{12,14},{14,12},{1,3},{3,1},... | collective-permute-start | bytes 589832 | tf_op jit(solution)/shard_map/ppermute | solution.py:16
  65.7 13.0 %collective-permute-start.17 = (bf16[256,384]{1,0:T(8,128)(2,1)S(1)}, bf16[256,384]{1,0:T(8,128)(2,1)S(1)}, u32[]{:S(2)}, u32[]{:S(2)}) collective-permute-start(bf16[256,384]{1,0:T(8,128)(2,1)S(1)} %get-tuple-element.34), channel_id=1, source_target_pairs={{0,4},{2,6},{4,0},{6,2},{8,12},{10,14},{12,8},{14,10},{1,5},{3,7},... | collective-permute-start | bytes 589832 | tf_op jit(solution)/shard_map/ppermute | solution.py:16
  68.9 12.2 %collective-permute-start.18 = (bf16[256,384]{1,0:T(8,128)(2,1)S(1)}, bf16[256,384]{1,0:T(8,128)(2,1)S(1)}, u32[]{:S(2)}, u32[]{:S(2)}) collective-permute-start(bf16[256,384]{1,0:T(8,128)(2,1)S(1)} %get-tuple-element.35), channel_id=1, source_target_pairs={{0,6},{2,4},{4,2},{6,0},{8,14},{10,12},{12,10},{14,8},{1,7},{3,5},... | collective-permute-start | bytes 589832 | tf_op jit(solution)/shard_map/ppermute | solution.py:16

commit v4 on v3

--- a/solution.py
+++ b/solution.py
@@ -7,7 +7,7 @@
 
 
 NT = (((1,), (1,)), ((), ()))
-CHUNK = 384
+CHUNKS = (512, 256)
 ANY = pl.BlockSpec(memory_space=pl.ANY)
 
 
@@ -73,11 +73,13 @@
     rows = aligned(place[1] * half, half)
     start = place[0] * (own.shape[1] - window)
     copies = []
-    for j, out in enumerate((first, second)):
+    at = 0
+    for out in (first, second):
         size = out.shape[1]
-        lanes = pl.ds(pl.multiple_of(start + j * size, 128), size)
+        lanes = pl.ds(pl.multiple_of(start + at, 128), size)
         copies.append((own.at[rows, lanes], out.at[pl.ds(0, half), :]))
-        copies.append((given.at[rows, pl.ds(j * size, size)], out.at[pl.ds(half, half), :]))
+        copies.append((given.at[rows, pl.ds(at, size)], out.at[pl.ds(half, half), :]))
+        at += size
     copies = [pltpu.make_async_copy(a, b, sems.at[k]) for k, (a, b) in enumerate(copies)]
     for copy in copies:
         copy.start()
@@ -89,9 +91,9 @@
     units = own.shape[0]
     return call(
         message_kernel,
-        [jax.ShapeDtypeStruct((units, CHUNK), jnp.bfloat16)] * 2,
+        [jax.ShapeDtypeStruct((units, size), jnp.bfloat16) for size in CHUNKS],
         [ANY, ANY],
-        [full((units, CHUNK))] * 2,
+        [full((units, size)) for size in CHUNKS],
         [pltpu.SemaphoreType.DMA((4,))],
         room=60,
     )(place, own, given)
@@ -273,20 +275,22 @@
             pltpu.SemaphoreType.DMA((len(sources),)),
             pltpu.SemaphoreType.DMA((3,)),
         ],
-        room=16,
+        room=12,
     )(place, *sources, *weights, *biases)
 
 
-def down_kernel(chunk, place, ours, theirs, own, given, near, crossed, *refs):
-    outs, (values, held, value_sems, sems) = refs[:4], refs[4:]
+def down_kernel(at, count, place, *refs):
+    hidden, (own, given, near, crossed) = refs[:count], refs[count : count + 4]
+    outs, (values, held, value_sems, sems) = refs[count + 4 : count + 8], refs[count + 8 :]
     units = given.shape[0]
     half = units // 2
     rows, size = outs[0].shape
-    start = place[0] * (own.shape[1] - given.shape[1]) + chunk * size
+    each = 8 // count
+    start = place[0] * (own.shape[1] - given.shape[1]) + at
     lanes = pl.ds(pl.multiple_of(start, 128), size)
     copies = [
         (own.at[:, lanes], held.at[0, pl.ds(0, units), :]),
-        (given.at[:, pl.ds(chunk * size, size)], held.at[1, pl.ds(0, units), :]),
+        (given.at[:, pl.ds(at, size)], held.at[1, pl.ds(0, units), :]),
     ]
     for lane in range(2):
         for part, source in enumerate((near, crossed)):
@@ -299,15 +303,12 @@
     copies = [pltpu.make_async_copy(a, b, sems.at[k]) for k, (a, b) in enumerate(copies)]
     loads = []
     for k in range(4):
-        block = pl.ds(k * rows, rows)
-        loads.append(
-            [
-                pltpu.make_async_copy(
-                    source.at[block, :], values.at[lane, block, :], value_sems.at[2 * k + lane]
-                )
-                for lane, source in enumerate((ours, theirs))
-            ]
-        )
+        pair = []
+        for lane in range(2):
+            source = hidden[k // each * 2 + lane].at[pl.ds(k % each * rows, rows), :]
+            to = values.at[lane, pl.ds(k * rows, rows), :]
+            pair.append(pltpu.make_async_copy(source, to, value_sems.at[2 * k + lane]))
+        loads.append(pair)
     order = (1, 2, 3, 0)
     for copy in copies + sum((loads[k] for k in order), []):
         copy.start()
@@ -323,23 +324,25 @@
         outs[k][...] = total.astype(outs[k].dtype)
 
 
-def down(chunk, place, ours, theirs, own, given, near, crossed):
-    height, depth = ours.shape
+def down(at, place, hidden, own, given, near, crossed, rows):
+    depth = hidden[0].shape[1]
     units = given.shape[0]
-    out = (height // 4, CHUNK)
-    return call(
-        lambda *refs: down_kernel(chunk, *refs),
-        [jax.ShapeDtypeStruct(out, jnp.float32)] + [jax.ShapeDtypeStruct(out, jnp.bfloat16)] * 3,
-        [ANY] * 6,
-        [full(out)] * 4,
+    size = near.shape[1]
+    count = len(hidden)
+    return call(
+        lambda *refs: down_kernel(at, count, *refs),
+        [jax.ShapeDtypeStruct((rows, size), jnp.float32)]
+        + [jax.ShapeDtypeStruct((rows, size), jnp.bfloat16)] * 3,
+        [ANY] * (count + 4),
+        [full((rows, size))] * 4,
         [
-            pltpu.VMEM((2, height, depth), jnp.bfloat16),
-            pltpu.VMEM((2, 2 * units, CHUNK), jnp.bfloat16),
+            pltpu.VMEM((2, 4 * rows, depth), jnp.bfloat16),
+            pltpu.VMEM((2, 2 * units, size), jnp.bfloat16),
             pltpu.SemaphoreType.DMA((8,)),
             pltpu.SemaphoreType.DMA((6,)),
         ],
         room=16,
-    )(place, ours, theirs, own, given, near, crossed)
+    )(place, *hidden, own, given, near, crossed)
 
 
 def final_kernel(place, first, second, keep, other, bias, *refs):
@@ -357,9 +360,10 @@
         out[...] = jnp.zeros_like(out)
 
     def write(is_first):
-        spare = 2 * CHUNK - columns
-        for j in range(2):
-            lanes = slice(j * CHUNK, (j + 1) * CHUNK)
+        spare = sum(CHUNKS) - columns
+        at = 0
+        for j, size in enumerate(CHUNKS):
+            lanes = slice(at, at + size)
             own, *others = parts[4 * j : 4 * j + 4]
             total = own[...]
             for part in others:
@@ -369,11 +373,12 @@
             total = total + residual.astype(jnp.float32)
             total = (total + bias[:, lanes]).astype(jnp.bfloat16).T
             if is_first and j == 1:
-                total = total[: CHUNK - spare]
+                total = total[: size - spare]
             if not is_first and j == 0:
                 total = total[spare:]
-            at = j * CHUNK if is_first or j == 0 else CHUNK - spare
-            out[at : at + total.shape[0], :] = total
+            to = at if is_first or j == 0 else at - spare
+            out[to : to + total.shape[0], :] = total
+            at += size
 
     for side in range(2):
         pl.when((left == 0) & (core == side))(lambda side=side: write(side == 0))
@@ -411,43 +416,60 @@
     half = units // 2
     columns = width // 2
 
-    window = 2 * CHUNK
+    window = sum(CHUNKS)
     spare = window - columns
     up_own = up_weight.T
     down_own = down_weight.T
     up_half = lax.dynamic_slice_in_dim(up_own, plane * half, half, 0)
     cross_a = swap(up_half, "sec", 4)
     mine, keep, lend = lead(
-        place, window, patch_tokens[0], skip_features[0], skip_weight, norm_gain, norm_bias
+        place,
+        window,
+        patch_tokens[0],
+        skip_features[0],
+        skip_weight,
+        norm_gain,
+        norm_bias,
     )
     tok_z = swap(mine, "sec", 2)
     tok_x = swap(mine, "sec", 1)
     given = swap(give(place, down_own, window), "tp", 1)
-    message_0, message_1 = messages(after(place, mine), down_own, given)
+    message_0, message_1 = messages(after(place, tok_z), down_own, given)
     bias_own = up_bias.reshape(1, units)
     bias_far = swap(bias_own, "sec", 4)
     near_0 = swap(message_0, "sec", 4)
-    near_1 = swap(message_1, "sec", 4)
+    near_1 = swap(after(message_1, tok_x), "sec", 4)
+    cross_b = swap(after(cross_a, mine), "rep", 1)
     tok_d = swap(tok_z, "sec", 1)
+    pair_own = swap(mine, "tp", 1)
     pair_x = swap(tok_x, "tp", 1)
     pair_z = swap(tok_z, "tp", 1)
-    pair_own = swap(mine, "tp", 1)
     pair_keep = swap(lend, "tp", 1)
+    crossed_0 = swap(after(near_0, cross_a), "rep", 1)
+    crossed_1 = swap(near_1, "rep", 1)
     pair_d = swap(after(tok_d, near_0), "tp", 1)
-    cross_b = swap(after(cross_a, message_0), "rep", 1)
-    crossed_0 = swap(near_0, "rep", 1)
-    crossed_1 = swap(near_1, "rep", 1)
     bias_far = jnp.where(
         plane == 0, bias_far, jnp.concatenate([bias_far[:, half:], bias_far[:, :half]], axis=1)
     )
     tokens = (mine, pair_own, tok_x, pair_x, tok_z, pair_z, tok_d, pair_d)
-    ours = hidden_of(place, tokens, (up_own, cross_a, cross_b), (bias_own, bias_far))
-    theirs = swap(after(ours, near_1, crossed_0), "tp", 1)
-    sums_0 = down(0, place, ours, theirs, down_own, given, near_0, crossed_0)
-    sums_1 = down(1, after(place, sums_0[0]), ours, theirs, down_own, given, near_1, crossed_1)
-    parts = []
-    for own, *sent in (sums_0, sums_1):
-        parts += [own, *(swap(part, "sec", mask) for mask, part in enumerate(sent, 1))]
+    ups, biases = (up_own, cross_a, cross_b), (bias_own, bias_far)
+    per = 8 // 2
+    hidden = ()
+    for at in range(0, 8, per):
+        ours = hidden_of(after(place, *hidden[:1]), tokens[at : at + per], ups, biases)
+        if at + per == 8:
+            ours = after(ours, near_1, crossed_0)
+        hidden += (ours, swap(ours, "tp", 1))
+    rows = 2 * mine.shape[0]
+    own_0, *sent = down(
+        0, place, hidden, down_own, given, near_0, crossed_0, rows
+    )
+    got_0 = [swap(part, "sec", mask) for mask, part in enumerate(sent, 1)]
+    own_1, *sent = down(
+        CHUNKS[0], after(place, got_0[0], got_0[1]), hidden, down_own, given, near_1, crossed_1, rows
+    )
+    got_1 = [swap(part, "sec", mask) for mask, part in enumerate(sent, 1)]
+    parts = [own_0, *got_0, own_1, *got_1]
     shift = jnp.where(
         core == 0, jnp.pad(down_bias, (0, spare)), jnp.pad(down_bias, (spare, 0))
     ).reshape(1, window)

time: 83.4 us -> 83.9 us (level)
  starting transfers between devices: 24 us -> 21.5 us
  waiting for transfers between devices: 33.1 us -> 35.3 us
  Pallas kernels: 23 us -> 23.9 us
    ppermute x23 -> x24, starting transfers between devices: 24 us -> 21.5 us  [swap(): return lax.ppermute(values, axis, [(i, i ^ mask) for i in range(size)])]
    ppermute x23 -> x24, waiting for transfers between devices: 33.1 us -> 35.3 us  [swap(): return lax.ppermute(values, axis, [(i, i ^ mask) for i in range(size)])]
    pallas_call x1 -> x2, Pallas kernels: 4.95 us -> 5.96 us  [hidden_of(): call(hidden_kernel, jax.ShapeDtypeStruct(out, jnp.bfloat16), [ANY] * (len...]
  transfers between devices with their start and end apart: 23 -> 24, of which waited for: 14 -> 10; matrix products, arithmetic and copies ran while one was open for 0% -> 0% of each run, Pallas kernels for 19% -> 16%
where the time goes in v4:
time: 83.9 us; the launch traced here: 83.6 us
  waiting for transfers between devices  35.3 us (42%)
  Pallas kernels  23.9 us (28%)
  starting transfers between devices  21.5 us (26%)
  local copies, waits for them, and re-layouts  1.87 us (2%)
    ppermute x24, waiting for transfers between devices, swap(): return lax.ppermute(values, axis, [(i, i ^ mask) for i in range(size)])  35.3 us
    ppermute x24, starting transfers between devices, swap(): return lax.ppermute(values, axis, [(i, i ^ mask) for i in range(size)])  21.5 us
    pallas_call x2, Pallas kernels, down(): call(lambda *refs: down_kernel(at, count, *refs), [jax.ShapeDtypeStruct((...  6.03 us
    pallas_call x2, Pallas kernels, hidden_of(): call(hidden_kernel, jax.ShapeDtypeStruct(out, jnp.bfloat16), [ANY] * (len...  5.96 us
    pallas_call x1, Pallas kernels, lead(): call(lead_kernel, [jax.ShapeDtypeStruct((rows, size), jnp.bfloat16) for s...  5.02 us
    pallas_call x1, Pallas kernels, messages(): call(message_kernel, [jax.ShapeDtypeStruct((units, size), jnp.bfloat16) f...  2.4 us
    pallas_call x1, Pallas kernels, give(): call(give_kernel, jax.ShapeDtypeStruct((units, window), jnp.bfloat16), [A...  2.38 us
    pallas_call x1, Pallas kernels, final(): call(final_kernel, jax.ShapeDtypeStruct((columns, rows), jnp.bfloat16), [...  2.15 us
  transfers between devices with their start and end apart: 24, of which 10 were waited for; matrix products, arithmetic and copies ran while one was open for 0% of the time, Pallas kernels for 16%

profile of v4, /device:TPU:0, one launch (start us, length us, event | category | flops | bytes accessed | tf_op | source)
XLA Modules:
  0.0 83.6 jit_solution(11547278905466289988)
XLA Ops:
  0.0 0.6 pad_add_fusion.place.refs_0_
  0.6 5.0 %shard_map.109 = (bf16[128,1408]{1,0:T(8,128)(2,1)}, bf16[128,768]{1,0:T(8,128)(2,1)}, bf16[128,768]{1,0:T(8,128)(2,1)}) custom-call(s32[3]{0:T(128)} %pad_add_fusion.place.refs_0_, bf16[256,1408]{1,0:T(8,128)(2,1)} %bitcast.18, bf16[256,1024]{1,0:T(8,128)(2,1)} %bitcast.19, bf16[1024,1408]{1,0:T(8,128)(2,1)} %weight.1, f32[1408]{0:T(1024)} %gain.1, f32[1408]{0:T(1024)} %shift.1), custom_call_target="tpu_custom_call" | custom-call | flops 1000 | bytes 1000 | tf_op jit(solution)/shard_map/pallas_call | solution.py:157
  5.7 3.1 %collective-permute-start.8 = (bf16[128,1408]{1,0:T(8,128)(2,1)}, bf16[128,1408]{1,0:T(8,128)(2,1)S(1)}, u32[]{:S(2)}, u32[]{:S(2)}) collective-permute-start(bf16[128,1408]{1,0:T(8,128)(2,1)} %get-tuple-element.28.refs_0_), channel_id=1, source_target_pairs={{0,4},{2,6},{4,0},{6,2},{8,12},{10,14},{12,8},{14,10},{1,5},{3,7},... | collective-permute-start | bytes 1081352 | tf_op jit(solution)/shard_map/ppermute | solution.py:16
  8.7 2.4 %shard_map.111 = bf16[224,768]{1,0:T(8,128)(2,1)} custom-call(s32[3]{0:T(128)} %pad_add_fusion.place.refs_0_, bf16[224,1408]{1,0:T(8,128)(2,1)} %bitcast.12), custom_call_target="tpu_custom_call" | custom-call | flops 1000 | bytes 1000 | tf_op jit(solution)/shard_map/pallas_call | solution.py:60
  11.1 0.1 collective-permute-start.11
  11.3 2.7 %collective-permute-start.4 = (bf16[112,1408]{1,0:T(8,128)(2,1)S(1)}, bf16[112,1408]{1,0:T(8,128)(2,1)S(1)}, u32[]{:S(2)}, u32[]{:S(2)}) collective-permute-start(bf16[112,1408]{1,0:T(8,128)(2,1)S(1)} %dynamic-slice_bitcast_fusion), channel_id=1, source_target_pairs={{0,8},{2,10},{4,12},{6,14},{8,0},{10,2},{12,4},{14,6},{1,9},{3,11}... | collective-permute-start | bytes 946184 | tf_op jit(solution)/shard_map/ppermute | solution.py:16
  13.9 1.5 %collective-permute-start.2 = (bf16[128,1408]{1,0:T(8,128)(2,1)}, bf16[128,1408]{1,0:T(8,128)(2,1)S(1)}, u32[]{:S(2)}, u32[]{:S(2)}) collective-permute-start(bf16[128,1408]{1,0:T(8,128)(2,1)} %get-tuple-element.28.refs_0_), channel_id=1, source_target_pairs={{0,2},{2,0},{4,6},{6,4},{8,10},{10,8},{12,14},{14,12},{1,3},{3,1},... | collective-permute-start | bytes 1081352 | tf_op jit(solution)/shard_map/ppermute | solution.py:16
  15.4 6.3 %collective-permute-done.8.refs_0_ = bf16[128,1408]{1,0:T(8,128)(2,1)S(1)} collective-permute-done((bf16[128,1408]{1,0:T(8,128)(2,1)}, bf16[128,1408]{1,0:T(8,128)(2,1)S(1)}, u32[]{:S(2)}, u32[]{:S(2)}) %collective-permute-start.8) | collective-permute-done | bytes 360480 | tf_op jit(solution)/shard_map/ppermute | solution.py:16
  21.7 1.6 %collective-permute-start.10 = (bf16[128,1408]{1,0:T(8,128)(2,1)S(1)}, bf16[128,1408]{1,0:T(8,128)(2,1)S(1)}, u32[]{:S(2)}, u32[]{:S(2)}) collective-permute-start(bf16[128,1408]{1,0:T(8,128)(2,1)S(1)} %collective-permute-done.8.refs_0_), channel_id=1, source_target_pairs={{0,2},{2,0},{4,6},{6,4},{8,10},{10,8},{12,14},{14,12},{1,3},{3,1},... | collective-permute-start | bytes 1081352 | tf_op jit(solution)/shard_map/ppermute | solution.py:16
  23.3 0.0 collective-permute-start.1
  23.3 0.0 collective-permute-done.11.given.refs_6_
  23.3 0.7 copy-done.2
  24.1 2.4 %shard_map.112 = (bf16[224,512]{1,0:T(8,128)(2,1)}, bf16[224,256]{1,0:T(8,128)(2,1)}) custom-call(s32[3]{0:T(128)} %pad_add_fusion.place.refs_0_, bf16[224,1408]{1,0:T(8,128)(2,1)} %bitcast.13, bf16[224,768]{1,0:T(8,128)(2,1)} %copy-done.2), custom_call_target="tpu_custom_call" | custom-call | flops 1000 | bytes 1000 | tf_op jit(solution)/shard_map/pallas_call | solution.py:92
  26.5 0.7 collective-permute-start.12
  27.2 1.6 %collective-permute-done.4.refs_5_ = bf16[112,1408]{1,0:T(8,128)(2,1)S(1)} collective-permute-done((bf16[112,1408]{1,0:T(8,128)(2,1)S(1)}, bf16[112,1408]{1,0:T(8,128)(2,1)S(1)}, u32[]{:S(2)}, u32[]{:S(2)}) %collective-permute-start.4) | collective-permute-done | bytes 315424 | tf_op jit(solution)/shard_map/ppermute | solution.py:16
  28.9 1.5 %collective-permute-start.5 = (bf16[112,1408]{1,0:T(8,128)(2,1)S(1)}, bf16[112,1408]{1,0:T(8,128)(2,1)S(1)}, u32[]{:S(2)}, u32[]{:S(2)}) collective-permute-start(bf16[112,1408]{1,0:T(8,128)(2,1)S(1)} %collective-permute-done.4.refs_5_), channel_id=1, source_target_pairs={{0,16},{16,0},{1,17},{17,1},{2,18},{18,2},{3,19},{19,3},{4,20},{20... | collective-permute-start | bytes 946184 | tf_op jit(solution)/shard_map/ppermute | solution.py:16
  30.4 10.0 %collective-permute-done.12.refs_7_ = bf16[224,512]{1,0:T(8,128)(2,1)S(1)} collective-permute-done((bf16[224,512]{1,0:T(8,128)(2,1)}, bf16[224,512]{1,0:T(8,128)(2,1)S(1)}, u32[]{:S(2)}, u32[]{:S(2)}) %collective-permute-start.12) | collective-permute-done | bytes 229408 | tf_op jit(solution)/shard_map/ppermute | solution.py:16
  40.4 0.0 collective-permute-start.6
  40.4 0.0 collective-permute-done.2.refs_2_
  40.4 0.1 collective-permute-start.9
  40.5 0.0 collective-permute-done.10.refs_2_
  40.5 0.4 collective-permute-start.3
  40.9 3.9 %collective-permute-done.6 = bf16[1,224]{1,0:T(2,128)(2,1)S(1)} collective-permute-done((bf16[1,224]{1,0:T(2,128)(2,1)S(1)}, bf16[1,224]{1,0:T(2,128)(2,1)S(1)}, u32[]{:S(2)}, u32[]{:S(2)}) %collective-permute-start.6) | collective-permute-done | bytes 480 | tf_op jit(solution)/shard_map/ppermute | solution.py:16
  44.9 1.5 %collective-permute-start.15 = (bf16[224,512]{1,0:T(8,128)(2,1)S(1)}, bf16[224,512]{1,0:T(8,128)(2,1)S(1)}, u32[]{:S(2)}, u32[]{:S(2)}) collective-permute-start(bf16[224,512]{1,0:T(8,128)(2,1)S(1)} %collective-permute-done.12.refs_7_), channel_id=1, source_target_pairs={{0,16},{16,0},{1,17},{17,1},{2,18},{18,2},{3,19},{19,3},{4,20},{20... | collective-permute-start | bytes 688136 | tf_op jit(solution)/shard_map/ppermute | solution.py:16
  46.4 0.0 collective-permute-done.1.refs_1_
  46.4 0.0 collective-permute-start.13
  46.4 0.1 fusion
  46.5 0.0 collective-permute-done.5.refs_6_
  46.5 0.0 collective-permute-start.14
  46.5 0.1 broadcast_select_fusion.refs_8_
  46.6 0.0 collective-permute-done.3.refs_3_
  46.6 1.0 %copy-done.4 = bf16[128,1408]{1,0:T(8,128)(2,1)S(1)} copy-done((bf16[128,1408]{1,0:T(8,128)(2,1)S(1)}, bf16[128,1408]{1,0:T(8,128)(2,1)}, u32[]{:S(2)}) %copy-start.4) | copy-done | bytes 360472
  47.6 3.0 %shard_map.110.refs_1_ = bf16[512,512]{1,0:T(8,128)(2,1)S(1)} custom-call(s32[3]{0:T(128)S(1)} %copy-done.6, bf16[128,1408]{1,0:T(8,128)(2,1)S(1)} %copy-done.4, bf16[128,1408]{1,0:T(8,128)(2,1)S(1)} %collective-permute-done.1.refs_1_, bf16[128,1408]{1,0:T(8,128)(2,1)S(1)} %collective-permute-done.2.refs_2_, ...), custom_call_target="tpu_custom_call" | custom-call | flops 1000 | bytes 1000 | tf_op jit(solution)/shard_map/pallas_call | solution.py:267
  50.6 0.6 collective-permute-start.7
  51.1 0.0 collective-permute-done.9.refs_1_
  51.2 0.0 collective-permute-done.13.refs_3_
  51.2 3.0 %shard_map.113.refs_3_ = bf16[512,512]{1,0:T(8,128)(2,1)S(1)} custom-call(s32[3]{0:T(128)S(1)} %copy-done.6, bf16[128,1408]{1,0:T(8,128)(2,1)S(1)} %collective-permute-done.8.refs_0_, bf16[128,1408]{1,0:T(8,128)(2,1)S(1)} %collective-permute-done.9.refs_1_, bf16[128,1408]{1,0:T(8,128)(2,1)S(1)} %collective-permute-done.10.refs_2_, ...), custom_call_target="tpu_custom_call" | custom-call | flops 1000 | bytes 1000 | tf_op jit(solution)/shard_map/pallas_call | solution.py:267
  54.1 0.0 copy-start.9
  54.2 0.0 copy-start.7
  54.2 0.0 copy-start.8
  54.2 0.5 collective-permute-done.14.refs_7_
  54.7 0.0 collective-permute-done.15.refs_8_
  54.7 0.1 collective-permute-start.16
  54.8 0.0 collective-permute-done.7.refs_2_
  54.8 1.8 %collective-permute-done.16.refs_4_ = bf16[512,512]{1,0:T(8,128)(2,1)S(1)} collective-permute-done((bf16[512,512]{1,0:T(8,128)(2,1)S(1)}, bf16[512,512]{1,0:T(8,128)(2,1)S(1)}, u32[]{:S(2)}, u32[]{:S(2)}) %collective-permute-start.16) | collective-permute-done | bytes 524320 | tf_op jit(solution)/shard_map/ppermute | solution.py:16
  56.6 3.2 %shard_map.114 = (f32[256,512]{1,0:T(8,128)S(1)}, bf16[256,512]{1,0:T(8,128)(2,1)S(1)}, bf16[256,512]{1,0:T(8,128)(2,1)S(1)}, bf16[256,512]{1,0:T(8,128)(2,1)S(1)}) custom-call(s32[3]{0:T(128)S(1)} %copy-done.6, bf16[512,512]{1,0:T(8,128)(2,1)S(1)} %shard_map.110.refs_1_, bf16[512,512]{1,0:T(8,128)(2,1)S(1)} %collective-permute-done.7.refs_2_, ...), custom_call_target="tpu_custom_call" | custom-call | flops 1000 | bytes 1000 | tf_op jit(solution)/shard_map/pallas_call | solution.py:332
  59.8 0.6 collective-permute-start.17
  60.4 1.6 %collective-permute-start.18 = (bf16[256,512]{1,0:T(8,128)(2,1)S(1)}, bf16[256,512]{1,0:T(8,128)(2,1)S(1)}, u32[]{:S(2)}, u32[]{:S(2)}) collective-permute-start(bf16[256,512]{1,0:T(8,128)(2,1)S(1)} %get-tuple-element.40), channel_id=1, source_target_pairs={{0,4},{2,6},{4,0},{6,2},{8,12},{10,14},{12,8},{14,10},{1,5},{3,7},... | collective-permute-start | bytes 786440 | tf_op jit(solution)/shard_map/ppermute | solution.py:16
  62.0 1.4 %collective-permute-start.19 = (bf16[256,512]{1,0:T(8,128)(2,1)S(1)}, bf16[256,512]{1,0:T(8,128)(2,1)S(1)}, u32[]{:S(2)}, u32[]{:S(2)}) collective-permute-start(bf16[256,512]{1,0:T(8,128)(2,1)S(1)} %get-tuple-element.41), channel_id=1, source_target_pairs={{0,6},{2,4},{4,2},{6,0},{8,14},{10,12},{12,10},{14,8},{1,7},{3,5},... | collective-permute-start | bytes 786440 | tf_op jit(solution)/shard_map/ppermute | solution.py:16
  63.4 0.5 collective-permute-start.20
  63.9 0.0 collective-permute-start
  63.9 4.3 %collective-permute-done.17.refs_1_ = bf16[256,512]{1,0:T(8,128)(2,1)S(1)} collective-permute-done((bf16[256,512]{1,0:T(8,128)(2,1)S(1)}, bf16[256,512]{1,0:T(8,128)(2,1)S(1)}, u32[]{:S(2)}, u32[]{:S(2)}) %collective-permute-start.17) | collective-permute-done | bytes 262176 | tf_op jit(solution)/shard_map/ppermute | solution.py:16
  68.2 1.4 %collective-permute-done.18.refs_2_ = bf16[256,512]{1,0:T(8,128)(2,1)S(1)} collective-permute-done((bf16[256,512]{1,0:T(8,128)(2,1)S(1)}, bf16[256,512]{1,0:T(8,128)(2,1)S(1)}, u32[]{:S(2)}, u32[]{:S(2)}) %collective-permute-start.18) | collective-permute-done | bytes 262176 | tf_op jit(solution)/shard_map/ppermute | solution.py:16
  69.6 0.0 collective-permute-done.20.refs_8_
  69.6 2.8 %shard_map.115 = (f32[256,256]{1,0:T(8,128)S(1)}, bf16[256,256]{1,0:T(8,128)(2,1)S(1)}, bf16[256,256]{1,0:T(8,128)(2,1)S(1)}, bf16[256,256]{1,0:T(8,128)(2,1)S(1)}) custom-call(s32[3]{0:T(128)S(1)} %copy-done.6, bf16[512,512]{1,0:T(8,128)(2,1)S(1)} %shard_map.110.refs_1_, bf16[512,512]{1,0:T(8,128)(2,1)S(1)} %collective-permute-done.7.refs_2_, ...), custom_call_target="tpu_custom_call" | custom-call | flops 1000 | bytes 1000 | tf_op jit(solution)/shard_map/pallas_call | solution.py:332
  72.5 1.6 %collective-permute-start.21 = (bf16[256,256]{1,0:T(8,128)(2,1)S(1)}, bf16[256,256]{1,0:T(8,128)(2,1)S(1)}, u32[]{:S(2)}, u32[]{:S(2)}) collective-permute-start(bf16[256,256]{1,0:T(8,128)(2,1)S(1)} %get-tuple-element.44), channel_id=1, source_target_pairs={{0,2},{2,0},{4,6},{6,4},{8,10},{10,8},{12,14},{14,12},{1,3},{3,1},... | collective-permute-start | bytes 393224 | tf_op jit(solution)/shard_map/ppermute | solution.py:16
  74.0 1.5 %collective-permute-start.22 = (bf16[256,256]{1,0:T(8,128)(2,1)S(1)}, bf16[256,256]{1,0:T(8,128)(2,1)S(1)}, u32[]{:S(2)}, u32[]{:S(2)}) collective-permute-start(bf16[256,256]{1,0:T(8,128)(2,1)S(1)} %get-tuple-element.45), channel_id=1, source_target_pairs={{0,4},{2,6},{4,0},{6,2},{8,12},{10,14},{12,8},{14,10},{1,5},{3,7},... | collective-permute-start | bytes 393224 | tf_op jit(solution)/shard_map/ppermute | solution.py:16
  75.6 0.5 collective-permute-start.23
  76.0 0.1 pad_select_fusion
  76.1 0.0 collective-permute-done.other
  76.1 3.1 %collective-permute-done.21.refs_5_ = bf16[256,256]{1,0:T(8,128)(2,1)S(1)} collective-permute-done((bf16[256,256]{1,0:T(8,128)(2,1)S(1)}, bf16[256,256]{1,0:T(8,128)(2,1)S(1)}, u32[]{:S(2)}, u32[]{:S(2)}) %collective-permute-start.21) | collective-permute-done | bytes 131104 | tf_op jit(solution)/shard_map/ppermute | solution.py:16
  79.3 0.0 collective-permute-done.22.refs_6_
  79.3 2.2 %collective-permute-done.23.refs_7_ = bf16[256,256]{1,0:T(8,128)(2,1)S(1)} collective-permute-done((bf16[256,256]{1,0:T(8,128)(2,1)S(1)}, bf16[256,256]{1,0:T(8,128)(2,1)S(1)}, u32[]{:S(2)}, u32[]{:S(2)}) %collective-permute-start.23) | collective-permute-done | bytes 131104 | tf_op jit(solution)/shard_map/ppermute | solution.py:16
  81.4 2.1 %shard_map.116 = bf16[704,256]{1,0:T(8,128)(2,1)} custom-call(s32[3]{0:T(128)S(1)} %copy-done.6, s32[2]{0:T(128)S(1)} %copy-done.7, s32[2]{0:T(128)S(1)} %copy-done.8, bf16[128,768]{1,0:T(8,128)(2,1)S(1)} %copy-done.5, bf16[128,768]{1,0:T(8,128)(2,1)S(1)} %collective-permute-done.other, f32[1,768]{1,0:T(1,128)S(1)} %reshape.6.bias, ...), custom_call_target="tpu_custom_call" | custom-call | flops 1000 | bytes 1000 | tf_op jit(solution)/shard_map/pallas_call | solution.py:390
  (23 shorter events, 0.1 us)
Async XLA Ops:
  0.0 11.2 %copy-start.1 = (bf16[1408,224]{0,1:T(8,128)(2,1)S(1)}, bf16[1408,224]{0,1:T(8,128)(2,1)}, u32[]{:S(2)}) copy-start(bf16[1408,224]{0,1:T(8,128)(2,1)} %param.18) | copy-start | bytes 1892356
  0.6 29.8 %copy-start.11 = (bf16[224]{0:T(256)(128)(2,1)S(1)}, bf16[224]{0:T(256)(128)(2,1)}, u32[]{:S(2)}) copy-start(bf16[224]{0:T(256)(128)(2,1)} %param.19) | copy-start | bytes 1348
  0.6 46.0 %copy-start.6 = (s32[3]{0:T(128)S(1)}, s32[3]{0:T(128)}, u32[]{:S(2)}) copy-start(s32[3]{0:T(128)} %pad_add_fusion.place.refs_0_) | copy-start | bytes 40
  5.7 16.0 %collective-permute-start.8 = (bf16[128,1408]{1,0:T(8,128)(2,1)}, bf16[128,1408]{1,0:T(8,128)(2,1)S(1)}, u32[]{:S(2)}, u32[]{:S(2)}) collective-permute-start(bf16[128,1408]{1,0:T(8,128)(2,1)} %get-tuple-element.28.refs_0_), channel_id=1, source_target_pairs={{0,4},{2,6},{4,0},{6,2},{8,12},{10,14},{12,8},{14,10},{1,5},{3,7},... | collective-permute-start | bytes 1081352 | tf_op jit(solution)/shard_map/ppermute | solution.py:16
  11.1 12.2 %collective-permute-start.11 = (bf16[224,768]{1,0:T(8,128)(2,1)}, bf16[224,768]{1,0:T(8,128)(2,1)S(1)}, u32[]{:S(2)}, u32[]{:S(2)}) collective-permute-start(bf16[224,768]{1,0:T(8,128)(2,1)} %shard_map.111), channel_id=1, source_target_pairs={{0,1},{1,0},{2,3},{3,2},{4,5},{5,4},{6,7},{7,6},{8,9},{9,8},{10,11... | collective-permute-start | bytes 1032200 | tf_op jit(solution)/shard_map/ppermute | solution.py:16
  11.3 17.6 %collective-permute-start.4 = (bf16[112,1408]{1,0:T(8,128)(2,1)S(1)}, bf16[112,1408]{1,0:T(8,128)(2,1)S(1)}, u32[]{:S(2)}, u32[]{:S(2)}) collective-permute-start(bf16[112,1408]{1,0:T(8,128)(2,1)S(1)} %dynamic-slice_bitcast_fusion), channel_id=1, source_target_pairs={{0,8},{2,10},{4,12},{6,14},{8,0},{10,2},{12,4},{14,6},{1,9},{3,11}... | collective-permute-start | bytes 946184 | tf_op jit(solution)/shard_map/ppermute | solution.py:16
  13.9 26.5 %collective-permute-start.2 = (bf16[128,1408]{1,0:T(8,128)(2,1)}, bf16[128,1408]{1,0:T(8,128)(2,1)S(1)}, u32[]{:S(2)}, u32[]{:S(2)}) collective-permute-start(bf16[128,1408]{1,0:T(8,128)(2,1)} %get-tuple-element.28.refs_0_), channel_id=1, source_target_pairs={{0,2},{2,0},{4,6},{6,4},{8,10},{10,8},{12,14},{14,12},{1,3},{3,1},... | collective-permute-start | bytes 1081352 | tf_op jit(solution)/shard_map/ppermute | solution.py:16
  21.7 18.8 %collective-permute-start.10 = (bf16[128,1408]{1,0:T(8,128)(2,1)S(1)}, bf16[128,1408]{1,0:T(8,128)(2,1)S(1)}, u32[]{:S(2)}, u32[]{:S(2)}) collective-permute-start(bf16[128,1408]{1,0:T(8,128)(2,1)S(1)} %collective-permute-done.8.refs_0_), channel_id=1, source_target_pairs={{0,2},{2,0},{4,6},{6,4},{8,10},{10,8},{12,14},{14,12},{1,3},{3,1},... | collective-permute-start | bytes 1081352 | tf_op jit(solution)/shard_map/ppermute | solution.py:16
  23.3 23.1 %collective-permute-start.1 = (bf16[128,1408]{1,0:T(8,128)(2,1)}, bf16[128,1408]{1,0:T(8,128)(2,1)S(1)}, u32[]{:S(2)}, u32[]{:S(2)}) collective-permute-start(bf16[128,1408]{1,0:T(8,128)(2,1)} %get-tuple-element.28.refs_0_), channel_id=1, source_target_pairs={{0,1},{1,0},{2,3},{3,2},{4,5},{5,4},{6,7},{7,6},{8,9},{9,8},{10,11... | collective-permute-start | bytes 1081352 | tf_op jit(solution)/shard_map/ppermute | solution.py:16
  23.3 0.7 copy-start.2
  26.5 13.9 %collective-permute-start.12 = (bf16[224,512]{1,0:T(8,128)(2,1)}, bf16[224,512]{1,0:T(8,128)(2,1)S(1)}, u32[]{:S(2)}, u32[]{:S(2)}) collective-permute-start(bf16[224,512]{1,0:T(8,128)(2,1)} %get-tuple-element.32), channel_id=1, source_target_pairs={{0,8},{2,10},{4,12},{6,14},{8,0},{10,2},{12,4},{14,6},{1,9},{3,11}... | collective-permute-start | bytes 688136 | tf_op jit(solution)/shard_map/ppermute | solution.py:16
  28.9 17.6 %collective-permute-start.5 = (bf16[112,1408]{1,0:T(8,128)(2,1)S(1)}, bf16[112,1408]{1,0:T(8,128)(2,1)S(1)}, u32[]{:S(2)}, u32[]{:S(2)}) collective-permute-start(bf16[112,1408]{1,0:T(8,128)(2,1)S(1)} %collective-permute-done.4.refs_5_), channel_id=1, source_target_pairs={{0,16},{16,0},{1,17},{17,1},{2,18},{18,2},{3,19},{19,3},{4,20},{20... | collective-permute-start | bytes 946184 | tf_op jit(solution)/shard_map/ppermute | solution.py:16
  40.4 4.5 %collective-permute-start.6 = (bf16[1,224]{1,0:T(2,128)(2,1)S(1)}, bf16[1,224]{1,0:T(2,128)(2,1)S(1)}, u32[]{:S(2)}, u32[]{:S(2)}) collective-permute-start(bf16[1,224]{1,0:T(2,128)(2,1)S(1)} %reshape.7.refs_7_), channel_id=1, source_target_pairs={{0,8},{2,10},{4,12},{6,14},{8,0},{10,2},{12,4},{14,6},{1,9},{3,11}... | collective-permute-start | bytes 1352 | tf_op jit(solution)/shard_map/ppermute | solution.py:16
  40.4 10.7 %collective-permute-start.9 = (bf16[128,1408]{1,0:T(8,128)(2,1)S(1)}, bf16[128,1408]{1,0:T(8,128)(2,1)S(1)}, u32[]{:S(2)}, u32[]{:S(2)}) collective-permute-start(bf16[128,1408]{1,0:T(8,128)(2,1)S(1)} %collective-permute-done.8.refs_0_), channel_id=1, source_target_pairs={{0,1},{1,0},{2,3},{3,2},{4,5},{5,4},{6,7},{7,6},{8,9},{9,8},{10,11... | collective-permute-start | bytes 1081352 | tf_op jit(solution)/shard_map/ppermute | solution.py:16
  40.5 6.1 %collective-permute-start.3 = (bf16[128,1408]{1,0:T(8,128)(2,1)S(1)}, bf16[128,1408]{1,0:T(8,128)(2,1)S(1)}, u32[]{:S(2)}, u32[]{:S(2)}) collective-permute-start(bf16[128,1408]{1,0:T(8,128)(2,1)S(1)} %collective-permute-done.2.refs_2_), channel_id=1, source_target_pairs={{0,1},{1,0},{2,3},{3,2},{4,5},{5,4},{6,7},{7,6},{8,9},{9,8},{10,11... | collective-permute-start | bytes 1081352 | tf_op jit(solution)/shard_map/ppermute | solution.py:16
  44.9 9.8 %collective-permute-start.15 = (bf16[224,512]{1,0:T(8,128)(2,1)S(1)}, bf16[224,512]{1,0:T(8,128)(2,1)S(1)}, u32[]{:S(2)}, u32[]{:S(2)}) collective-permute-start(bf16[224,512]{1,0:T(8,128)(2,1)S(1)} %collective-permute-done.12.refs_7_), channel_id=1, source_target_pairs={{0,16},{16,0},{1,17},{17,1},{2,18},{18,2},{3,19},{19,3},{4,20},{20... | collective-permute-start | bytes 688136 | tf_op jit(solution)/shard_map/ppermute | solution.py:16
  46.4 4.7 %collective-permute-start.13 = (bf16[128,1408]{1,0:T(8,128)(2,1)S(1)}, bf16[128,1408]{1,0:T(8,128)(2,1)S(1)}, u32[]{:S(2)}, u32[]{:S(2)}) collective-permute-start(bf16[128,1408]{1,0:T(8,128)(2,1)S(1)} %collective-permute-done.10.refs_2_), channel_id=1, source_target_pairs={{0,1},{1,0},{2,3},{3,2},{4,5},{5,4},{6,7},{7,6},{8,9},{9,8},{10,11... | collective-permute-start | bytes 1081352 | tf_op jit(solution)/shard_map/ppermute | solution.py:16
  46.5 8.2 %collective-permute-start.14 = (bf16[224,256]{1,0:T(8,128)(2,1)}, bf16[224,256]{1,0:T(8,128)(2,1)S(1)}, u32[]{:S(2)}, u32[]{:S(2)}) collective-permute-start(bf16[224,256]{1,0:T(8,128)(2,1)} %get-tuple-element.35), channel_id=1, source_target_pairs={{0,8},{2,10},{4,12},{6,14},{8,0},{10,2},{12,4},{14,6},{1,9},{3,11}... | collective-permute-start | bytes 344072 | tf_op jit(solution)/shard_map/ppermute | solution.py:16
  46.6 1.0 %copy-start.4 = (bf16[128,1408]{1,0:T(8,128)(2,1)S(1)}, bf16[128,1408]{1,0:T(8,128)(2,1)}, u32[]{:S(2)}) copy-start(bf16[128,1408]{1,0:T(8,128)(2,1)} %get-tuple-element.28.refs_0_) | copy-start | bytes 1081348
  47.6 9.0 %copy-start = (bf16[1408,224]{0,1:T(8,128)(2,1)S(1)}, bf16[1408,224]{0,1:T(8,128)(2,1)}, u32[]{:S(2)}) copy-start(bf16[1408,224]{0,1:T(8,128)(2,1)} %param.20) | copy-start | bytes 1892356
  47.6 9.0 %copy-start.3 = (bf16[224,768]{1,0:T(8,128)(2,1)S(1)}, bf16[224,768]{1,0:T(8,128)(2,1)}, u32[]{:S(2)}) copy-start(bf16[224,768]{1,0:T(8,128)(2,1)} %copy-done.2) | copy-start | bytes 1032196
  50.6 13.3 %copy-start.10 = (bf16[128,768]{1,0:T(8,128)(2,1)S(1)}, bf16[128,768]{1,0:T(8,128)(2,1)}, u32[]{:S(2)}) copy-start(bf16[128,768]{1,0:T(8,128)(2,1)} %get-tuple-element.27) | copy-start | bytes 589828
  50.6 4.2 %collective-permute-start.7 = (bf16[512,512]{1,0:T(8,128)(2,1)S(1)}, bf16[512,512]{1,0:T(8,128)(2,1)S(1)}, u32[]{:S(2)}, u32[]{:S(2)}) collective-permute-start(bf16[512,512]{1,0:T(8,128)(2,1)S(1)} %shard_map.110.refs_1_), channel_id=1, source_target_pairs={{0,1},{1,0},{2,3},{3,2},{4,5},{5,4},{6,7},{7,6},{8,9},{9,8},{10,11... | collective-permute-start | bytes 1572872 | tf_op jit(solution)/shard_map/ppermute | solution.py:16
  54.1 21.9 %copy-start.9 = (f32[704]{0:T(1024)S(1)}, f32[704]{0:T(1024)}, u32[]{:S(2)}) copy-start(f32[704]{0:T(1024)} %param.21) | copy-start | bytes 8452
  54.2 27.3 %copy-start.5 = (bf16[128,768]{1,0:T(8,128)(2,1)S(1)}, bf16[128,768]{1,0:T(8,128)(2,1)}, u32[]{:S(2)}) copy-start(bf16[128,768]{1,0:T(8,128)(2,1)} %get-tuple-element.26.keep) | copy-start | bytes 589828
  54.2 27.3 %copy-start.7 = (s32[2]{0:T(128)S(1)}, s32[2]{0:T(128)}, u32[]{:S(2)}) copy-start(s32[2]{0:T(128)} %first.1) | copy-start | bytes 28
  54.2 27.3 %copy-start.8 = (s32[2]{0:T(128)S(1)}, s32[2]{0:T(128)}, u32[]{:S(2)}) copy-start(s32[2]{0:T(128)} %second.1) | copy-start | bytes 28
  54.7 1.9 %collective-permute-start.16 = (bf16[512,512]{1,0:T(8,128)(2,1)S(1)}, bf16[512,512]{1,0:T(8,128)(2,1)S(1)}, u32[]{:S(2)}, u32[]{:S(2)}) collective-permute-start(bf16[512,512]{1,0:T(8,128)(2,1)S(1)} %shard_map.113.refs_3_), channel_id=1, source_target_pairs={{0,1},{1,0},{2,3},{3,2},{4,5},{5,4},{6,7},{7,6},{8,9},{9,8},{10,11... | collective-permute-start | bytes 1572872 | tf_op jit(solution)/shard_map/ppermute | solution.py:16
  59.8 8.4 %collective-permute-start.17 = (bf16[256,512]{1,0:T(8,128)(2,1)S(1)}, bf16[256,512]{1,0:T(8,128)(2,1)S(1)}, u32[]{:S(2)}, u32[]{:S(2)}) collective-permute-start(bf16[256,512]{1,0:T(8,128)(2,1)S(1)} %get-tuple-element.39), channel_id=1, source_target_pairs={{0,2},{2,0},{4,6},{6,4},{8,10},{10,8},{12,14},{14,12},{1,3},{3,1},... | collective-permute-start | bytes 786440 | tf_op jit(solution)/shard_map/ppermute | solution.py:16
  60.4 9.2 %collective-permute-start.18 = (bf16[256,512]{1,0:T(8,128)(2,1)S(1)}, bf16[256,512]{1,0:T(8,128)(2,1)S(1)}, u32[]{:S(2)}, u32[]{:S(2)}) collective-permute-start(bf16[256,512]{1,0:T(8,128)(2,1)S(1)} %get-tuple-element.40), channel_id=1, source_target_pairs={{0,4},{2,6},{4,0},{6,2},{8,12},{10,14},{12,8},{14,10},{1,5},{3,7},... | collective-permute-start | bytes 786440 | tf_op jit(solution)/shard_map/ppermute | solution.py:16
  62.0 14.1 %collective-permute-start.19 = (bf16[256,512]{1,0:T(8,128)(2,1)S(1)}, bf16[256,512]{1,0:T(8,128)(2,1)S(1)}, u32[]{:S(2)}, u32[]{:S(2)}) collective-permute-start(bf16[256,512]{1,0:T(8,128)(2,1)S(1)} %get-tuple-element.41), channel_id=1, source_target_pairs={{0,6},{2,4},{4,2},{6,0},{8,14},{10,12},{12,10},{14,8},{1,7},{3,5},... | collective-permute-start | bytes 786440 | tf_op jit(solution)/shard_map/ppermute | solution.py:16
  63.4 6.2 %collective-permute-start.20 = (bf16[224,256]{1,0:T(8,128)(2,1)S(1)}, bf16[224,256]{1,0:T(8,128)(2,1)S(1)}, u32[]{:S(2)}, u32[]{:S(2)}) collective-permute-start(bf16[224,256]{1,0:T(8,128)(2,1)S(1)} %collective-permute-done.14.refs_7_), channel_id=1, source_target_pairs={{0,16},{16,0},{1,17},{17,1},{2,18},{18,2},{3,19},{19,3},{4,20},{20... | collective-permute-start | bytes 344072 | tf_op jit(solution)/shard_map/ppermute | solution.py:16
  63.9 12.2 %collective-permute-start = (bf16[128,768]{1,0:T(8,128)(2,1)S(1)}, bf16[128,768]{1,0:T(8,128)(2,1)S(1)}, u32[]{:S(2)}, u32[]{:S(2)}) collective-permute-start(bf16[128,768]{1,0:T(8,128)(2,1)S(1)} %copy-done.10), channel_id=1, source_target_pairs={{0,1},{1,0},{2,3},{3,2},{4,5},{5,4},{6,7},{7,6},{8,9},{9,8},{10,11... | collective-permute-start | bytes 589832 | tf_op jit(solution)/shard_map/ppermute | solution.py:16
  72.5 6.8 %collective-permute-start.21 = (bf16[256,256]{1,0:T(8,128)(2,1)S(1)}, bf16[256,256]{1,0:T(8,128)(2,1)S(1)}, u32[]{:S(2)}, u32[]{:S(2)}) collective-permute-start(bf16[256,256]{1,0:T(8,128)(2,1)S(1)} %get-tuple-element.44), channel_id=1, source_target_pairs={{0,2},{2,0},{4,6},{6,4},{8,10},{10,8},{12,14},{14,12},{1,3},{3,1},... | collective-permute-start | bytes 393224 | tf_op jit(solution)/shard_map/ppermute | solution.py:16
  74.0 5.2 %collective-permute-start.22 = (bf16[256,256]{1,0:T(8,128)(2,1)S(1)}, bf16[256,256]{1,0:T(8,128)(2,1)S(1)}, u32[]{:S(2)}, u32[]{:S(2)}) collective-permute-start(bf16[256,256]{1,0:T(8,128)(2,1)S(1)} %get-tuple-element.45), channel_id=1, source_target_pairs={{0,4},{2,6},{4,0},{6,2},{8,12},{10,14},{12,8},{14,10},{1,5},{3,7},... | collective-permute-start | bytes 393224 | tf_op jit(solution)/shard_map/ppermute | solution.py:16
  75.6 5.9 %collective-permute-start.23 = (bf16[256,256]{1,0:T(8,128)(2,1)S(1)}, bf16[256,256]{1,0:T(8,128)(2,1)S(1)}, u32[]{:S(2)}, u32[]{:S(2)}) collective-permute-start(bf16[256,256]{1,0:T(8,128)(2,1)S(1)} %get-tuple-element.46), channel_id=1, source_target_pairs={{0,6},{2,4},{4,2},{6,0},{8,14},{10,12},{12,10},{14,8},{1,7},{3,5},... | collective-permute-start | bytes 393224 | tf_op jit(solution)/shard_map/ppermute | solution.py:16

commit v5 on v4

--- a/solution.py
+++ b/solution.py
@@ -423,7 +423,7 @@
     up_half = lax.dynamic_slice_in_dim(up_own, plane * half, half, 0)
     cross_a = swap(up_half, "sec", 4)
     mine, keep, lend = lead(
-        place,
+        after(place, place),
         window,
         patch_tokens[0],
         skip_features[0],
@@ -433,20 +433,20 @@
     )
     tok_z = swap(mine, "sec", 2)
     tok_x = swap(mine, "sec", 1)
-    given = swap(give(place, down_own, window), "tp", 1)
+    given = swap(give(after(place, place), down_own, window), "tp", 1)
     message_0, message_1 = messages(after(place, tok_z), down_own, given)
     bias_own = up_bias.reshape(1, units)
-    bias_far = swap(bias_own, "sec", 4)
+    bias_far = swap(after(bias_own, bias_own), "sec", 4)
     near_0 = swap(message_0, "sec", 4)
     near_1 = swap(after(message_1, tok_x), "sec", 4)
     cross_b = swap(after(cross_a, mine), "rep", 1)
-    tok_d = swap(tok_z, "sec", 1)
-    pair_own = swap(mine, "tp", 1)
-    pair_x = swap(tok_x, "tp", 1)
-    pair_z = swap(tok_z, "tp", 1)
-    pair_keep = swap(lend, "tp", 1)
+    tok_d = swap(after(tok_z, tok_z), "sec", 1)
+    pair_own = swap(after(mine, mine), "tp", 1)
+    pair_x = swap(after(tok_x, tok_x), "tp", 1)
+    pair_z = swap(after(tok_z, tok_z), "tp", 1)
+    pair_keep = swap(after(lend, lend), "tp", 1)
     crossed_0 = swap(after(near_0, cross_a), "rep", 1)
-    crossed_1 = swap(near_1, "rep", 1)
+    crossed_1 = swap(after(near_1, near_1), "rep", 1)
     pair_d = swap(after(tok_d, near_0), "tp", 1)
     bias_far = jnp.where(
         plane == 0, bias_far, jnp.concatenate([bias_far[:, half:], bias_far[:, :half]], axis=1)
@@ -456,13 +456,13 @@
     per = 8 // 2
     hidden = ()
     for at in range(0, 8, per):
-        ours = hidden_of(after(place, *hidden[:1]), tokens[at : at + per], ups, biases)
+        ours = hidden_of(after(place, place, *hidden[:1]), tokens[at : at + per], ups, biases)
         if at + per == 8:
             ours = after(ours, near_1, crossed_0)
         hidden += (ours, swap(ours, "tp", 1))
     rows = 2 * mine.shape[0]
     own_0, *sent = down(
-        0, place, hidden, down_own, given, near_0, crossed_0, rows
+        0, after(place, place), hidden, down_own, given, near_0, crossed_0, rows
     )
     got_0 = [swap(part, "sec", mask) for mask, part in enumerate(sent, 1)]
     own_1, *sent = down(

time: 83.9 us -> 79.9 us (0.952)
  waiting for transfers between devices: 35.3 us -> 30.5 us
  starting transfers between devices: 21.5 us -> 22.4 us
    ppermute x24, waiting for transfers between devices: 35.3 us -> 30.5 us  [swap(): return lax.ppermute(values, axis, [(i, i ^ mask) for i in range(size)])]
    ppermute x24, starting transfers between devices: 21.5 us -> 22.4 us  [swap(): return lax.ppermute(values, axis, [(i, i ^ mask) for i in range(size)])]
  transfers between devices with their start and end apart: 24 -> 24, of which waited for: 10 -> 9; matrix products, arithmetic and copies ran while one was open for 0% -> 0% of each run, Pallas kernels for 16% -> 17%
where the time goes in v5:
time: 79.9 us; the launch traced here: 79.7 us
  waiting for transfers between devices  30.5 us (38%)
  Pallas kernels  23.9 us (30%)
  starting transfers between devices  22.4 us (28%)
  local copies, waits for them, and re-layouts  1.87 us (2%)
    ppermute x24, waiting for transfers between devices, swap(): return lax.ppermute(values, axis, [(i, i ^ mask) for i in range(size)])  30.5 us
    ppermute x24, starting transfers between devices, swap(): return lax.ppermute(values, axis, [(i, i ^ mask) for i in range(size)])  22.4 us
    pallas_call x2, Pallas kernels, down(): call(lambda *refs: down_kernel(at, count, *refs), [jax.ShapeDtypeStruct((...  6.03 us
    pallas_call x2, Pallas kernels, hidden_of(): call(hidden_kernel, jax.ShapeDtypeStruct(out, jnp.bfloat16), [ANY] * (len...  5.95 us
    pallas_call x1, Pallas kernels, lead(): call(lead_kernel, [jax.ShapeDtypeStruct((rows, size), jnp.bfloat16) for s...  5.02 us
    pallas_call x1, Pallas kernels, messages(): call(message_kernel, [jax.ShapeDtypeStruct((units, size), jnp.bfloat16) f...  2.4 us
    pallas_call x1, Pallas kernels, give(): call(give_kernel, jax.ShapeDtypeStruct((units, window), jnp.bfloat16), [A...  2.38 us
    pallas_call x1, Pallas kernels, final(): call(final_kernel, jax.ShapeDtypeStruct((columns, rows), jnp.bfloat16), [...  2.15 us
  transfers between devices with their start and end apart: 24, of which 9 were waited for; matrix products, arithmetic and copies ran while one was open for 0% of the time, Pallas kernels for 17%

profile of v5, /device:TPU:0, one launch (start us, length us, event | category | flops | bytes accessed | tf_op | source)
XLA Modules:
  0.0 79.7 jit_solution(7888849263019441885)
XLA Ops:
  0.0 0.6 pad_add_fusion.place.refs_0_
  0.6 5.0 %shard_map.109 = (bf16[128,1408]{1,0:T(8,128)(2,1)}, bf16[128,768]{1,0:T(8,128)(2,1)}, bf16[128,768]{1,0:T(8,128)(2,1)}) custom-call(s32[3]{0:T(128)} %pad_add_fusion.place.refs_0_, bf16[256,1408]{1,0:T(8,128)(2,1)} %bitcast.18, bf16[256,1024]{1,0:T(8,128)(2,1)} %bitcast.19, bf16[1024,1408]{1,0:T(8,128)(2,1)} %weight.1, f32[1408]{0:T(1024)} %gain.1, f32[1408]{0:T(1024)} %shift.1), custom_call_target="tpu_custom_call" | custom-call | flops 1000 | bytes 1000 | tf_op jit(solution)/shard_map/pallas_call | solution.py:157
  5.7 3.1 %collective-permute-start.8 = (bf16[128,1408]{1,0:T(8,128)(2,1)}, bf16[128,1408]{1,0:T(8,128)(2,1)S(1)}, u32[]{:S(2)}, u32[]{:S(2)}) collective-permute-start(bf16[128,1408]{1,0:T(8,128)(2,1)} %get-tuple-element.36.refs_0_), channel_id=1, source_target_pairs={{0,4},{2,6},{4,0},{6,2},{8,12},{10,14},{12,8},{14,10},{1,5},{3,7},... | collective-permute-start | bytes 1081352 | tf_op jit(solution)/shard_map/ppermute | solution.py:16
  8.7 2.4 %shard_map.111 = bf16[224,768]{1,0:T(8,128)(2,1)} custom-call(s32[3]{0:T(128)} %pad_add_fusion.place.refs_0_, bf16[224,1408]{1,0:T(8,128)(2,1)} %bitcast.12), custom_call_target="tpu_custom_call" | custom-call | flops 1000 | bytes 1000 | tf_op jit(solution)/shard_map/pallas_call | solution.py:60
  11.1 0.1 collective-permute-start.11
  11.3 2.7 %collective-permute-start.4 = (bf16[112,1408]{1,0:T(8,128)(2,1)S(1)}, bf16[112,1408]{1,0:T(8,128)(2,1)S(1)}, u32[]{:S(2)}, u32[]{:S(2)}) collective-permute-start(bf16[112,1408]{1,0:T(8,128)(2,1)S(1)} %dynamic-slice_bitcast_fusion), channel_id=1, source_target_pairs={{0,8},{2,10},{4,12},{6,14},{8,0},{10,2},{12,4},{14,6},{1,9},{3,11}... | collective-permute-start | bytes 946184 | tf_op jit(solution)/shard_map/ppermute | solution.py:16
  13.9 1.5 %collective-permute-start.2 = (bf16[128,1408]{1,0:T(8,128)(2,1)}, bf16[128,1408]{1,0:T(8,128)(2,1)S(1)}, u32[]{:S(2)}, u32[]{:S(2)}) collective-permute-start(bf16[128,1408]{1,0:T(8,128)(2,1)} %get-tuple-element.36.refs_0_), channel_id=1, source_target_pairs={{0,2},{2,0},{4,6},{6,4},{8,10},{10,8},{12,14},{14,12},{1,3},{3,1},... | collective-permute-start | bytes 1081352 | tf_op jit(solution)/shard_map/ppermute | solution.py:16
  15.4 6.3 %collective-permute-done.8.refs_0_ = bf16[128,1408]{1,0:T(8,128)(2,1)S(1)} collective-permute-done((bf16[128,1408]{1,0:T(8,128)(2,1)}, bf16[128,1408]{1,0:T(8,128)(2,1)S(1)}, u32[]{:S(2)}, u32[]{:S(2)}) %collective-permute-start.8) | collective-permute-done | bytes 360480 | tf_op jit(solution)/shard_map/ppermute | solution.py:16
  21.7 1.6 %collective-permute-start.10 = (bf16[128,1408]{1,0:T(8,128)(2,1)S(1)}, bf16[128,1408]{1,0:T(8,128)(2,1)S(1)}, u32[]{:S(2)}, u32[]{:S(2)}) collective-permute-start(bf16[128,1408]{1,0:T(8,128)(2,1)S(1)} %collective-permute-done.8.refs_0_), channel_id=1, source_target_pairs={{0,2},{2,0},{4,6},{6,4},{8,10},{10,8},{12,14},{14,12},{1,3},{3,1},... | collective-permute-start | bytes 1081352 | tf_op jit(solution)/shard_map/ppermute | solution.py:16
  23.3 0.0 collective-permute-start.1
  23.3 0.0 collective-permute-done.11.given.refs_6_
  23.3 0.7 copy-done.2
  24.1 2.4 %shard_map.112 = (bf16[224,512]{1,0:T(8,128)(2,1)}, bf16[224,256]{1,0:T(8,128)(2,1)}) custom-call(s32[3]{0:T(128)} %pad_add_fusion.place.refs_0_, bf16[224,1408]{1,0:T(8,128)(2,1)} %bitcast.13, bf16[224,768]{1,0:T(8,128)(2,1)} %copy-done.2), custom_call_target="tpu_custom_call" | custom-call | flops 1000 | bytes 1000 | tf_op jit(solution)/shard_map/pallas_call | solution.py:92
  26.5 0.7 collective-permute-start.12
  27.2 1.6 %collective-permute-done.4.refs_5_ = bf16[112,1408]{1,0:T(8,128)(2,1)S(1)} collective-permute-done((bf16[112,1408]{1,0:T(8,128)(2,1)S(1)}, bf16[112,1408]{1,0:T(8,128)(2,1)S(1)}, u32[]{:S(2)}, u32[]{:S(2)}) %collective-permute-start.4) | collective-permute-done | bytes 315424 | tf_op jit(solution)/shard_map/ppermute | solution.py:16
  28.9 1.5 %collective-permute-start.5 = (bf16[112,1408]{1,0:T(8,128)(2,1)S(1)}, bf16[112,1408]{1,0:T(8,128)(2,1)S(1)}, u32[]{:S(2)}, u32[]{:S(2)}) collective-permute-start(bf16[112,1408]{1,0:T(8,128)(2,1)S(1)} %collective-permute-done.4.refs_5_), channel_id=1, source_target_pairs={{0,16},{16,0},{1,17},{17,1},{2,18},{18,2},{3,19},{19,3},{4,20},{20... | collective-permute-start | bytes 946184 | tf_op jit(solution)/shard_map/ppermute | solution.py:16
  30.4 0.0 collective-permute-done.2.refs_2_
  30.4 0.7 collective-permute-start.6
  31.1 9.4 %collective-permute-done.12.refs_7_ = bf16[224,512]{1,0:T(8,128)(2,1)S(1)} collective-permute-done((bf16[224,512]{1,0:T(8,128)(2,1)}, bf16[224,512]{1,0:T(8,128)(2,1)S(1)}, u32[]{:S(2)}, u32[]{:S(2)}) %collective-permute-start.12) | collective-permute-done | bytes 229408 | tf_op jit(solution)/shard_map/ppermute | solution.py:16
  40.5 0.1 collective-permute-start.9
  40.5 0.0 collective-permute-done.10.refs_2_
  40.5 0.5 collective-permute-start.3
  41.0 0.0 collective-permute-done.6
  41.0 1.5 %collective-permute-start.15 = (bf16[224,512]{1,0:T(8,128)(2,1)S(1)}, bf16[224,512]{1,0:T(8,128)(2,1)S(1)}, u32[]{:S(2)}, u32[]{:S(2)}) collective-permute-start(bf16[224,512]{1,0:T(8,128)(2,1)S(1)} %collective-permute-done.12.refs_7_), channel_id=1, source_target_pairs={{0,16},{16,0},{1,17},{17,1},{2,18},{18,2},{3,19},{19,3},{4,20},{20... | collective-permute-start | bytes 688136 | tf_op jit(solution)/shard_map/ppermute | solution.py:16
  42.5 0.0 collective-permute-done.1.refs_1_
  42.5 0.0 collective-permute-start.13
  42.5 0.1 fusion
  42.6 0.0 collective-permute-done.5.refs_6_
  42.6 0.0 collective-permute-start.14
  42.6 0.1 broadcast_select_fusion.refs_8_
  42.7 0.0 collective-permute-done.3.refs_3_
  42.7 1.0 %copy-done.4 = bf16[128,1408]{1,0:T(8,128)(2,1)S(1)} copy-done((bf16[128,1408]{1,0:T(8,128)(2,1)S(1)}, bf16[128,1408]{1,0:T(8,128)(2,1)}, u32[]{:S(2)}) %copy-start.4) | copy-done | bytes 360472
  43.7 3.0 %shard_map.110.refs_1_ = bf16[512,512]{1,0:T(8,128)(2,1)S(1)} custom-call(s32[3]{0:T(128)S(1)} %copy-done.6, bf16[128,1408]{1,0:T(8,128)(2,1)S(1)} %copy-done.4, bf16[128,1408]{1,0:T(8,128)(2,1)S(1)} %collective-permute-done.1.refs_1_, bf16[128,1408]{1,0:T(8,128)(2,1)S(1)} %collective-permute-done.2.refs_2_, ...), custom_call_target="tpu_custom_call" | custom-call | flops 1000 | bytes 1000 | tf_op jit(solution)/shard_map/pallas_call | solution.py:267
  46.7 0.6 collective-permute-start.7
  47.2 0.0 collective-permute-done.9.refs_1_
  47.2 0.0 collective-permute-done.13.refs_3_
  47.2 3.0 %shard_map.113.refs_3_ = bf16[512,512]{1,0:T(8,128)(2,1)S(1)} custom-call(s32[3]{0:T(128)S(1)} %copy-done.6, bf16[128,1408]{1,0:T(8,128)(2,1)S(1)} %collective-permute-done.8.refs_0_, bf16[128,1408]{1,0:T(8,128)(2,1)S(1)} %collective-permute-done.9.refs_1_, bf16[128,1408]{1,0:T(8,128)(2,1)S(1)} %collective-permute-done.10.refs_2_, ...), custom_call_target="tpu_custom_call" | custom-call | flops 1000 | bytes 1000 | tf_op jit(solution)/shard_map/pallas_call | solution.py:267
  50.2 0.0 copy-start.9
  50.2 0.0 copy-start.7
  50.3 0.0 copy-start.8
  50.3 0.5 collective-permute-done.14.refs_7_
  50.8 0.0 collective-permute-done.15.refs_8_
  50.8 0.1 collective-permute-start.16
  50.9 0.0 collective-permute-done.7.refs_2_
  50.9 1.8 %collective-permute-done.16.refs_4_ = bf16[512,512]{1,0:T(8,128)(2,1)S(1)} collective-permute-done((bf16[512,512]{1,0:T(8,128)(2,1)S(1)}, bf16[512,512]{1,0:T(8,128)(2,1)S(1)}, u32[]{:S(2)}, u32[]{:S(2)}) %collective-permute-start.16) | collective-permute-done | bytes 524320 | tf_op jit(solution)/shard_map/ppermute | solution.py:16
  52.7 3.2 %shard_map.114 = (f32[256,512]{1,0:T(8,128)S(1)}, bf16[256,512]{1,0:T(8,128)(2,1)S(1)}, bf16[256,512]{1,0:T(8,128)(2,1)S(1)}, bf16[256,512]{1,0:T(8,128)(2,1)S(1)}) custom-call(s32[3]{0:T(128)S(1)} %copy-done.6, bf16[512,512]{1,0:T(8,128)(2,1)S(1)} %shard_map.110.refs_1_, bf16[512,512]{1,0:T(8,128)(2,1)S(1)} %collective-permute-done.7.refs_2_, ...), custom_call_target="tpu_custom_call" | custom-call | flops 1000 | bytes 1000 | tf_op jit(solution)/shard_map/pallas_call | solution.py:332
  55.9 0.6 collective-permute-start.17
  56.5 1.6 %collective-permute-start.18 = (bf16[256,512]{1,0:T(8,128)(2,1)S(1)}, bf16[256,512]{1,0:T(8,128)(2,1)S(1)}, u32[]{:S(2)}, u32[]{:S(2)}) collective-permute-start(bf16[256,512]{1,0:T(8,128)(2,1)S(1)} %get-tuple-element.51), channel_id=1, source_target_pairs={{0,4},{2,6},{4,0},{6,2},{8,12},{10,14},{12,8},{14,10},{1,5},{3,7},... | collective-permute-start | bytes 786440 | tf_op jit(solution)/shard_map/ppermute | solution.py:16
  58.1 1.4 %collective-permute-start.19 = (bf16[256,512]{1,0:T(8,128)(2,1)S(1)}, bf16[256,512]{1,0:T(8,128)(2,1)S(1)}, u32[]{:S(2)}, u32[]{:S(2)}) collective-permute-start(bf16[256,512]{1,0:T(8,128)(2,1)S(1)} %get-tuple-element.52), channel_id=1, source_target_pairs={{0,6},{2,4},{4,2},{6,0},{8,14},{10,12},{12,10},{14,8},{1,7},{3,5},... | collective-permute-start | bytes 786440 | tf_op jit(solution)/shard_map/ppermute | solution.py:16
  59.5 0.7 collective-permute-start.20
  60.2 0.0 collective-permute-start
  60.2 4.1 %collective-permute-done.17.refs_1_ = bf16[256,512]{1,0:T(8,128)(2,1)S(1)} collective-permute-done((bf16[256,512]{1,0:T(8,128)(2,1)S(1)}, bf16[256,512]{1,0:T(8,128)(2,1)S(1)}, u32[]{:S(2)}, u32[]{:S(2)}) %collective-permute-start.17) | collective-permute-done | bytes 262176 | tf_op jit(solution)/shard_map/ppermute | solution.py:16
  64.3 1.4 %collective-permute-done.18.refs_2_ = bf16[256,512]{1,0:T(8,128)(2,1)S(1)} collective-permute-done((bf16[256,512]{1,0:T(8,128)(2,1)S(1)}, bf16[256,512]{1,0:T(8,128)(2,1)S(1)}, u32[]{:S(2)}, u32[]{:S(2)}) %collective-permute-start.18) | collective-permute-done | bytes 262176 | tf_op jit(solution)/shard_map/ppermute | solution.py:16
  65.7 0.0 collective-permute-done.20.refs_8_
  65.7 2.8 %shard_map.115 = (f32[256,256]{1,0:T(8,128)S(1)}, bf16[256,256]{1,0:T(8,128)(2,1)S(1)}, bf16[256,256]{1,0:T(8,128)(2,1)S(1)}, bf16[256,256]{1,0:T(8,128)(2,1)S(1)}) custom-call(s32[3]{0:T(128)S(1)} %copy-done.6, bf16[512,512]{1,0:T(8,128)(2,1)S(1)} %shard_map.110.refs_1_, bf16[512,512]{1,0:T(8,128)(2,1)S(1)} %collective-permute-done.7.refs_2_, ...), custom_call_target="tpu_custom_call" | custom-call | flops 1000 | bytes 1000 | tf_op jit(solution)/shard_map/pallas_call | solution.py:332
  68.6 1.6 %collective-permute-start.21 = (bf16[256,256]{1,0:T(8,128)(2,1)S(1)}, bf16[256,256]{1,0:T(8,128)(2,1)S(1)}, u32[]{:S(2)}, u32[]{:S(2)}) collective-permute-start(bf16[256,256]{1,0:T(8,128)(2,1)S(1)} %get-tuple-element.56), channel_id=1, source_target_pairs={{0,2},{2,0},{4,6},{6,4},{8,10},{10,8},{12,14},{14,12},{1,3},{3,1},... | collective-permute-start | bytes 393224 | tf_op jit(solution)/shard_map/ppermute | solution.py:16
  70.1 1.5 %collective-permute-start.22 = (bf16[256,256]{1,0:T(8,128)(2,1)S(1)}, bf16[256,256]{1,0:T(8,128)(2,1)S(1)}, u32[]{:S(2)}, u32[]{:S(2)}) collective-permute-start(bf16[256,256]{1,0:T(8,128)(2,1)S(1)} %get-tuple-element.57), channel_id=1, source_target_pairs={{0,4},{2,6},{4,0},{6,2},{8,12},{10,14},{12,8},{14,10},{1,5},{3,7},... | collective-permute-start | bytes 393224 | tf_op jit(solution)/shard_map/ppermute | solution.py:16
  71.6 0.5 collective-permute-start.23
  72.1 0.1 pad_select_fusion
  72.2 0.0 collective-permute-done.other
  72.2 0.0 collective-permute-done.19.refs_3_
  72.2 3.1 %collective-permute-done.21.refs_5_ = bf16[256,256]{1,0:T(8,128)(2,1)S(1)} collective-permute-done((bf16[256,256]{1,0:T(8,128)(2,1)S(1)}, bf16[256,256]{1,0:T(8,128)(2,1)S(1)}, u32[]{:S(2)}, u32[]{:S(2)}) %collective-permute-start.21) | collective-permute-done | bytes 131104 | tf_op jit(solution)/shard_map/ppermute | solution.py:16
  75.3 2.2 %collective-permute-done.23.refs_7_ = bf16[256,256]{1,0:T(8,128)(2,1)S(1)} collective-permute-done((bf16[256,256]{1,0:T(8,128)(2,1)S(1)}, bf16[256,256]{1,0:T(8,128)(2,1)S(1)}, u32[]{:S(2)}, u32[]{:S(2)}) %collective-permute-start.23) | collective-permute-done | bytes 131104 | tf_op jit(solution)/shard_map/ppermute | solution.py:16
  77.5 2.1 %shard_map.116 = bf16[704,256]{1,0:T(8,128)(2,1)} custom-call(s32[3]{0:T(128)S(1)} %copy-done.6, s32[2]{0:T(128)S(1)} %copy-done.7, s32[2]{0:T(128)S(1)} %copy-done.8, bf16[128,768]{1,0:T(8,128)(2,1)S(1)} %copy-done.5, bf16[128,768]{1,0:T(8,128)(2,1)S(1)} %collective-permute-done.other, f32[1,768]{1,0:T(1,128)S(1)} %reshape.6.bias, ...), custom_call_target="tpu_custom_call" | custom-call | flops 1000 | bytes 1000 | tf_op jit(solution)/shard_map/pallas_call | solution.py:390
  (23 shorter events, 0.1 us)
Async XLA Ops:
  0.0 11.2 %copy-start.1 = (bf16[1408,224]{0,1:T(8,128)(2,1)S(1)}, bf16[1408,224]{0,1:T(8,128)(2,1)}, u32[]{:S(2)}) copy-start(bf16[1408,224]{0,1:T(8,128)(2,1)} %param.18) | copy-start | bytes 1892356
  0.6 29.8 %copy-start.11 = (bf16[224]{0:T(256)(128)(2,1)S(1)}, bf16[224]{0:T(256)(128)(2,1)}, u32[]{:S(2)}) copy-start(bf16[224]{0:T(256)(128)(2,1)} %param.19) | copy-start | bytes 1348
  0.6 42.1 %copy-start.6 = (s32[3]{0:T(128)S(1)}, s32[3]{0:T(128)}, u32[]{:S(2)}) copy-start(s32[3]{0:T(128)} %pad_add_fusion.place.refs_0_) | copy-start | bytes 40
  5.7 16.0 %collective-permute-start.8 = (bf16[128,1408]{1,0:T(8,128)(2,1)}, bf16[128,1408]{1,0:T(8,128)(2,1)S(1)}, u32[]{:S(2)}, u32[]{:S(2)}) collective-permute-start(bf16[128,1408]{1,0:T(8,128)(2,1)} %get-tuple-element.36.refs_0_), channel_id=1, source_target_pairs={{0,4},{2,6},{4,0},{6,2},{8,12},{10,14},{12,8},{14,10},{1,5},{3,7},... | collective-permute-start | bytes 1081352 | tf_op jit(solution)/shard_map/ppermute | solution.py:16
  11.1 12.2 %collective-permute-start.11 = (bf16[224,768]{1,0:T(8,128)(2,1)}, bf16[224,768]{1,0:T(8,128)(2,1)S(1)}, u32[]{:S(2)}, u32[]{:S(2)}) collective-permute-start(bf16[224,768]{1,0:T(8,128)(2,1)} %shard_map.111), channel_id=1, source_target_pairs={{0,1},{1,0},{2,3},{3,2},{4,5},{5,4},{6,7},{7,6},{8,9},{9,8},{10,11... | collective-permute-start | bytes 1032200 | tf_op jit(solution)/shard_map/ppermute | solution.py:16
  11.3 17.6 %collective-permute-start.4 = (bf16[112,1408]{1,0:T(8,128)(2,1)S(1)}, bf16[112,1408]{1,0:T(8,128)(2,1)S(1)}, u32[]{:S(2)}, u32[]{:S(2)}) collective-permute-start(bf16[112,1408]{1,0:T(8,128)(2,1)S(1)} %dynamic-slice_bitcast_fusion), channel_id=1, source_target_pairs={{0,8},{2,10},{4,12},{6,14},{8,0},{10,2},{12,4},{14,6},{1,9},{3,11}... | collective-permute-start | bytes 946184 | tf_op jit(solution)/shard_map/ppermute | solution.py:16
  13.9 16.5 %collective-permute-start.2 = (bf16[128,1408]{1,0:T(8,128)(2,1)}, bf16[128,1408]{1,0:T(8,128)(2,1)S(1)}, u32[]{:S(2)}, u32[]{:S(2)}) collective-permute-start(bf16[128,1408]{1,0:T(8,128)(2,1)} %get-tuple-element.36.refs_0_), channel_id=1, source_target_pairs={{0,2},{2,0},{4,6},{6,4},{8,10},{10,8},{12,14},{14,12},{1,3},{3,1},... | collective-permute-start | bytes 1081352 | tf_op jit(solution)/shard_map/ppermute | solution.py:16
  21.7 18.8 %collective-permute-start.10 = (bf16[128,1408]{1,0:T(8,128)(2,1)S(1)}, bf16[128,1408]{1,0:T(8,128)(2,1)S(1)}, u32[]{:S(2)}, u32[]{:S(2)}) collective-permute-start(bf16[128,1408]{1,0:T(8,128)(2,1)S(1)} %collective-permute-done.8.refs_0_), channel_id=1, source_target_pairs={{0,2},{2,0},{4,6},{6,4},{8,10},{10,8},{12,14},{14,12},{1,3},{3,1},... | collective-permute-start | bytes 1081352 | tf_op jit(solution)/shard_map/ppermute | solution.py:16
  23.3 19.2 %collective-permute-start.1 = (bf16[128,1408]{1,0:T(8,128)(2,1)}, bf16[128,1408]{1,0:T(8,128)(2,1)S(1)}, u32[]{:S(2)}, u32[]{:S(2)}) collective-permute-start(bf16[128,1408]{1,0:T(8,128)(2,1)} %get-tuple-element.36.refs_0_), channel_id=1, source_target_pairs={{0,1},{1,0},{2,3},{3,2},{4,5},{5,4},{6,7},{7,6},{8,9},{9,8},{10,11... | collective-permute-start | bytes 1081352 | tf_op jit(solution)/shard_map/ppermute | solution.py:16
  23.3 0.7 copy-start.2
  26.5 14.0 %collective-permute-start.12 = (bf16[224,512]{1,0:T(8,128)(2,1)}, bf16[224,512]{1,0:T(8,128)(2,1)S(1)}, u32[]{:S(2)}, u32[]{:S(2)}) collective-permute-start(bf16[224,512]{1,0:T(8,128)(2,1)} %get-tuple-element.43), channel_id=1, source_target_pairs={{0,8},{2,10},{4,12},{6,14},{8,0},{10,2},{12,4},{14,6},{1,9},{3,11}... | collective-permute-start | bytes 688136 | tf_op jit(solution)/shard_map/ppermute | solution.py:16
  28.9 13.7 %collective-permute-start.5 = (bf16[112,1408]{1,0:T(8,128)(2,1)S(1)}, bf16[112,1408]{1,0:T(8,128)(2,1)S(1)}, u32[]{:S(2)}, u32[]{:S(2)}) collective-permute-start(bf16[112,1408]{1,0:T(8,128)(2,1)S(1)} %collective-permute-done.4.refs_5_), channel_id=1, source_target_pairs={{0,16},{16,0},{1,17},{17,1},{2,18},{18,2},{3,19},{19,3},{4,20},{20... | collective-permute-start | bytes 946184 | tf_op jit(solution)/shard_map/ppermute | solution.py:16
  30.4 10.6 %collective-permute-start.6 = (bf16[1,224]{1,0:T(2,128)(2,1)S(1)}, bf16[1,224]{1,0:T(2,128)(2,1)S(1)}, u32[]{:S(2)}, u32[]{:S(2)}) collective-permute-start(bf16[1,224]{1,0:T(2,128)(2,1)S(1)} %reshape.7.refs_7_), channel_id=1, source_target_pairs={{0,8},{2,10},{4,12},{6,14},{8,0},{10,2},{12,4},{14,6},{1,9},{3,11}... | collective-permute-start | bytes 1352 | tf_op jit(solution)/shard_map/ppermute | solution.py:16
  40.5 6.8 %collective-permute-start.9 = (bf16[128,1408]{1,0:T(8,128)(2,1)S(1)}, bf16[128,1408]{1,0:T(8,128)(2,1)S(1)}, u32[]{:S(2)}, u32[]{:S(2)}) collective-permute-start(bf16[128,1408]{1,0:T(8,128)(2,1)S(1)} %collective-permute-done.8.refs_0_), channel_id=1, source_target_pairs={{0,1},{1,0},{2,3},{3,2},{4,5},{5,4},{6,7},{7,6},{8,9},{9,8},{10,11... | collective-permute-start | bytes 1081352 | tf_op jit(solution)/shard_map/ppermute | solution.py:16
  40.5 2.2 %collective-permute-start.3 = (bf16[128,1408]{1,0:T(8,128)(2,1)S(1)}, bf16[128,1408]{1,0:T(8,128)(2,1)S(1)}, u32[]{:S(2)}, u32[]{:S(2)}) collective-permute-start(bf16[128,1408]{1,0:T(8,128)(2,1)S(1)} %collective-permute-done.2.refs_2_), channel_id=1, source_target_pairs={{0,1},{1,0},{2,3},{3,2},{4,5},{5,4},{6,7},{7,6},{8,9},{9,8},{10,11... | collective-permute-start | bytes 1081352 | tf_op jit(solution)/shard_map/ppermute | solution.py:16
  41.0 9.8 %collective-permute-start.15 = (bf16[224,512]{1,0:T(8,128)(2,1)S(1)}, bf16[224,512]{1,0:T(8,128)(2,1)S(1)}, u32[]{:S(2)}, u32[]{:S(2)}) collective-permute-start(bf16[224,512]{1,0:T(8,128)(2,1)S(1)} %collective-permute-done.12.refs_7_), channel_id=1, source_target_pairs={{0,16},{16,0},{1,17},{17,1},{2,18},{18,2},{3,19},{19,3},{4,20},{20... | collective-permute-start | bytes 688136 | tf_op jit(solution)/shard_map/ppermute | solution.py:16
  42.5 4.7 %collective-permute-start.13 = (bf16[128,1408]{1,0:T(8,128)(2,1)S(1)}, bf16[128,1408]{1,0:T(8,128)(2,1)S(1)}, u32[]{:S(2)}, u32[]{:S(2)}) collective-permute-start(bf16[128,1408]{1,0:T(8,128)(2,1)S(1)} %collective-permute-done.10.refs_2_), channel_id=1, source_target_pairs={{0,1},{1,0},{2,3},{3,2},{4,5},{5,4},{6,7},{7,6},{8,9},{9,8},{10,11... | collective-permute-start | bytes 1081352 | tf_op jit(solution)/shard_map/ppermute | solution.py:16
  42.6 8.2 %collective-permute-start.14 = (bf16[224,256]{1,0:T(8,128)(2,1)}, bf16[224,256]{1,0:T(8,128)(2,1)S(1)}, u32[]{:S(2)}, u32[]{:S(2)}) collective-permute-start(bf16[224,256]{1,0:T(8,128)(2,1)} %get-tuple-element.46), channel_id=1, source_target_pairs={{0,8},{2,10},{4,12},{6,14},{8,0},{10,2},{12,4},{14,6},{1,9},{3,11}... | collective-permute-start | bytes 344072 | tf_op jit(solution)/shard_map/ppermute | solution.py:16
  42.7 1.0 %copy-start.4 = (bf16[128,1408]{1,0:T(8,128)(2,1)S(1)}, bf16[128,1408]{1,0:T(8,128)(2,1)}, u32[]{:S(2)}) copy-start(bf16[128,1408]{1,0:T(8,128)(2,1)} %get-tuple-element.36.refs_0_) | copy-start | bytes 1081348
  43.7 9.0 %copy-start = (bf16[1408,224]{0,1:T(8,128)(2,1)S(1)}, bf16[1408,224]{0,1:T(8,128)(2,1)}, u32[]{:S(2)}) copy-start(bf16[1408,224]{0,1:T(8,128)(2,1)} %param.20) | copy-start | bytes 1892356
  43.7 9.0 %copy-start.3 = (bf16[224,768]{1,0:T(8,128)(2,1)S(1)}, bf16[224,768]{1,0:T(8,128)(2,1)}, u32[]{:S(2)}) copy-start(bf16[224,768]{1,0:T(8,128)(2,1)} %copy-done.2) | copy-start | bytes 1032196
  46.7 13.5 %copy-start.10 = (bf16[128,768]{1,0:T(8,128)(2,1)S(1)}, bf16[128,768]{1,0:T(8,128)(2,1)}, u32[]{:S(2)}) copy-start(bf16[128,768]{1,0:T(8,128)(2,1)} %get-tuple-element.34) | copy-start | bytes 589828
  46.7 4.2 %collective-permute-start.7 = (bf16[512,512]{1,0:T(8,128)(2,1)S(1)}, bf16[512,512]{1,0:T(8,128)(2,1)S(1)}, u32[]{:S(2)}, u32[]{:S(2)}) collective-permute-start(bf16[512,512]{1,0:T(8,128)(2,1)S(1)} %shard_map.110.refs_1_), channel_id=1, source_target_pairs={{0,1},{1,0},{2,3},{3,2},{4,5},{5,4},{6,7},{7,6},{8,9},{9,8},{10,11... | collective-permute-start | bytes 1572872 | tf_op jit(solution)/shard_map/ppermute | solution.py:16
  50.2 21.9 %copy-start.9 = (f32[704]{0:T(1024)S(1)}, f32[704]{0:T(1024)}, u32[]{:S(2)}) copy-start(f32[704]{0:T(1024)} %param.21) | copy-start | bytes 8452
  50.2 27.3 %copy-start.5 = (bf16[128,768]{1,0:T(8,128)(2,1)S(1)}, bf16[128,768]{1,0:T(8,128)(2,1)}, u32[]{:S(2)}) copy-start(bf16[128,768]{1,0:T(8,128)(2,1)} %get-tuple-element.33.keep) | copy-start | bytes 589828
  50.2 27.3 %copy-start.7 = (s32[2]{0:T(128)S(1)}, s32[2]{0:T(128)}, u32[]{:S(2)}) copy-start(s32[2]{0:T(128)} %first.1) | copy-start | bytes 28
  50.3 27.3 %copy-start.8 = (s32[2]{0:T(128)S(1)}, s32[2]{0:T(128)}, u32[]{:S(2)}) copy-start(s32[2]{0:T(128)} %second.1) | copy-start | bytes 28
  50.8 1.9 %collective-permute-start.16 = (bf16[512,512]{1,0:T(8,128)(2,1)S(1)}, bf16[512,512]{1,0:T(8,128)(2,1)S(1)}, u32[]{:S(2)}, u32[]{:S(2)}) collective-permute-start(bf16[512,512]{1,0:T(8,128)(2,1)S(1)} %shard_map.113.refs_3_), channel_id=1, source_target_pairs={{0,1},{1,0},{2,3},{3,2},{4,5},{5,4},{6,7},{7,6},{8,9},{9,8},{10,11... | collective-permute-start | bytes 1572872 | tf_op jit(solution)/shard_map/ppermute | solution.py:16
  55.9 8.4 %collective-permute-start.17 = (bf16[256,512]{1,0:T(8,128)(2,1)S(1)}, bf16[256,512]{1,0:T(8,128)(2,1)S(1)}, u32[]{:S(2)}, u32[]{:S(2)}) collective-permute-start(bf16[256,512]{1,0:T(8,128)(2,1)S(1)} %get-tuple-element.50), channel_id=1, source_target_pairs={{0,2},{2,0},{4,6},{6,4},{8,10},{10,8},{12,14},{14,12},{1,3},{3,1},... | collective-permute-start | bytes 786440 | tf_op jit(solution)/shard_map/ppermute | solution.py:16
  56.5 9.2 %collective-permute-start.18 = (bf16[256,512]{1,0:T(8,128)(2,1)S(1)}, bf16[256,512]{1,0:T(8,128)(2,1)S(1)}, u32[]{:S(2)}, u32[]{:S(2)}) collective-permute-start(bf16[256,512]{1,0:T(8,128)(2,1)S(1)} %get-tuple-element.51), channel_id=1, source_target_pairs={{0,4},{2,6},{4,0},{6,2},{8,12},{10,14},{12,8},{14,10},{1,5},{3,7},... | collective-permute-start | bytes 786440 | tf_op jit(solution)/shard_map/ppermute | solution.py:16
  58.1 14.1 %collective-permute-start.19 = (bf16[256,512]{1,0:T(8,128)(2,1)S(1)}, bf16[256,512]{1,0:T(8,128)(2,1)S(1)}, u32[]{:S(2)}, u32[]{:S(2)}) collective-permute-start(bf16[256,512]{1,0:T(8,128)(2,1)S(1)} %get-tuple-element.52), channel_id=1, source_target_pairs={{0,6},{2,4},{4,2},{6,0},{8,14},{10,12},{12,10},{14,8},{1,7},{3,5},... | collective-permute-start | bytes 786440 | tf_op jit(solution)/shard_map/ppermute | solution.py:16
  59.5 6.2 %collective-permute-start.20 = (bf16[224,256]{1,0:T(8,128)(2,1)S(1)}, bf16[224,256]{1,0:T(8,128)(2,1)S(1)}, u32[]{:S(2)}, u32[]{:S(2)}) collective-permute-start(bf16[224,256]{1,0:T(8,128)(2,1)S(1)} %collective-permute-done.14.refs_7_), channel_id=1, source_target_pairs={{0,16},{16,0},{1,17},{17,1},{2,18},{18,2},{3,19},{19,3},{4,20},{20... | collective-permute-start | bytes 344072 | tf_op jit(solution)/shard_map/ppermute | solution.py:16
  60.2 12.0 %collective-permute-start = (bf16[128,768]{1,0:T(8,128)(2,1)S(1)}, bf16[128,768]{1,0:T(8,128)(2,1)S(1)}, u32[]{:S(2)}, u32[]{:S(2)}) collective-permute-start(bf16[128,768]{1,0:T(8,128)(2,1)S(1)} %copy-done.10), channel_id=1, source_target_pairs={{0,1},{1,0},{2,3},{3,2},{4,5},{5,4},{6,7},{7,6},{8,9},{9,8},{10,11... | collective-permute-start | bytes 589832 | tf_op jit(solution)/shard_map/ppermute | solution.py:16
  68.6 6.8 %collective-permute-start.21 = (bf16[256,256]{1,0:T(8,128)(2,1)S(1)}, bf16[256,256]{1,0:T(8,128)(2,1)S(1)}, u32[]{:S(2)}, u32[]{:S(2)}) collective-permute-start(bf16[256,256]{1,0:T(8,128)(2,1)S(1)} %get-tuple-element.56), channel_id=1, source_target_pairs={{0,2},{2,0},{4,6},{6,4},{8,10},{10,8},{12,14},{14,12},{1,3},{3,1},... | collective-permute-start | bytes 393224 | tf_op jit(solution)/shard_map/ppermute | solution.py:16
  70.1 5.2 %collective-permute-start.22 = (bf16[256,256]{1,0:T(8,128)(2,1)S(1)}, bf16[256,256]{1,0:T(8,128)(2,1)S(1)}, u32[]{:S(2)}, u32[]{:S(2)}) collective-permute-start(bf16[256,256]{1,0:T(8,128)(2,1)S(1)} %get-tuple-element.57), channel_id=1, source_target_pairs={{0,4},{2,6},{4,0},{6,2},{8,12},{10,14},{12,8},{14,10},{1,5},{3,7},... | collective-permute-start | bytes 393224 | tf_op jit(solution)/shard_map/ppermute | solution.py:16
  71.6 5.9 %collective-permute-start.23 = (bf16[256,256]{1,0:T(8,128)(2,1)S(1)}, bf16[256,256]{1,0:T(8,128)(2,1)S(1)}, u32[]{:S(2)}, u32[]{:S(2)}) collective-permute-start(bf16[256,256]{1,0:T(8,128)(2,1)S(1)} %get-tuple-element.58), channel_id=1, source_target_pairs={{0,6},{2,4},{4,2},{6,0},{8,14},{10,12},{12,10},{14,8},{1,7},{3,5},... | collective-permute-start | bytes 393224 | tf_op jit(solution)/shard_map/ppermute | solution.py:16

commit v6 on v5

--- a/solution.py
+++ b/solution.py
@@ -464,11 +464,11 @@
     own_0, *sent = down(
         0, after(place, place), hidden, down_own, given, near_0, crossed_0, rows
     )
-    got_0 = [swap(part, "sec", mask) for mask, part in enumerate(sent, 1)]
+    got_0 = [swap(sent[k], "sec", k + 1) for k in (0, 1, 2)]
     own_1, *sent = down(
         CHUNKS[0], after(place, got_0[0], got_0[1]), hidden, down_own, given, near_1, crossed_1, rows
     )
-    got_1 = [swap(part, "sec", mask) for mask, part in enumerate(sent, 1)]
+    got_1 = [swap(sent[k], "sec", k + 1) for k in (2, 0, 1)]
     parts = [own_0, *got_0, own_1, *got_1]
     shift = jnp.where(
         core == 0, jnp.pad(down_bias, (0, spare)), jnp.pad(down_bias, (spare, 0))

time: 79.9 us -> 79.2 us (level)
  no operation moved by 1% of the time
where the time goes in v6:
time: 79.2 us; the launch traced here: 78.9 us
  waiting for transfers between devices  29.8 us (38%)
  Pallas kernels  23.9 us (30%)
  starting transfers between devices  22.4 us (28%)
  local copies, waits for them, and re-layouts  1.87 us (2%)
    ppermute x24, waiting for transfers between devices, swap(): return lax.ppermute(values, axis, [(i, i ^ mask) for i in range(size)])  29.8 us
    ppermute x24, starting transfers between devices, swap(): return lax.ppermute(values, axis, [(i, i ^ mask) for i in range(size)])  22.4 us
    pallas_call x2, Pallas kernels, down(): call(lambda *refs: down_kernel(at, count, *refs), [jax.ShapeDtypeStruct((...  6.03 us
    pallas_call x2, Pallas kernels, hidden_of(): call(hidden_kernel, jax.ShapeDtypeStruct(out, jnp.bfloat16), [ANY] * (len...  5.95 us
    pallas_call x1, Pallas kernels, lead(): call(lead_kernel, [jax.ShapeDtypeStruct((rows, size), jnp.bfloat16) for s...  5.02 us
    pallas_call x1, Pallas kernels, messages(): call(message_kernel, [jax.ShapeDtypeStruct((units, size), jnp.bfloat16) f...  2.4 us
    pallas_call x1, Pallas kernels, give(): call(give_kernel, jax.ShapeDtypeStruct((units, window), jnp.bfloat16), [A...  2.38 us
    pallas_call x1, Pallas kernels, final(): call(final_kernel, jax.ShapeDtypeStruct((columns, rows), jnp.bfloat16), [...  2.15 us
  transfers between devices with their start and end apart: 24, of which 9 were waited for; matrix products, arithmetic and copies ran while one was open for 0% of the time, Pallas kernels for 17%

profile of v6, /device:TPU:0, one launch (start us, length us, event | category | flops | bytes accessed | tf_op | source)
XLA Modules:
  0.0 78.9 jit_solution(5472317163109028590)
XLA Ops:
  0.0 0.6 pad_add_fusion.place.refs_0_
  0.6 5.0 %shard_map.109 = (bf16[128,1408]{1,0:T(8,128)(2,1)}, bf16[128,768]{1,0:T(8,128)(2,1)}, bf16[128,768]{1,0:T(8,128)(2,1)}) custom-call(s32[3]{0:T(128)} %pad_add_fusion.place.refs_0_, bf16[256,1408]{1,0:T(8,128)(2,1)} %bitcast.18, bf16[256,1024]{1,0:T(8,128)(2,1)} %bitcast.19, bf16[1024,1408]{1,0:T(8,128)(2,1)} %weight.1, f32[1408]{0:T(1024)} %gain.1, f32[1408]{0:T(1024)} %shift.1), custom_call_target="tpu_custom_call" | custom-call | flops 1000 | bytes 1000 | tf_op jit(solution)/shard_map/pallas_call | solution.py:157
  5.7 3.1 %collective-permute-start.8 = (bf16[128,1408]{1,0:T(8,128)(2,1)}, bf16[128,1408]{1,0:T(8,128)(2,1)S(1)}, u32[]{:S(2)}, u32[]{:S(2)}) collective-permute-start(bf16[128,1408]{1,0:T(8,128)(2,1)} %get-tuple-element.36.refs_0_), channel_id=1, source_target_pairs={{0,4},{2,6},{4,0},{6,2},{8,12},{10,14},{12,8},{14,10},{1,5},{3,7},... | collective-permute-start | bytes 1081352 | tf_op jit(solution)/shard_map/ppermute | solution.py:16
  8.7 2.4 %shard_map.111 = bf16[224,768]{1,0:T(8,128)(2,1)} custom-call(s32[3]{0:T(128)} %pad_add_fusion.place.refs_0_, bf16[224,1408]{1,0:T(8,128)(2,1)} %bitcast.12), custom_call_target="tpu_custom_call" | custom-call | flops 1000 | bytes 1000 | tf_op jit(solution)/shard_map/pallas_call | solution.py:60
  11.1 0.1 collective-permute-start.11
  11.3 2.7 %collective-permute-start.4 = (bf16[112,1408]{1,0:T(8,128)(2,1)S(1)}, bf16[112,1408]{1,0:T(8,128)(2,1)S(1)}, u32[]{:S(2)}, u32[]{:S(2)}) collective-permute-start(bf16[112,1408]{1,0:T(8,128)(2,1)S(1)} %dynamic-slice_bitcast_fusion), channel_id=1, source_target_pairs={{0,8},{2,10},{4,12},{6,14},{8,0},{10,2},{12,4},{14,6},{1,9},{3,11}... | collective-permute-start | bytes 946184 | tf_op jit(solution)/shard_map/ppermute | solution.py:16
  13.9 1.5 %collective-permute-start.2 = (bf16[128,1408]{1,0:T(8,128)(2,1)}, bf16[128,1408]{1,0:T(8,128)(2,1)S(1)}, u32[]{:S(2)}, u32[]{:S(2)}) collective-permute-start(bf16[128,1408]{1,0:T(8,128)(2,1)} %get-tuple-element.36.refs_0_), channel_id=1, source_target_pairs={{0,2},{2,0},{4,6},{6,4},{8,10},{10,8},{12,14},{14,12},{1,3},{3,1},... | collective-permute-start | bytes 1081352 | tf_op jit(solution)/shard_map/ppermute | solution.py:16
  15.4 6.3 %collective-permute-done.8.refs_0_ = bf16[128,1408]{1,0:T(8,128)(2,1)S(1)} collective-permute-done((bf16[128,1408]{1,0:T(8,128)(2,1)}, bf16[128,1408]{1,0:T(8,128)(2,1)S(1)}, u32[]{:S(2)}, u32[]{:S(2)}) %collective-permute-start.8) | collective-permute-done | bytes 360480 | tf_op jit(solution)/shard_map/ppermute | solution.py:16
  21.7 1.6 %collective-permute-start.10 = (bf16[128,1408]{1,0:T(8,128)(2,1)S(1)}, bf16[128,1408]{1,0:T(8,128)(2,1)S(1)}, u32[]{:S(2)}, u32[]{:S(2)}) collective-permute-start(bf16[128,1408]{1,0:T(8,128)(2,1)S(1)} %collective-permute-done.8.refs_0_), channel_id=1, source_target_pairs={{0,2},{2,0},{4,6},{6,4},{8,10},{10,8},{12,14},{14,12},{1,3},{3,1},... | collective-permute-start | bytes 1081352 | tf_op jit(solution)/shard_map/ppermute | solution.py:16
  23.3 0.0 collective-permute-start.1
  23.3 0.0 collective-permute-done.11.given.refs_6_
  23.3 0.7 copy-done.2
  24.1 2.4 %shard_map.112 = (bf16[224,512]{1,0:T(8,128)(2,1)}, bf16[224,256]{1,0:T(8,128)(2,1)}) custom-call(s32[3]{0:T(128)} %pad_add_fusion.place.refs_0_, bf16[224,1408]{1,0:T(8,128)(2,1)} %bitcast.13, bf16[224,768]{1,0:T(8,128)(2,1)} %copy-done.2), custom_call_target="tpu_custom_call" | custom-call | flops 1000 | bytes 1000 | tf_op jit(solution)/shard_map/pallas_call | solution.py:92
  26.5 0.7 collective-permute-start.12
  27.2 1.6 %collective-permute-done.4.refs_5_ = bf16[112,1408]{1,0:T(8,128)(2,1)S(1)} collective-permute-done((bf16[112,1408]{1,0:T(8,128)(2,1)S(1)}, bf16[112,1408]{1,0:T(8,128)(2,1)S(1)}, u32[]{:S(2)}, u32[]{:S(2)}) %collective-permute-start.4) | collective-permute-done | bytes 315424 | tf_op jit(solution)/shard_map/ppermute | solution.py:16
  28.9 1.5 %collective-permute-start.5 = (bf16[112,1408]{1,0:T(8,128)(2,1)S(1)}, bf16[112,1408]{1,0:T(8,128)(2,1)S(1)}, u32[]{:S(2)}, u32[]{:S(2)}) collective-permute-start(bf16[112,1408]{1,0:T(8,128)(2,1)S(1)} %collective-permute-done.4.refs_5_), channel_id=1, source_target_pairs={{0,16},{16,0},{1,17},{17,1},{2,18},{18,2},{3,19},{19,3},{4,20},{20... | collective-permute-start | bytes 946184 | tf_op jit(solution)/shard_map/ppermute | solution.py:16
  30.4 0.0 collective-permute-done.2.refs_2_
  30.4 0.7 collective-permute-start.6
  31.1 9.4 %collective-permute-done.12.refs_7_ = bf16[224,512]{1,0:T(8,128)(2,1)S(1)} collective-permute-done((bf16[224,512]{1,0:T(8,128)(2,1)}, bf16[224,512]{1,0:T(8,128)(2,1)S(1)}, u32[]{:S(2)}, u32[]{:S(2)}) %collective-permute-start.12) | collective-permute-done | bytes 229408 | tf_op jit(solution)/shard_map/ppermute | solution.py:16
  40.5 0.1 collective-permute-start.9
  40.5 0.0 collective-permute-done.10.refs_2_
  40.5 0.5 collective-permute-start.3
  41.0 0.0 collective-permute-done.6
  41.0 1.5 %collective-permute-start.15 = (bf16[224,512]{1,0:T(8,128)(2,1)S(1)}, bf16[224,512]{1,0:T(8,128)(2,1)S(1)}, u32[]{:S(2)}, u32[]{:S(2)}) collective-permute-start(bf16[224,512]{1,0:T(8,128)(2,1)S(1)} %collective-permute-done.12.refs_7_), channel_id=1, source_target_pairs={{0,16},{16,0},{1,17},{17,1},{2,18},{18,2},{3,19},{19,3},{4,20},{20... | collective-permute-start | bytes 688136 | tf_op jit(solution)/shard_map/ppermute | solution.py:16
  42.5 0.0 collective-permute-done.1.refs_1_
  42.5 0.0 collective-permute-start.13
  42.5 0.1 fusion
  42.6 0.0 collective-permute-done.5.refs_6_
  42.6 0.0 collective-permute-start.14
  42.6 0.1 broadcast_select_fusion.refs_8_
  42.7 0.0 collective-permute-done.3.refs_3_
  42.7 1.0 %copy-done.4 = bf16[128,1408]{1,0:T(8,128)(2,1)S(1)} copy-done((bf16[128,1408]{1,0:T(8,128)(2,1)S(1)}, bf16[128,1408]{1,0:T(8,128)(2,1)}, u32[]{:S(2)}) %copy-start.4) | copy-done | bytes 360472
  43.7 3.0 %shard_map.110.refs_1_ = bf16[512,512]{1,0:T(8,128)(2,1)S(1)} custom-call(s32[3]{0:T(128)S(1)} %copy-done.6, bf16[128,1408]{1,0:T(8,128)(2,1)S(1)} %copy-done.4, bf16[128,1408]{1,0:T(8,128)(2,1)S(1)} %collective-permute-done.1.refs_1_, bf16[128,1408]{1,0:T(8,128)(2,1)S(1)} %collective-permute-done.2.refs_2_, ...), custom_call_target="tpu_custom_call" | custom-call | flops 1000 | bytes 1000 | tf_op jit(solution)/shard_map/pallas_call | solution.py:267
  46.7 0.6 collective-permute-start.7
  47.2 0.0 collective-permute-done.9.refs_1_
  47.2 0.0 collective-permute-done.13.refs_3_
  47.2 3.0 %shard_map.113.refs_3_ = bf16[512,512]{1,0:T(8,128)(2,1)S(1)} custom-call(s32[3]{0:T(128)S(1)} %copy-done.6, bf16[128,1408]{1,0:T(8,128)(2,1)S(1)} %collective-permute-done.8.refs_0_, bf16[128,1408]{1,0:T(8,128)(2,1)S(1)} %collective-permute-done.9.refs_1_, bf16[128,1408]{1,0:T(8,128)(2,1)S(1)} %collective-permute-done.10.refs_2_, ...), custom_call_target="tpu_custom_call" | custom-call | flops 1000 | bytes 1000 | tf_op jit(solution)/shard_map/pallas_call | solution.py:267
  50.2 0.0 copy-start.9
  50.2 0.0 copy-start.7
  50.3 0.0 copy-start.8
  50.3 0.5 collective-permute-done.14.refs_7_
  50.8 0.0 collective-permute-done.15.refs_8_
  50.8 0.1 collective-permute-start.16
  50.9 0.0 collective-permute-done.7.refs_2_
  50.9 1.8 %collective-permute-done.16.refs_4_ = bf16[512,512]{1,0:T(8,128)(2,1)S(1)} collective-permute-done((bf16[512,512]{1,0:T(8,128)(2,1)S(1)}, bf16[512,512]{1,0:T(8,128)(2,1)S(1)}, u32[]{:S(2)}, u32[]{:S(2)}) %collective-permute-start.16) | collective-permute-done | bytes 524320 | tf_op jit(solution)/shard_map/ppermute | solution.py:16
  52.7 3.2 %shard_map.114 = (f32[256,512]{1,0:T(8,128)S(1)}, bf16[256,512]{1,0:T(8,128)(2,1)S(1)}, bf16[256,512]{1,0:T(8,128)(2,1)S(1)}, bf16[256,512]{1,0:T(8,128)(2,1)S(1)}) custom-call(s32[3]{0:T(128)S(1)} %copy-done.6, bf16[512,512]{1,0:T(8,128)(2,1)S(1)} %shard_map.110.refs_1_, bf16[512,512]{1,0:T(8,128)(2,1)S(1)} %collective-permute-done.7.refs_2_, ...), custom_call_target="tpu_custom_call" | custom-call | flops 1000 | bytes 1000 | tf_op jit(solution)/shard_map/pallas_call | solution.py:332
  55.9 0.6 collective-permute-start.17
  56.5 1.6 %collective-permute-start.18 = (bf16[256,512]{1,0:T(8,128)(2,1)S(1)}, bf16[256,512]{1,0:T(8,128)(2,1)S(1)}, u32[]{:S(2)}, u32[]{:S(2)}) collective-permute-start(bf16[256,512]{1,0:T(8,128)(2,1)S(1)} %get-tuple-element.51), channel_id=1, source_target_pairs={{0,4},{2,6},{4,0},{6,2},{8,12},{10,14},{12,8},{14,10},{1,5},{3,7},... | collective-permute-start | bytes 786440 | tf_op jit(solution)/shard_map/ppermute | solution.py:16
  58.1 1.4 %collective-permute-start.19 = (bf16[256,512]{1,0:T(8,128)(2,1)S(1)}, bf16[256,512]{1,0:T(8,128)(2,1)S(1)}, u32[]{:S(2)}, u32[]{:S(2)}) collective-permute-start(bf16[256,512]{1,0:T(8,128)(2,1)S(1)} %get-tuple-element.52), channel_id=1, source_target_pairs={{0,6},{2,4},{4,2},{6,0},{8,14},{10,12},{12,10},{14,8},{1,7},{3,5},... | collective-permute-start | bytes 786440 | tf_op jit(solution)/shard_map/ppermute | solution.py:16
  59.5 0.7 collective-permute-start.20
  60.2 0.0 collective-permute-start
  60.2 4.1 %collective-permute-done.17.refs_1_ = bf16[256,512]{1,0:T(8,128)(2,1)S(1)} collective-permute-done((bf16[256,512]{1,0:T(8,128)(2,1)S(1)}, bf16[256,512]{1,0:T(8,128)(2,1)S(1)}, u32[]{:S(2)}, u32[]{:S(2)}) %collective-permute-start.17) | collective-permute-done | bytes 262176 | tf_op jit(solution)/shard_map/ppermute | solution.py:16
  64.3 1.4 %collective-permute-done.18.refs_2_ = bf16[256,512]{1,0:T(8,128)(2,1)S(1)} collective-permute-done((bf16[256,512]{1,0:T(8,128)(2,1)S(1)}, bf16[256,512]{1,0:T(8,128)(2,1)S(1)}, u32[]{:S(2)}, u32[]{:S(2)}) %collective-permute-start.18) | collective-permute-done | bytes 262176 | tf_op jit(solution)/shard_map/ppermute | solution.py:16
  65.7 0.0 collective-permute-done.20.refs_8_
  65.7 2.8 %shard_map.115 = (f32[256,256]{1,0:T(8,128)S(1)}, bf16[256,256]{1,0:T(8,128)(2,1)S(1)}, bf16[256,256]{1,0:T(8,128)(2,1)S(1)}, bf16[256,256]{1,0:T(8,128)(2,1)S(1)}) custom-call(s32[3]{0:T(128)S(1)} %copy-done.6, bf16[512,512]{1,0:T(8,128)(2,1)S(1)} %shard_map.110.refs_1_, bf16[512,512]{1,0:T(8,128)(2,1)S(1)} %collective-permute-done.7.refs_2_, ...), custom_call_target="tpu_custom_call" | custom-call | flops 1000 | bytes 1000 | tf_op jit(solution)/shard_map/pallas_call | solution.py:332
  68.6 2.5 %collective-permute-start.21 = (bf16[256,256]{1,0:T(8,128)(2,1)S(1)}, bf16[256,256]{1,0:T(8,128)(2,1)S(1)}, u32[]{:S(2)}, u32[]{:S(2)}) collective-permute-start(bf16[256,256]{1,0:T(8,128)(2,1)S(1)} %get-tuple-element.56), channel_id=1, source_target_pairs={{0,6},{2,4},{4,2},{6,0},{8,14},{10,12},{12,10},{14,8},{1,7},{3,5},... | collective-permute-start | bytes 393224 | tf_op jit(solution)/shard_map/ppermute | solution.py:16
  71.1 0.5 collective-permute-start.22
  71.6 0.5 collective-permute-start.23
  72.1 0.1 pad_select_fusion
  72.2 0.0 collective-permute-done.other
  72.2 0.0 collective-permute-done.19.refs_3_
  72.2 3.5 %collective-permute-done.21.refs_5_ = bf16[256,256]{1,0:T(8,128)(2,1)S(1)} collective-permute-done((bf16[256,256]{1,0:T(8,128)(2,1)S(1)}, bf16[256,256]{1,0:T(8,128)(2,1)S(1)}, u32[]{:S(2)}, u32[]{:S(2)}) %collective-permute-start.21) | collective-permute-done | bytes 131104 | tf_op jit(solution)/shard_map/ppermute | solution.py:16
  75.7 1.0 %collective-permute-done.22.refs_6_ = bf16[256,256]{1,0:T(8,128)(2,1)S(1)} collective-permute-done((bf16[256,256]{1,0:T(8,128)(2,1)S(1)}, bf16[256,256]{1,0:T(8,128)(2,1)S(1)}, u32[]{:S(2)}, u32[]{:S(2)}) %collective-permute-start.22) | collective-permute-done | bytes 131104 | tf_op jit(solution)/shard_map/ppermute | solution.py:16
  76.8 2.1 %shard_map.116 = bf16[704,256]{1,0:T(8,128)(2,1)} custom-call(s32[3]{0:T(128)S(1)} %copy-done.6, s32[2]{0:T(128)S(1)} %copy-done.7, s32[2]{0:T(128)S(1)} %copy-done.8, bf16[128,768]{1,0:T(8,128)(2,1)S(1)} %copy-done.5, bf16[128,768]{1,0:T(8,128)(2,1)S(1)} %collective-permute-done.other, f32[1,768]{1,0:T(1,128)S(1)} %reshape.6.bias, ...), custom_call_target="tpu_custom_call" | custom-call | flops 1000 | bytes 1000 | tf_op jit(solution)/shard_map/pallas_call | solution.py:390
  (23 shorter events, 0.1 us)
Async XLA Ops:
  0.0 11.2 %copy-start.1 = (bf16[1408,224]{0,1:T(8,128)(2,1)S(1)}, bf16[1408,224]{0,1:T(8,128)(2,1)}, u32[]{:S(2)}) copy-start(bf16[1408,224]{0,1:T(8,128)(2,1)} %param.18) | copy-start | bytes 1892356
  0.6 29.8 %copy-start.11 = (bf16[224]{0:T(256)(128)(2,1)S(1)}, bf16[224]{0:T(256)(128)(2,1)}, u32[]{:S(2)}) copy-start(bf16[224]{0:T(256)(128)(2,1)} %param.19) | copy-start | bytes 1348
  0.6 42.1 %copy-start.6 = (s32[3]{0:T(128)S(1)}, s32[3]{0:T(128)}, u32[]{:S(2)}) copy-start(s32[3]{0:T(128)} %pad_add_fusion.place.refs_0_) | copy-start | bytes 40
  5.7 16.0 %collective-permute-start.8 = (bf16[128,1408]{1,0:T(8,128)(2,1)}, bf16[128,1408]{1,0:T(8,128)(2,1)S(1)}, u32[]{:S(2)}, u32[]{:S(2)}) collective-permute-start(bf16[128,1408]{1,0:T(8,128)(2,1)} %get-tuple-element.36.refs_0_), channel_id=1, source_target_pairs={{0,4},{2,6},{4,0},{6,2},{8,12},{10,14},{12,8},{14,10},{1,5},{3,7},... | collective-permute-start | bytes 1081352 | tf_op jit(solution)/shard_map/ppermute | solution.py:16
  11.1 12.2 %collective-permute-start.11 = (bf16[224,768]{1,0:T(8,128)(2,1)}, bf16[224,768]{1,0:T(8,128)(2,1)S(1)}, u32[]{:S(2)}, u32[]{:S(2)}) collective-permute-start(bf16[224,768]{1,0:T(8,128)(2,1)} %shard_map.111), channel_id=1, source_target_pairs={{0,1},{1,0},{2,3},{3,2},{4,5},{5,4},{6,7},{7,6},{8,9},{9,8},{10,11... | collective-permute-start | bytes 1032200 | tf_op jit(solution)/shard_map/ppermute | solution.py:16
  11.3 17.6 %collective-permute-start.4 = (bf16[112,1408]{1,0:T(8,128)(2,1)S(1)}, bf16[112,1408]{1,0:T(8,128)(2,1)S(1)}, u32[]{:S(2)}, u32[]{:S(2)}) collective-permute-start(bf16[112,1408]{1,0:T(8,128)(2,1)S(1)} %dynamic-slice_bitcast_fusion), channel_id=1, source_target_pairs={{0,8},{2,10},{4,12},{6,14},{8,0},{10,2},{12,4},{14,6},{1,9},{3,11}... | collective-permute-start | bytes 946184 | tf_op jit(solution)/shard_map/ppermute | solution.py:16
  13.9 16.5 %collective-permute-start.2 = (bf16[128,1408]{1,0:T(8,128)(2,1)}, bf16[128,1408]{1,0:T(8,128)(2,1)S(1)}, u32[]{:S(2)}, u32[]{:S(2)}) collective-permute-start(bf16[128,1408]{1,0:T(8,128)(2,1)} %get-tuple-element.36.refs_0_), channel_id=1, source_target_pairs={{0,2},{2,0},{4,6},{6,4},{8,10},{10,8},{12,14},{14,12},{1,3},{3,1},... | collective-permute-start | bytes 1081352 | tf_op jit(solution)/shard_map/ppermute | solution.py:16
  21.7 18.8 %collective-permute-start.10 = (bf16[128,1408]{1,0:T(8,128)(2,1)S(1)}, bf16[128,1408]{1,0:T(8,128)(2,1)S(1)}, u32[]{:S(2)}, u32[]{:S(2)}) collective-permute-start(bf16[128,1408]{1,0:T(8,128)(2,1)S(1)} %collective-permute-done.8.refs_0_), channel_id=1, source_target_pairs={{0,2},{2,0},{4,6},{6,4},{8,10},{10,8},{12,14},{14,12},{1,3},{3,1},... | collective-permute-start | bytes 1081352 | tf_op jit(solution)/shard_map/ppermute | solution.py:16
  23.3 19.2 %collective-permute-start.1 = (bf16[128,1408]{1,0:T(8,128)(2,1)}, bf16[128,1408]{1,0:T(8,128)(2,1)S(1)}, u32[]{:S(2)}, u32[]{:S(2)}) collective-permute-start(bf16[128,1408]{1,0:T(8,128)(2,1)} %get-tuple-element.36.refs_0_), channel_id=1, source_target_pairs={{0,1},{1,0},{2,3},{3,2},{4,5},{5,4},{6,7},{7,6},{8,9},{9,8},{10,11... | collective-permute-start | bytes 1081352 | tf_op jit(solution)/shard_map/ppermute | solution.py:16
  23.3 0.7 copy-start.2
  26.5 14.0 %collective-permute-start.12 = (bf16[224,512]{1,0:T(8,128)(2,1)}, bf16[224,512]{1,0:T(8,128)(2,1)S(1)}, u32[]{:S(2)}, u32[]{:S(2)}) collective-permute-start(bf16[224,512]{1,0:T(8,128)(2,1)} %get-tuple-element.43), channel_id=1, source_target_pairs={{0,8},{2,10},{4,12},{6,14},{8,0},{10,2},{12,4},{14,6},{1,9},{3,11}... | collective-permute-start | bytes 688136 | tf_op jit(solution)/shard_map/ppermute | solution.py:16
  28.9 13.7 %collective-permute-start.5 = (bf16[112,1408]{1,0:T(8,128)(2,1)S(1)}, bf16[112,1408]{1,0:T(8,128)(2,1)S(1)}, u32[]{:S(2)}, u32[]{:S(2)}) collective-permute-start(bf16[112,1408]{1,0:T(8,128)(2,1)S(1)} %collective-permute-done.4.refs_5_), channel_id=1, source_target_pairs={{0,16},{16,0},{1,17},{17,1},{2,18},{18,2},{3,19},{19,3},{4,20},{20... | collective-permute-start | bytes 946184 | tf_op jit(solution)/shard_map/ppermute | solution.py:16
  30.4 10.6 %collective-permute-start.6 = (bf16[1,224]{1,0:T(2,128)(2,1)S(1)}, bf16[1,224]{1,0:T(2,128)(2,1)S(1)}, u32[]{:S(2)}, u32[]{:S(2)}) collective-permute-start(bf16[1,224]{1,0:T(2,128)(2,1)S(1)} %reshape.7.refs_7_), channel_id=1, source_target_pairs={{0,8},{2,10},{4,12},{6,14},{8,0},{10,2},{12,4},{14,6},{1,9},{3,11}... | collective-permute-start | bytes 1352 | tf_op jit(solution)/shard_map/ppermute | solution.py:16
  40.5 6.8 %collective-permute-start.9 = (bf16[128,1408]{1,0:T(8,128)(2,1)S(1)}, bf16[128,1408]{1,0:T(8,128)(2,1)S(1)}, u32[]{:S(2)}, u32[]{:S(2)}) collective-permute-start(bf16[128,1408]{1,0:T(8,128)(2,1)S(1)} %collective-permute-done.8.refs_0_), channel_id=1, source_target_pairs={{0,1},{1,0},{2,3},{3,2},{4,5},{5,4},{6,7},{7,6},{8,9},{9,8},{10,11... | collective-permute-start | bytes 1081352 | tf_op jit(solution)/shard_map/ppermute | solution.py:16
  40.5 2.2 %collective-permute-start.3 = (bf16[128,1408]{1,0:T(8,128)(2,1)S(1)}, bf16[128,1408]{1,0:T(8,128)(2,1)S(1)}, u32[]{:S(2)}, u32[]{:S(2)}) collective-permute-start(bf16[128,1408]{1,0:T(8,128)(2,1)S(1)} %collective-permute-done.2.refs_2_), channel_id=1, source_target_pairs={{0,1},{1,0},{2,3},{3,2},{4,5},{5,4},{6,7},{7,6},{8,9},{9,8},{10,11... | collective-permute-start | bytes 1081352 | tf_op jit(solution)/shard_map/ppermute | solution.py:16
  41.0 9.8 %collective-permute-start.15 = (bf16[224,512]{1,0:T(8,128)(2,1)S(1)}, bf16[224,512]{1,0:T(8,128)(2,1)S(1)}, u32[]{:S(2)}, u32[]{:S(2)}) collective-permute-start(bf16[224,512]{1,0:T(8,128)(2,1)S(1)} %collective-permute-done.12.refs_7_), channel_id=1, source_target_pairs={{0,16},{16,0},{1,17},{17,1},{2,18},{18,2},{3,19},{19,3},{4,20},{20... | collective-permute-start | bytes 688136 | tf_op jit(solution)/shard_map/ppermute | solution.py:16
  42.5 4.7 %collective-permute-start.13 = (bf16[128,1408]{1,0:T(8,128)(2,1)S(1)}, bf16[128,1408]{1,0:T(8,128)(2,1)S(1)}, u32[]{:S(2)}, u32[]{:S(2)}) collective-permute-start(bf16[128,1408]{1,0:T(8,128)(2,1)S(1)} %collective-permute-done.10.refs_2_), channel_id=1, source_target_pairs={{0,1},{1,0},{2,3},{3,2},{4,5},{5,4},{6,7},{7,6},{8,9},{9,8},{10,11... | collective-permute-start | bytes 1081352 | tf_op jit(solution)/shard_map/ppermute | solution.py:16
  42.6 8.2 %collective-permute-start.14 = (bf16[224,256]{1,0:T(8,128)(2,1)}, bf16[224,256]{1,0:T(8,128)(2,1)S(1)}, u32[]{:S(2)}, u32[]{:S(2)}) collective-permute-start(bf16[224,256]{1,0:T(8,128)(2,1)} %get-tuple-element.46), channel_id=1, source_target_pairs={{0,8},{2,10},{4,12},{6,14},{8,0},{10,2},{12,4},{14,6},{1,9},{3,11}... | collective-permute-start | bytes 344072 | tf_op jit(solution)/shard_map/ppermute | solution.py:16
  42.7 1.0 %copy-start.4 = (bf16[128,1408]{1,0:T(8,128)(2,1)S(1)}, bf16[128,1408]{1,0:T(8,128)(2,1)}, u32[]{:S(2)}) copy-start(bf16[128,1408]{1,0:T(8,128)(2,1)} %get-tuple-element.36.refs_0_) | copy-start | bytes 1081348
  43.7 9.0 %copy-start = (bf16[1408,224]{0,1:T(8,128)(2,1)S(1)}, bf16[1408,224]{0,1:T(8,128)(2,1)}, u32[]{:S(2)}) copy-start(bf16[1408,224]{0,1:T(8,128)(2,1)} %param.20) | copy-start | bytes 1892356
  43.7 9.0 %copy-start.3 = (bf16[224,768]{1,0:T(8,128)(2,1)S(1)}, bf16[224,768]{1,0:T(8,128)(2,1)}, u32[]{:S(2)}) copy-start(bf16[224,768]{1,0:T(8,128)(2,1)} %copy-done.2) | copy-start | bytes 1032196
  46.7 13.5 %copy-start.10 = (bf16[128,768]{1,0:T(8,128)(2,1)S(1)}, bf16[128,768]{1,0:T(8,128)(2,1)}, u32[]{:S(2)}) copy-start(bf16[128,768]{1,0:T(8,128)(2,1)} %get-tuple-element.34) | copy-start | bytes 589828
  46.7 4.2 %collective-permute-start.7 = (bf16[512,512]{1,0:T(8,128)(2,1)S(1)}, bf16[512,512]{1,0:T(8,128)(2,1)S(1)}, u32[]{:S(2)}, u32[]{:S(2)}) collective-permute-start(bf16[512,512]{1,0:T(8,128)(2,1)S(1)} %shard_map.110.refs_1_), channel_id=1, source_target_pairs={{0,1},{1,0},{2,3},{3,2},{4,5},{5,4},{6,7},{7,6},{8,9},{9,8},{10,11... | collective-permute-start | bytes 1572872 | tf_op jit(solution)/shard_map/ppermute | solution.py:16
  50.2 21.9 %copy-start.9 = (f32[704]{0:T(1024)S(1)}, f32[704]{0:T(1024)}, u32[]{:S(2)}) copy-start(f32[704]{0:T(1024)} %param.21) | copy-start | bytes 8452
  50.2 26.5 %copy-start.5 = (bf16[128,768]{1,0:T(8,128)(2,1)S(1)}, bf16[128,768]{1,0:T(8,128)(2,1)}, u32[]{:S(2)}) copy-start(bf16[128,768]{1,0:T(8,128)(2,1)} %get-tuple-element.33.keep) | copy-start | bytes 589828
  50.2 26.5 %copy-start.7 = (s32[2]{0:T(128)S(1)}, s32[2]{0:T(128)}, u32[]{:S(2)}) copy-start(s32[2]{0:T(128)} %first.1) | copy-start | bytes 28
  50.3 26.5 %copy-start.8 = (s32[2]{0:T(128)S(1)}, s32[2]{0:T(128)}, u32[]{:S(2)}) copy-start(s32[2]{0:T(128)} %second.1) | copy-start | bytes 28
  50.8 1.9 %collective-permute-start.16 = (bf16[512,512]{1,0:T(8,128)(2,1)S(1)}, bf16[512,512]{1,0:T(8,128)(2,1)S(1)}, u32[]{:S(2)}, u32[]{:S(2)}) collective-permute-start(bf16[512,512]{1,0:T(8,128)(2,1)S(1)} %shard_map.113.refs_3_), channel_id=1, source_target_pairs={{0,1},{1,0},{2,3},{3,2},{4,5},{5,4},{6,7},{7,6},{8,9},{9,8},{10,11... | collective-permute-start | bytes 1572872 | tf_op jit(solution)/shard_map/ppermute | solution.py:16
  55.9 8.4 %collective-permute-start.17 = (bf16[256,512]{1,0:T(8,128)(2,1)S(1)}, bf16[256,512]{1,0:T(8,128)(2,1)S(1)}, u32[]{:S(2)}, u32[]{:S(2)}) collective-permute-start(bf16[256,512]{1,0:T(8,128)(2,1)S(1)} %get-tuple-element.50), channel_id=1, source_target_pairs={{0,2},{2,0},{4,6},{6,4},{8,10},{10,8},{12,14},{14,12},{1,3},{3,1},... | collective-permute-start | bytes 786440 | tf_op jit(solution)/shard_map/ppermute | solution.py:16
  56.5 9.2 %collective-permute-start.18 = (bf16[256,512]{1,0:T(8,128)(2,1)S(1)}, bf16[256,512]{1,0:T(8,128)(2,1)S(1)}, u32[]{:S(2)}, u32[]{:S(2)}) collective-permute-start(bf16[256,512]{1,0:T(8,128)(2,1)S(1)} %get-tuple-element.51), channel_id=1, source_target_pairs={{0,4},{2,6},{4,0},{6,2},{8,12},{10,14},{12,8},{14,10},{1,5},{3,7},... | collective-permute-start | bytes 786440 | tf_op jit(solution)/shard_map/ppermute | solution.py:16
  58.1 14.1 %collective-permute-start.19 = (bf16[256,512]{1,0:T(8,128)(2,1)S(1)}, bf16[256,512]{1,0:T(8,128)(2,1)S(1)}, u32[]{:S(2)}, u32[]{:S(2)}) collective-permute-start(bf16[256,512]{1,0:T(8,128)(2,1)S(1)} %get-tuple-element.52), channel_id=1, source_target_pairs={{0,6},{2,4},{4,2},{6,0},{8,14},{10,12},{12,10},{14,8},{1,7},{3,5},... | collective-permute-start | bytes 786440 | tf_op jit(solution)/shard_map/ppermute | solution.py:16
  59.5 6.2 %collective-permute-start.20 = (bf16[224,256]{1,0:T(8,128)(2,1)S(1)}, bf16[224,256]{1,0:T(8,128)(2,1)S(1)}, u32[]{:S(2)}, u32[]{:S(2)}) collective-permute-start(bf16[224,256]{1,0:T(8,128)(2,1)S(1)} %collective-permute-done.14.refs_7_), channel_id=1, source_target_pairs={{0,16},{16,0},{1,17},{17,1},{2,18},{18,2},{3,19},{19,3},{4,20},{20... | collective-permute-start | bytes 344072 | tf_op jit(solution)/shard_map/ppermute | solution.py:16
  60.2 12.0 %collective-permute-start = (bf16[128,768]{1,0:T(8,128)(2,1)S(1)}, bf16[128,768]{1,0:T(8,128)(2,1)S(1)}, u32[]{:S(2)}, u32[]{:S(2)}) collective-permute-start(bf16[128,768]{1,0:T(8,128)(2,1)S(1)} %copy-done.10), channel_id=1, source_target_pairs={{0,1},{1,0},{2,3},{3,2},{4,5},{5,4},{6,7},{7,6},{8,9},{9,8},{10,11... | collective-permute-start | bytes 589832 | tf_op jit(solution)/shard_map/ppermute | solution.py:16
  68.6 7.1 %collective-permute-start.21 = (bf16[256,256]{1,0:T(8,128)(2,1)S(1)}, bf16[256,256]{1,0:T(8,128)(2,1)S(1)}, u32[]{:S(2)}, u32[]{:S(2)}) collective-permute-start(bf16[256,256]{1,0:T(8,128)(2,1)S(1)} %get-tuple-element.56), channel_id=1, source_target_pairs={{0,6},{2,4},{4,2},{6,0},{8,14},{10,12},{12,10},{14,8},{1,7},{3,5},... | collective-permute-start | bytes 393224 | tf_op jit(solution)/shard_map/ppermute | solution.py:16
  71.1 5.7 %collective-permute-start.22 = (bf16[256,256]{1,0:T(8,128)(2,1)S(1)}, bf16[256,256]{1,0:T(8,128)(2,1)S(1)}, u32[]{:S(2)}, u32[]{:S(2)}) collective-permute-start(bf16[256,256]{1,0:T(8,128)(2,1)S(1)} %get-tuple-element.57), channel_id=1, source_target_pairs={{0,2},{2,0},{4,6},{6,4},{8,10},{10,8},{12,14},{14,12},{1,3},{3,1},... | collective-permute-start | bytes 393224 | tf_op jit(solution)/shard_map/ppermute | solution.py:16
  71.6 5.1 %collective-permute-start.23 = (bf16[256,256]{1,0:T(8,128)(2,1)S(1)}, bf16[256,256]{1,0:T(8,128)(2,1)S(1)}, u32[]{:S(2)}, u32[]{:S(2)}) collective-permute-start(bf16[256,256]{1,0:T(8,128)(2,1)S(1)} %get-tuple-element.58), channel_id=1, source_target_pairs={{0,4},{2,6},{4,0},{6,2},{8,12},{10,14},{12,8},{14,10},{1,5},{3,7},... | collective-permute-start | bytes 393224 | tf_op jit(solution)/shard_map/ppermute | solution.py:16
